TPU v7x, 32 devices: a whole 2x2x4 slice. The times are simulated.
32 devices in a mesh: dp: 4 (over z), seq: 8 (over y, x, core).
Axes of the slice: x: 2, y: 2, z: 4, core: 2. Of those that a mesh axis runs over, the one named last changes fastest.
Arguments:
- hidden_in: bfloat16 [4, 2048, 2048], P('dp', 'seq'), may hold values from -6 to 6
- positions: int32 [4, 2048], P('dp', 'seq'), may hold values from 0 to 2047, as said below
- expert_ids: int32 [4, 2048, 6], P('dp', 'seq'), may hold values from 0 to 15, all different within a row; in each aligned block of 256 rows (0 to 255, 256 to 511, ..., all dimensions but the last counted through in order) at most 160 rows name the same one
- gate_weights: float32 [4, 2048, 6], P('dp', 'seq'), may hold values from 0.05 to 0.5
- attention_gain: bfloat16 [2048], P('dp'), may hold values from 0.25 to 1.75
- w_query: bfloat16 [2048, 3072], P('dp'), may hold values from -0.125 to 0.125
- w_compress: bfloat16 [2048, 576], P('dp'), may hold values from -0.125 to 0.125
- latent_gain: bfloat16 [512], P('dp'), may hold values from 0.25 to 1.75
- w_expand: bfloat16 [512, 4096], P('dp'), may hold values from -0.25 to 0.25
- w_output: bfloat16 [2048, 2048], P('dp'), may hold values from -1.5 to 1.5
- feedforward_gain: bfloat16 [2048], P('dp'), may hold values from 0.25 to 1.75
- w_shared_in: bfloat16 [2048, 5632], P('dp'), may hold values from -0.125 to 0.125
- w_shared_out: bfloat16 [2816, 2048], P('dp'), may hold values from -0.109375 to 0.109375
- w_expert_in: bfloat16 [32, 2048, 1408], P(('dp', 'seq')), may hold values from -0.125 to 0.125
- w_expert_out: bfloat16 [32, 704, 2048], P(('dp', 'seq')), may hold values from -0.15625 to 0.15625
- cotangent: bfloat16 [4, 2048, 2048], P('dp', 'seq'), may hold values from -6 to 6
Outputs:
- block_out: bfloat16 [4, 2048, 2048], P('dp', 'seq')
- hidden_gradient: bfloat16 [4, 2048, 2048], P('dp', 'seq')
- gate_gradient: float32 [4, 2048, 6], P('dp', 'seq')
- attention_gain_gradient: float32 [2048], P('dp')
- w_query_gradient: float32 [2048, 3072], P('dp')
- w_compress_gradient: float32 [2048, 576], P('dp')
- latent_gain_gradient: float32 [512], P('dp')
- w_expand_gradient: float32 [512, 4096], P('dp')
- w_output_gradient: float32 [2048, 2048], P('dp')
- feedforward_gain_gradient: float32 [2048], P('dp')
- w_shared_in_gradient: float32 [2048, 5632], P('dp')
- w_shared_out_gradient: float32 [2816, 2048], P('dp')
- w_expert_in_gradient: float32 [32, 2048, 1408], P(('dp', 'seq'))
- w_expert_out_gradient: float32 [32, 704, 2048], P(('dp', 'seq'))
Inputs may be any that keep to these rules, and one draw needn't show every extreme that they name: `expert_ids`: each token names 6 different experts. Within the tokens of one sequence that one device holds (aligned blocks of 256 tokens) no expert is named by more than 160 tokens, a bound that some block reaches. `positions`: each sequence is a pack of documents; a token's position counts from the start of its document, and the first sequence is one document.
All inputs are finite; a program needn't handle non-finite values.
Results may differ from a plain program's by a relative error of at most 0.017.
Values may be sent and summed in bfloat16 or wider, within the bound.
A program may use at most 512 MiB of HBM per device.

v0:
```python
import math

import jax
import jax.numpy as jnp
from jax import lax
from jax.sharding import PartitionSpec as P

HEADS = 16
NOPE = 128
ROPE = 64
VDIM = 128
LATENT = 512
TOP = 6
QK = 192
SH_FF = 2816
HALF = 704


EPSILON = 1e-06


def rms_scale(entries):
    return lax.rsqrt(jnp.mean(entries * entries, axis=-1, keepdims=True) + EPSILON)


def rotary_angles(position_rows):
    steps_index = jnp.arange(ROPE // 2, dtype=jnp.float32)
    frequency = 10000.0 ** (-2.0 * steps_index / ROPE)
    return position_rows.astype(jnp.float32)[..., None] * frequency


def rotate(values, angle):
    half_width = values.shape[-1] // 2
    front_half = values[..., :half_width]
    back_half = values[..., half_width:]
    cosine_values = jnp.cos(angle)
    sine_values = jnp.sin(angle)
    return jnp.concatenate(
        [
            front_half * cosine_values - back_half * sine_values,
            front_half * sine_values + back_half * cosine_values,
        ],
        axis=-1,
    )


def norm_backward(upstream, entries, inverse_scale, gain_row):
    scaled = upstream * gain_row
    return inverse_scale * scaled - entries * inverse_scale**3 * jnp.mean(
        scaled * entries, axis=-1, keepdims=True
    )


def gated_pass(rows_in, upstream, weight_in, weight_out, half_width):
    gate_up = jnp.dot(rows_in, weight_in, preferred_element_type=jnp.float32)
    gate_part = gate_up[:, :half_width]
    up_part = gate_up[:, half_width:]
    sigmoid_part = 1.0 / (1.0 + jnp.exp(-gate_part))
    activated = gate_part * sigmoid_part
    hidden = (activated * up_part).astype(jnp.bfloat16)
    result = jnp.dot(hidden, weight_out, preferred_element_type=jnp.float32)
    hidden_back = jnp.einsum("rd,fd->rf", upstream, weight_out, preferred_element_type=jnp.float32)
    gate_back = hidden_back * up_part * sigmoid_part * (1.0 + gate_part * (1.0 - sigmoid_part))
    gate_up_back = jnp.concatenate([gate_back, hidden_back * activated], axis=-1).astype(
        jnp.bfloat16
    )
    out_weight_grad = jnp.einsum("rf,rd->fd", hidden, upstream, preferred_element_type=jnp.float32)
    in_weight_grad = jnp.einsum(
        "rd,rf->df", rows_in, gate_up_back, preferred_element_type=jnp.float32
    )
    rows_back = jnp.einsum("rf,df->rd", gate_up_back, weight_in, preferred_element_type=jnp.float32)
    return (result, rows_back, in_weight_grad, out_weight_grad)


def attention_forward(queries, keys_all, values_all):
    sequence_count, length, head_count, head_width = queries.shape
    value_width = values_all.shape[-1]
    block_rows = min(512, length)
    block_count = length // block_rows
    scale_factor = 1.0 / math.sqrt(head_width)
    key_index = jnp.arange(length, dtype=jnp.int32)

    def attention_one_block(position):
        sequence = position // block_count
        block_start = position % block_count * block_rows
        sequence_queries = lax.dynamic_index_in_dim(queries, sequence, 0, keepdims=False)
        sequence_keys = lax.dynamic_index_in_dim(keys_all, sequence, 0, keepdims=False)
        sequence_values = lax.dynamic_index_in_dim(values_all, sequence, 0, keepdims=False)
        query_rows = lax.dynamic_slice_in_dim(sequence_queries, block_start, block_rows, 0)
        scores = (
            jnp.einsum(
                "qhd,khd->hqk", query_rows, sequence_keys, preferred_element_type=jnp.float32
            )
            * scale_factor
        )
        allowed = (
            key_index[None, :] <= (block_start + jnp.arange(block_rows, dtype=jnp.int32))[:, None]
        )
        scores = jnp.where(allowed[None], scores, -1e30)
        largest = jnp.max(scores, axis=-1, keepdims=True)
        weights = jnp.exp(scores - largest)
        totals = jnp.sum(weights, axis=-1, keepdims=True)
        shares = (weights / totals).astype(jnp.bfloat16)
        attended = jnp.einsum(
            "hqk,khd->qhd", shares, sequence_values, preferred_element_type=jnp.float32
        )
        return (attended.astype(jnp.bfloat16), (largest + jnp.log(totals))[..., 0])

    attended, log_totals = lax.map(
        attention_one_block, jnp.arange(sequence_count * block_count, dtype=jnp.int32)
    )
    return (attended.reshape(sequence_count, length, head_count, value_width), log_totals)


def attention_backward(queries, keys_all, values_all, log_totals, upstream_heads):
    sequence_count, length, head_count, head_width = queries.shape
    value_width = values_all.shape[-1]
    block_rows = min(512, length)
    block_count = length // block_rows
    scale_factor = 1.0 / math.sqrt(head_width)
    key_index = jnp.arange(length, dtype=jnp.int32)
    log_table = log_totals.reshape(sequence_count, block_count, head_count, block_rows)

    def one_sequence(sequence):
        sequence_queries = lax.dynamic_index_in_dim(queries, sequence, 0, keepdims=False)
        sequence_keys = lax.dynamic_index_in_dim(keys_all, sequence, 0, keepdims=False)
        sequence_values = lax.dynamic_index_in_dim(values_all, sequence, 0, keepdims=False)
        sequence_upstream = lax.dynamic_index_in_dim(upstream_heads, sequence, 0, keepdims=False)
        sequence_logs = lax.dynamic_index_in_dim(log_table, sequence, 0, keepdims=False)

        def one_one_block(running_sums, block_index):
            key_sums, value_sums = running_sums
            block_start = block_index * block_rows
            query_rows = lax.dynamic_slice_in_dim(sequence_queries, block_start, block_rows, 0)
            upstream = lax.dynamic_slice_in_dim(sequence_upstream, block_start, block_rows, 0)
            log_rows = lax.dynamic_index_in_dim(sequence_logs, block_index, 0, keepdims=False)
            scores = (
                jnp.einsum(
                    "qhd,khd->hqk", query_rows, sequence_keys, preferred_element_type=jnp.float32
                )
                * scale_factor
            )
            allowed = (
                key_index[None, :]
                <= (block_start + jnp.arange(block_rows, dtype=jnp.int32))[:, None]
            )
            scores = jnp.where(allowed[None], scores, -1e30)
            shares = jnp.exp(scores - log_rows[..., None])
            share_grad = jnp.einsum(
                "qhd,khd->hqk", upstream, sequence_values, preferred_element_type=jnp.float32
            )
            centre = jnp.sum(shares * share_grad, axis=-1, keepdims=True)
            score_grad = (shares * (share_grad - centre)).astype(jnp.bfloat16)
            query_grad = (
                jnp.einsum(
                    "hqk,khd->qhd", score_grad, sequence_keys, preferred_element_type=jnp.float32
                )
                * scale_factor
            )
            key_sums = (
                key_sums
                + jnp.einsum(
                    "hqk,qhd->khd", score_grad, query_rows, preferred_element_type=jnp.float32
                )
                * scale_factor
            )
            value_sums = value_sums + jnp.einsum(
                "hqk,qhd->khd",
                shares.astype(jnp.bfloat16),
                upstream,
                preferred_element_type=jnp.float32,
            )
            return ((key_sums, value_sums), query_grad)

        start_sums = (
            jnp.zeros((length, head_count, head_width), jnp.float32),
            jnp.zeros((length, head_count, value_width), jnp.float32),
        )
        final_sums, query_grads = lax.scan(
            one_one_block, start_sums, jnp.arange(block_count, dtype=jnp.int32)
        )
        return jnp.concatenate(
            [query_grads.reshape(length, head_count, head_width), final_sums[0], final_sums[1]],
            axis=-1,
        ).astype(jnp.bfloat16)

    return lax.map(one_sequence, jnp.arange(sequence_count, dtype=jnp.int32))


def on_device(
    hidden_in,
    positions,
    expert_ids,
    gate_weights,
    attention_gain,
    w_query,
    w_compress,
    latent_gain,
    w_expand,
    w_output,
    feedforward_gain,
    w_shared_in,
    w_shared_out,
    w_expert_in,
    w_expert_out,
    cotangent,
):
    sequence_count, local_length, feature_count = hidden_in.shape
    row_count = sequence_count * local_length
    (
        gain_first,
        query_weight,
        compress_weight,
        gain_latent,
        expand_weight,
        output_weight,
        gain_second,
        shared_in,
        shared_out,
    ) = (
        lax.all_gather(attention_gain, "dp", axis=0, tiled=True),
        lax.all_gather(w_query, "dp", axis=0, tiled=True),
        lax.all_gather(w_compress, "dp", axis=0, tiled=True),
        lax.all_gather(latent_gain, "dp", axis=0, tiled=True),
        lax.all_gather(w_expand, "dp", axis=0, tiled=True),
        lax.all_gather(w_output, "dp", axis=0, tiled=True),
        lax.all_gather(feedforward_gain, "dp", axis=0, tiled=True),
        lax.all_gather(w_shared_in, "dp", axis=0, tiled=True),
        lax.all_gather(w_shared_out, "dp", axis=0, tiled=True),
    )
    first_gain = gain_first.astype(jnp.float32)
    latent_gain_row = gain_latent.astype(jnp.float32)
    second_gain = gain_second.astype(jnp.float32)
    hidden_float = hidden_in.reshape(row_count, feature_count).astype(jnp.float32)
    first_scale = rms_scale(hidden_float)
    normed = (hidden_float * first_scale * first_gain).astype(jnp.bfloat16)
    angle_table = rotary_angles(positions.reshape(row_count))
    query_raw = jnp.dot(normed, query_weight, preferred_element_type=jnp.float32).reshape(
        row_count, HEADS, QK
    )
    queries = jnp.concatenate(
        [query_raw[..., :NOPE], rotate(query_raw[..., NOPE:], angle_table[:, None, :])], axis=-1
    ).astype(jnp.bfloat16)
    compressed = jnp.dot(normed, compress_weight, preferred_element_type=jnp.float32)
    latent = compressed[:, :LATENT]
    key_rotary = rotate(compressed[:, LATENT:], angle_table)
    latent_scale = rms_scale(latent)
    latent_normed = (latent * latent_scale * latent_gain_row).astype(jnp.bfloat16)
    expanded = jnp.dot(latent_normed, expand_weight, preferred_element_type=jnp.float32).reshape(
        row_count, HEADS, NOPE + VDIM
    )
    keys_all = jnp.concatenate(
        [expanded[..., :NOPE], jnp.broadcast_to(key_rotary[:, None, :], (row_count, HEADS, ROPE))],
        axis=-1,
    ).astype(jnp.bfloat16)
    values_all = expanded[..., NOPE:].astype(jnp.bfloat16)
    packed = jnp.concatenate([queries, keys_all, values_all], axis=-1).reshape(
        sequence_count, local_length, HEADS, 2 * QK + VDIM
    )
    by_head = lax.all_to_all(packed, "seq", split_axis=2, concat_axis=1, tiled=True)
    head_queries = by_head[..., :QK]
    head_keys = by_head[..., QK : 2 * QK]
    head_values = by_head[..., 2 * QK :]
    attended_heads, log_totals = attention_forward(head_queries, head_keys, head_values)
    attended = lax.all_to_all(
        attended_heads, "seq", split_axis=1, concat_axis=2, tiled=True
    ).reshape(row_count, HEADS * VDIM)
    middle = hidden_float + jnp.dot(attended, output_weight, preferred_element_type=jnp.float32)
    second_scale = rms_scale(middle)
    moe_rows = (middle * second_scale * second_gain).astype(jnp.bfloat16)
    upstream_rows = cotangent.reshape(row_count, feature_count)
    upstream_float = upstream_rows.astype(jnp.float32)
    device_count = lax.axis_size("dp") * lax.axis_size("seq")
    expert_count = device_count // 2
    capacity = max(2, local_length * TOP * 5 // (expert_count * 3))
    slot_count = sequence_count * capacity
    flat_ids = expert_ids.reshape(sequence_count, local_length * TOP)
    one_hot = (flat_ids[:, :, None] == jnp.arange(expert_count, dtype=jnp.int32)).astype(jnp.int32)
    within = jnp.sum((jnp.cumsum(one_hot, axis=1) - 1) * one_hot, axis=2)
    target = (
        flat_ids * slot_count
        + jnp.arange(sequence_count, dtype=jnp.int32)[:, None] * capacity
        + within
    ).reshape(row_count * TOP)
    gate_table = gate_weights.reshape(row_count, TOP)
    scaled_upstream = (
        (gate_table[:, :, None] * upstream_float[:, None, :])
        .astype(jnp.bfloat16)
        .reshape(row_count * TOP, feature_count)
    )
    repeated = jnp.repeat(moe_rows, TOP, axis=0)
    pair_shape = (expert_count, 2, slot_count, feature_count)
    send_rows = jnp.broadcast_to(
        jnp.zeros((expert_count * slot_count, feature_count), jnp.bfloat16)
        .at[target]
        .set(repeated)
        .reshape(expert_count, 1, slot_count, feature_count),
        pair_shape,
    ).reshape(device_count, slot_count, feature_count)
    send_upstream = jnp.broadcast_to(
        jnp.zeros((expert_count * slot_count, feature_count), jnp.bfloat16)
        .at[target]
        .set(scaled_upstream)
        .reshape(expert_count, 1, slot_count, feature_count),
        pair_shape,
    ).reshape(device_count, slot_count, feature_count)
    arrived_rows, arrived_upstream = (
        lax.all_to_all(send_rows, ("dp", "seq"), split_axis=0, concat_axis=0, tiled=True),
        lax.all_to_all(send_upstream, ("dp", "seq"), split_axis=0, concat_axis=0, tiled=True),
    )
    expert_result, expert_back, expert_in_grad, expert_out_grad = gated_pass(
        arrived_rows.reshape(device_count * slot_count, feature_count),
        arrived_upstream.reshape(device_count * slot_count, feature_count),
        w_expert_in[0],
        w_expert_out[0],
        HALF,
    )
    result_low = expert_result.astype(jnp.bfloat16)
    back_low = expert_back.astype(jnp.bfloat16)
    returned_rows, returned_back = (
        lax.all_to_all(
            result_low.reshape(device_count, slot_count, feature_count),
            ("dp", "seq"),
            split_axis=0,
            concat_axis=0,
            tiled=True,
        ),
        lax.all_to_all(
            back_low.reshape(device_count, slot_count, feature_count),
            ("dp", "seq"),
            split_axis=0,
            concat_axis=0,
            tiled=True,
        ),
    )
    summed_result = jnp.sum(returned_rows.reshape(pair_shape).astype(jnp.float32), axis=1).reshape(
        expert_count * slot_count, feature_count
    )
    summed_back = jnp.sum(returned_back.reshape(pair_shape).astype(jnp.float32), axis=1).reshape(
        expert_count * slot_count, feature_count
    )
    picked_result = summed_result[target].reshape(row_count, TOP, feature_count)
    picked_back = summed_back[target].reshape(row_count, TOP, feature_count)
    routed = jnp.sum(gate_table[:, :, None] * picked_result, axis=1)
    gate_gradient = jnp.sum(upstream_float[:, None, :] * picked_result, axis=-1)
    shared_result, shared_back, shared_in_grad, shared_out_grad = gated_pass(
        moe_rows, upstream_rows, shared_in, shared_out, SH_FF
    )
    block_out = (middle + shared_result + routed).astype(jnp.bfloat16)
    moe_back = shared_back + jnp.sum(picked_back, axis=1)
    second_gain_grad = jnp.sum(moe_back * middle * second_scale, axis=0)
    middle_back = upstream_float + norm_backward(moe_back, middle, second_scale, second_gain)
    middle_low = middle_back.astype(jnp.bfloat16)
    output_weight_grad = jnp.einsum(
        "ra,rd->ad", attended, middle_low, preferred_element_type=jnp.float32
    )
    attended_back = (
        jnp.einsum("rd,ad->ra", middle_low, output_weight, preferred_element_type=jnp.float32)
        .astype(jnp.bfloat16)
        .reshape(sequence_count, local_length, HEADS, VDIM)
    )
    upstream_heads = lax.all_to_all(attended_back, "seq", split_axis=2, concat_axis=1, tiled=True)
    packed_back_heads = attention_backward(
        head_queries, head_keys, head_values, log_totals, upstream_heads
    )
    packed_back = lax.all_to_all(
        packed_back_heads, "seq", split_axis=1, concat_axis=2, tiled=True
    ).reshape(row_count, HEADS, 2 * QK + VDIM)
    query_back = packed_back[..., :QK]
    key_back = packed_back[..., QK : 2 * QK]
    value_back = packed_back[..., 2 * QK :]
    query_raw_back = (
        jnp.concatenate(
            [
                query_back[..., :NOPE].astype(jnp.float32),
                rotate(query_back[..., NOPE:].astype(jnp.float32), -angle_table[:, None, :]),
            ],
            axis=-1,
        )
        .astype(jnp.bfloat16)
        .reshape(row_count, HEADS * QK)
    )
    query_weight_grad = jnp.einsum(
        "rd,rq->dq", normed, query_raw_back, preferred_element_type=jnp.float32
    )
    expanded_back = jnp.concatenate([key_back[..., :NOPE], value_back], axis=-1).reshape(
        row_count, HEADS * (NOPE + VDIM)
    )
    expand_weight_grad = jnp.einsum(
        "rl,rk->lk", latent_normed, expanded_back, preferred_element_type=jnp.float32
    )
    latent_normed_back = jnp.einsum(
        "rk,lk->rl", expanded_back, expand_weight, preferred_element_type=jnp.float32
    )
    latent_gain_grad = jnp.sum(latent_normed_back * latent * latent_scale, axis=0)
    latent_back = norm_backward(latent_normed_back, latent, latent_scale, latent_gain_row)
    rotary_back = rotate(jnp.sum(key_back[..., NOPE:].astype(jnp.float32), axis=1), -angle_table)
    compressed_back = jnp.concatenate([latent_back, rotary_back], axis=-1).astype(jnp.bfloat16)
    compress_weight_grad = jnp.einsum(
        "rd,rc->dc", normed, compressed_back, preferred_element_type=jnp.float32
    )
    normed_back = jnp.einsum(
        "rq,dq->rd", query_raw_back, query_weight, preferred_element_type=jnp.float32
    ) + jnp.einsum(
        "rc,dc->rd", compressed_back, compress_weight, preferred_element_type=jnp.float32
    )
    first_gain_grad = jnp.sum(normed_back * hidden_float * first_scale, axis=0)
    hidden_gradient = (
        middle_back + norm_backward(normed_back, hidden_float, first_scale, first_gain)
    ).astype(jnp.bfloat16)
    local_grads = (
        first_gain_grad,
        query_weight_grad,
        compress_weight_grad,
        latent_gain_grad,
        expand_weight_grad,
        output_weight_grad,
        second_gain_grad,
        shared_in_grad,
        shared_out_grad,
    )
    partial_shares = (
        lax.psum_scatter(local_grads[0], ("dp", "seq"), scatter_dimension=0, tiled=True),
        lax.psum_scatter(local_grads[1], ("dp", "seq"), scatter_dimension=0, tiled=True),
        lax.psum_scatter(local_grads[2], ("dp", "seq"), scatter_dimension=0, tiled=True),
        lax.psum_scatter(local_grads[3], ("dp", "seq"), scatter_dimension=0, tiled=True),
        lax.psum_scatter(local_grads[4], ("dp", "seq"), scatter_dimension=0, tiled=True),
        lax.psum_scatter(local_grads[5], ("dp", "seq"), scatter_dimension=0, tiled=True),
        lax.psum_scatter(local_grads[6], ("dp", "seq"), scatter_dimension=0, tiled=True),
        lax.psum_scatter(local_grads[7], ("dp", "seq"), scatter_dimension=0, tiled=True),
        lax.psum_scatter(local_grads[8], ("dp", "seq"), scatter_dimension=0, tiled=True),
    )
    summed = (
        lax.all_gather(partial_shares[0].astype(jnp.bfloat16), "seq", axis=0, tiled=True).astype(
            jnp.float32
        ),
        lax.all_gather(partial_shares[1].astype(jnp.bfloat16), "seq", axis=0, tiled=True).astype(
            jnp.float32
        ),
        lax.all_gather(partial_shares[2].astype(jnp.bfloat16), "seq", axis=0, tiled=True).astype(
            jnp.float32
        ),
        lax.all_gather(partial_shares[3].astype(jnp.bfloat16), "seq", axis=0, tiled=True).astype(
            jnp.float32
        ),
        lax.all_gather(partial_shares[4].astype(jnp.bfloat16), "seq", axis=0, tiled=True).astype(
            jnp.float32
        ),
        lax.all_gather(partial_shares[5].astype(jnp.bfloat16), "seq", axis=0, tiled=True).astype(
            jnp.float32
        ),
        lax.all_gather(partial_shares[6].astype(jnp.bfloat16), "seq", axis=0, tiled=True).astype(
            jnp.float32
        ),
        lax.all_gather(partial_shares[7].astype(jnp.bfloat16), "seq", axis=0, tiled=True).astype(
            jnp.float32
        ),
        lax.all_gather(partial_shares[8].astype(jnp.bfloat16), "seq", axis=0, tiled=True).astype(
            jnp.float32
        ),
    )
    return (
        block_out.reshape(sequence_count, local_length, feature_count),
        hidden_gradient.reshape(sequence_count, local_length, feature_count),
        gate_gradient.reshape(sequence_count, local_length, TOP),
        summed[0],
        summed[1],
        summed[2],
        summed[3],
        summed[4],
        summed[5],
        summed[6],
        summed[7],
        summed[8],
        expert_in_grad[None],
        expert_out_grad[None],
    )


def solution(mesh):
    return jax.shard_map(
        on_device,
        mesh=mesh,
        in_specs=(
            P("dp", "seq", None),
            P("dp", "seq"),
            P("dp", "seq", None),
            P("dp", "seq", None),
            P("dp"),
            P("dp", None),
            P("dp", None),
            P("dp"),
            P("dp", None),
            P("dp", None),
            P("dp"),
            P("dp", None),
            P("dp", None),
            P(("dp", "seq"), None, None),
            P(("dp", "seq"), None, None),
            P("dp", "seq", None),
        ),
        out_specs=(
            P("dp", "seq", None),
            P("dp", "seq", None),
            P("dp", "seq", None),
            P("dp"),
            P("dp", None),
            P("dp", None),
            P("dp"),
            P("dp", None),
            P("dp", None),
            P("dp"),
            P("dp", None),
            P("dp", None),
            P(("dp", "seq"), None, None),
            P(("dp", "seq"), None, None),
        ),
        check_vma=False,
    )
```

profile of v0, /device:TPU:0, one launch (start us, length us, event | category | flops | bytes accessed | tf_op | source)
XLA Modules:
  0.0 4856.0 jit_solution(1713544221163333790)
XLA Ops:
  9.5 13.6 all-gather
  23.1 9.7 all-gather.1
  35.1 27.7 all-gather.17.cloned.1.call-done
  67.2 76.8 %all-gather.19.cloned.1.call-done = bf16[512,4096]{1,0:T(8,128)(2,1)} async-done(((bf16[128,4096]{1,0:T(8,128)(2,1)}), bf16[512,4096]{1,0:T(8,128)(2,1)}) %all-gather.19.cloned.1.call-update) | async-done | bytes 4194320 | tf_op jit(solution)/shard_map/all_gather | solution.py:225
  153.1 209.3 %all-gather.15.cloned.1.call-done = bf16[2048,3072]{1,0:T(8,128)(2,1)} async-done(((bf16[512,3072]{1,0:T(8,128)(2,1)}), bf16[2048,3072]{1,0:T(8,128)(2,1)}) %all-gather.15.cloned.1.call-update) | async-done | bytes 12582928 | tf_op jit(solution)/shard_map/all_gather | solution.py:222
  362.4 16.7 copy.153
  395.6 48.2 all-to-all-done
  450.4 7.4 all_to_all.61
  467.9 59.6 %while.39 = (s32[]{:T(128)}, bf16[4,512,2,128]{3,1,0,2:T(8,128)(2,1)}, f32[4,2,512]{2,1,0:T(2,128)}, s32[4]{0:T(128)S(1)}, bf16[1,2048,2,192]{1,3,2,0:T(8,128)(2...) while((s32[]{:T(128)}, ...), condition=%wide.region_5.6_spmd.clone, body=%wide.region_2.5_spmd.clone.sunk | while | flops 1368522240 | bytes 41063780 | solution.py:109
  540.1 12.4 all-gather.2
  573.0 11.0 reshape.698
  584.1 16.6 scatter_custom_fusion
  600.6 13.1 broadcast_in_dim.117
  620.5 9.8 mul.486
  630.3 15.7 mul.487
  646.3 17.4 scatter_custom_fusion.1
  663.7 421.0 %all-to-all-done.2 = bf16[32,160,2048]{2,1,0:T(8,128)(2,1)} async-done(((bf16[32,160,2048]{2,1,0:T(8,128)(2,1)}), bf16[32,160,2048]{2,1,0:T(8,128)(2,1)}, u32[]{:S(2)}, u32[]{:S(2)}) %all-to-all-start.2) | async-done | bytes 20971552 | tf_op jit(solution)/shard_map/all_to_all | solution.py:308
  1084.7 13.1 broadcast_in_dim.119
  1102.4 37.8 fusion.48
  1140.2 787.0 %all-to-all-done.4 = bf16[32,160,2048]{2,1,0:T(8,128)(2,1)} async-done(((bf16[32,160,2048]{2,1,0:T(8,128)(2,1)}), bf16[32,160,2048]{2,1,0:T(8,128)(2,1)}, u32[]{:S(2)}, u32[]{:S(2)}) %all-to-all-start.4) | async-done | bytes 20971552 | tf_op jit(solution)/shard_map/all_to_all | solution.py:309
  1927.2 48.8 %multiply_convert_fusion.2 = (bf16[5120,704]{0,1:T(8,128)(2,1)S(1)}, bf16[5120,704]{0,1:T(8,128)(2,1)}, bf16[5120,704]{0,1:T(8,128)(2,1)}) fusion(f32[5120,1408]{0,1:T(8,128)} %fusion.48, bf16[5120,2048]{1,0:T(8,128)(2,1)} %bitcast.36, bf16[1,704,2048]{2,1,0:T(8,128)(2,1)S(1)} %copy-done), kind=kOutput, calls=%fused_computation.61 | convolution fusion | flops 14818017280 | bytes 74317824 | tf_op jit(solution)/shard_map/rd,fd->rf/dot_general | solution.py:62
  1976.0 41.3 convolution_convert_fusion.1
  2022.0 12.6 fusion.116
  2034.6 466.5 %all-gather.25.cloned.1.call-done = bf16[2816,2048]{1,0:T(8,128)(2,1)} async-done(((bf16[704,2048]{1,0:T(8,128)(2,1)}), bf16[2816,2048]{1,0:T(8,128)(2,1)}) %all-gather.25.cloned.1.call-update) | async-done | bytes 11534352 | tf_op jit(solution)/shard_map/all_gather | solution.py:229
  2501.1 12.0 multiply_convert_fusion.7
  2514.2 9.3 fusion.82
  2524.3 193.5 %all-to-all-done.5 = bf16[32,160,2048]{2,1,0:T(8,128)(2,1)} async-done(((bf16[32,160,2048]{2,1,0:T(8,128)(2,1)}), bf16[32,160,2048]{2,1,0:T(8,128)(2,1)}, u32[]{:S(2)}, u32[]{:S(2)}) %all-to-all-start.5) | async-done | bytes 20971552 | tf_op jit(solution)/shard_map/all_to_all | solution.py:328
  2717.8 20.6 convert_reduce_fusion
  2738.5 19.9 gather_fusion.1
  2758.3 15.4 reshape.667
  2773.8 10.0 reduce_sum.175
  2783.8 14.7 multiply_reduce_fusion.3
  2809.7 54.9 %all-to-all-start.6 = ((bf16[1,256,16,128]{3,1,0,2:T(8,128)(2,1)}), bf16[1,256,16,128]{3,1,0,2:T(8,128)(2,1)}, u32[]{:S(2)}, u32[]{:S(2)}) async-start(bf16[1,256,16,128]{3,1,0,2:T(8,128)(2,1)} %copy.168), calls=%async_computation.6 | async-start | bytes 2097152 | tf_op jit(solution)/shard_map/all_to_all | solution.py:362
  2867.1 13.0 all-to-all-done.6
  2882.4 154.2 %while.40 = (s32[]{:T(128)}, f32[2048,2,192]{0,2,1:T(8,128)}, f32[2048,2,128]{0,2,1:T(8,128)}, bf16[4,512,2,192]{1,3,2,0:T(8,128)(2,1)}, s32[4]{0:T(128)S(1)}, /...) while((s32[]{:T(128)}, f32[2048,2,192]{0,2,1:T(8,128)}, ...), condition=%wide.region_19.20_spmd.clone, body=%wide.region_17.19_spmd.clone.sunk | while | flops 3525770752 | bytes 153125392 | solution.py:179
  2912.2 7.5 fusion.181
  2950.4 8.1 fusion.181
  2989.3 8.1 fusion.181
  3028.3 8.1 fusion.181
  3049.3 11.1 copy.172
  3060.4 52.7 %all_to_all.83 = bf16[1,2048,2,512]{3,2,0,1:T(2,128)(2,1)S(1)} all-to-all(bf16[1,2048,2,512]{3,2,0,1:T(2,128)(2,1)} %copy.172), channel_id=1, replica_groups=mesh['dp'=4,'seq'=8] {'seq'}, dimensions={1} | all-to-all | bytes 8388608 | tf_op jit(solution)/shard_map/all_to_all | solution.py:366
  3130.0 20.1 fusion.78
  3150.1 10.2 fusion.90
  3179.7 10.5 fusion.88
  3190.2 22.8 convolution_convert_fusion
  3226.5 166.3 %reduce-scatter.11.cloned.1.call-done = f32[16,4096]{1,0:T(8,128)} async-done(((f32[512,4096]{1,0:T(8,128)}), f32[16,4096]{1,0:T(8,128)}) %reduce-scatter.11.cloned.1.call-update) | async-done | bytes 262160 | tf_op jit(solution)/shard_map/reduce_scatter | solution.py:427
  3394.5 600.2 %reduce-scatter.15.cloned.1.call-done = f32[64,5632]{1,0:T(8,128)} async-done(((f32[2048,5632]{1,0:T(8,128)}), f32[64,5632]{1,0:T(8,128)}) %reduce-scatter.15.cloned.1.call-update) | async-done | bytes 1441808 | tf_op jit(solution)/shard_map/reduce_scatter | solution.py:430
  3999.1 41.5 fusion.44
  4040.6 239.5 %reduce-scatter.13.cloned.1.call-done = f32[64,2048]{1,0:T(8,128)} async-done(((f32[2048,2048]{1,0:T(8,128)}), f32[64,2048]{1,0:T(8,128)}) %reduce-scatter.13.cloned.1.call-update) | async-done | bytes 524304 | tf_op jit(solution)/shard_map/reduce_scatter | solution.py:428
  4282.2 21.3 convolution_bitcast_fusion
  4303.5 11.5 all-gather.35.cloned.1.call-done
  4320.1 246.6 %reduce-scatter.7.cloned.1.call-done = f32[64,3072]{1,0:T(8,128)} async-done(((f32[2048,3072]{1,0:T(8,128)}), f32[64,3072]{1,0:T(8,128)}) %reduce-scatter.7.cloned.1.call-update) | async-done | bytes 786448 | tf_op jit(solution)/shard_map/reduce_scatter | solution.py:424
  4568.7 20.5 convert_reduce_fusion.1
  4589.1 19.6 gather_fusion
  4608.8 15.1 reshape.660
  4623.8 12.2 multiply_reduce_fusion.1
  4636.7 10.2 fusion.65
  4656.6 41.0 all-reduce.6
  4698.5 12.7 all-reduce.7
  4718.0 10.0 all_gather.65
  4737.2 42.5 all-gather.33.cloned.1.call-done
  4779.7 8.6 convert_element_type.260
  4788.3 21.3 all-gather.31.cloned.1.call-done
  4813.7 30.1 all-gather.27.cloned.1.call-done
  (445 shorter events, 393.9 us)
Async XLA Ops:
  7.2 1920.0 %copy-start = (bf16[1,704,2048]{2,1,0:T(8,128)(2,1)S(1)}, bf16[1,704,2048]{2,1,0:T(8,128)(2,1)}, u32[]{:S(2)}) copy-start(bf16[1,704,2048]{2,1,0:T(8,128)(2,1)} %param.34) | copy-start | bytes 8650756
  7.2 15.8 copy-start.66
  7.2 15.9 copy-start.67
  7.2 55.6 %all-gather.17.cloned.1.call-start = ((), (), s32[]{:S(2)}) async-start(), calls=%async_computation.15 | async-start | bytes 2949120 | tf_op jit(solution)/shard_map/all_gather | solution.py:223
  8.0 136.1 %all-gather.19.cloned.1.call-start = ((), (), s32[]{:S(2)}) async-start(), calls=%async_computation.16 | async-start | bytes 5242880 | tf_op jit(solution)/shard_map/all_gather | solution.py:225
  8.7 353.7 %all-gather.15.cloned.1.call-start = ((), (), s32[]{:S(2)}) async-start(), calls=%async_computation.14 | async-start | bytes 15728640 | tf_op jit(solution)/shard_map/all_gather | solution.py:222
  23.0 356.0 %copy-start.30 = (f32[4,1,512]{2,1,0:T(1,128)}, f32[4,1,512]{2,1,0:T(1,128)S(1)}, u32[]{:S(2)}) copy-start(f32[4,1,512]{2,1,0:T(1,128)S(1)} %convert_element_type.266) | copy-start | bytes 24580
  23.1 11.9 copy-start.52
  32.8 116.1 %copy-start.41 = (f32[4,1,128]{2,1,0:T(1,128)}, f32[4,1,128]{2,1,0:T(1,128)S(1)}, u32[]{:S(2)}) copy-start(f32[4,1,128]{2,1,0:T(1,128)S(1)} %convert_element_type.267) | copy-start | bytes 6148
  34.9 344.1 %copy-start.38 = (f32[256]{0:T(256)}, f32[256]{0:T(256)S(1)}, u32[]{:S(2)}) copy-start(f32[256]{0:T(256)S(1)} %get-tuple-element.512) | copy-start | bytes 3076
  65.7 87.4 %copy-start.15 = (f32[256,576]{0,1:T(8,128)}, f32[256,576]{0,1:T(8,128)S(1)}, u32[]{:S(2)}) copy-start(f32[256,576]{0,1:T(8,128)S(1)} %fusion.97) | copy-start | bytes 1769476
  390.0 53.8 %all-to-all-start = ((bf16[1,256,16,512]{1,3,0,2:T(8,128)(2,1)}), bf16[1,256,16,512]{1,3,0,2:T(8,128)(2,1)}, u32[]{:S(2)}, u32[]{:S(2)}) async-start(bf16[1,256,16,512]{1,3,0,2:T(8,128)(2,1)} %bitcast.281), calls=%async_computation | async-start | bytes 8388608 | tf_op jit(solution)/shard_map/all_to_all | solution.py:260
  394.7 163.3 %all-gather.21.cloned.1.call-start = ((), (), s32[]{:S(2)}) async-start(), calls=%async_computation.17 | async-start | bytes 10485760 | tf_op jit(solution)/shard_map/all_gather | solution.py:226
  527.5 12.6 copy-start.65
  531.1 22.2 all-to-all-start.1
  552.6 12.4 copy-start.45
  553.4 92.9 %copy-start.47 = (s32[1536]{0:T(1024)}, s32[1536]{0:T(1024)S(1)}, u32[]{:S(2)}) copy-start(s32[1536]{0:T(1024)S(1)} %fusion.104) | copy-start | bytes 18436
  565.0 8.0 copy-start.54
  613.7 471.0 %all-to-all-start.2 = ((bf16[32,160,2048]{2,1,0:T(8,128)(2,1)}), bf16[32,160,2048]{2,1,0:T(8,128)(2,1)}, u32[]{:S(2)}, u32[]{:S(2)}) async-start(bf16[32,160,2048]{2,1,0:T(8,128)(2,1)} %bitcast.262), calls=%async_computation.2 | async-start | bytes 41943040 | tf_op jit(solution)/shard_map/all_to_all | solution.py:308
  630.3 15.7 copy-start.57
  646.1 17.6 copy-start.27
  1097.8 829.4 %all-to-all-start.4 = ((bf16[32,160,2048]{2,1,0:T(8,128)(2,1)}), bf16[32,160,2048]{2,1,0:T(8,128)(2,1)}, u32[]{:S(2)}, u32[]{:S(2)}) async-start(bf16[32,160,2048]{2,1,0:T(8,128)(2,1)} %bitcast.263), calls=%async_computation.4 | async-start | bytes 41943040 | tf_op jit(solution)/shard_map/all_to_all | solution.py:309
  1101.8 920.2 %all-gather.23.cloned.1.call-start = ((), (), s32[]{:S(2)}) async-start(), calls=%async_computation.18 | async-start | bytes 28835840 | tf_op jit(solution)/shard_map/all_gather | solution.py:228
  1976.0 41.4 copy-start.69
  2017.4 700.5 %all-to-all-start.5 = ((bf16[32,160,2048]{2,1,0:T(8,128)(2,1)}), bf16[32,160,2048]{2,1,0:T(8,128)(2,1)}, u32[]{:S(2)}, u32[]{:S(2)}) async-start(bf16[32,160,2048]{2,1,0:T(8,128)(2,1)} %bitcast.270), calls=%async_computation.5 | async-start | bytes 41943040 | tf_op jit(solution)/shard_map/all_to_all | solution.py:328
  2021.4 479.7 %all-gather.25.cloned.1.call-start = ((), (), s32[]{:S(2)}) async-start(), calls=%async_computation.19 | async-start | bytes 14417920 | tf_op jit(solution)/shard_map/all_gather | solution.py:229
  2021.9 1138.4 %reduce-scatter.17.cloned.1.call-start = ((), (), s32[]{:S(2)}) async-start(), calls=%async_computation.29 | async-start | bytes 23789568 | tf_op jit(solution)/shard_map/reduce_scatter | solution.py:431
  2501.1 13.1 copy-start.13
  2524.3 214.2 %copy-start.43 = (s32[2048]{0:T(1024)}, s32[2048]{0:T(1024)S(1)}, u32[]{:S(2)}) copy-start(s32[2048]{0:T(1024)S(1)} %pad_clamp_fusion) | copy-start | bytes 24580
  2773.8 10.0 copy-start.46
  2773.8 10.0 copy-start.55
  2783.8 14.7 copy-start.61
  2809.7 70.4 %all-to-all-start.6 = ((bf16[1,256,16,128]{3,1,0,2:T(8,128)(2,1)}), bf16[1,256,16,128]{3,1,0,2:T(8,128)(2,1)}, u32[]{:S(2)}, u32[]{:S(2)}) async-start(bf16[1,256,16,128]{3,1,0,2:T(8,128)(2,1)} %copy.168), calls=%async_computation.6 | async-start | bytes 2097152 | tf_op jit(solution)/shard_map/all_to_all | solution.py:362
  2864.6 528.2 %reduce-scatter.11.cloned.1.call-start = ((), (), s32[]{:S(2)}) async-start(), calls=%async_computation.23 | async-start | bytes 8650752 | tf_op jit(solution)/shard_map/reduce_scatter | solution.py:427
  2893.2 7.1 copy-start.2
  2893.2 7.1 slice-start
  2893.2 7.1 slice-start.1
  2930.5 7.1 copy-start.2
  2930.5 7.1 slice-start
  2930.5 7.1 slice-start.1
  2969.3 7.1 copy-start.2
  2969.4 7.1 slice-start
  3008.3 7.2 copy-start.2
  3008.3 7.2 slice-start
  3008.3 7.1 slice-start.1
  3129.9 864.7 %reduce-scatter.15.cloned.1.call-start = ((), (), s32[]{:S(2)}) async-start(), calls=%async_computation.27 | async-start | bytes 47579136 | tf_op jit(solution)/shard_map/reduce_scatter | solution.py:430
  3150.1 1130.0 %reduce-scatter.13.cloned.1.call-start = ((), (), s32[]{:S(2)}) async-start(), calls=%async_computation.25 | async-start | bytes 17301504 | tf_op jit(solution)/shard_map/reduce_scatter | solution.py:428
  3160.3 1154.6 %all-gather.35.cloned.1.call-start = ((), (), s32[]{:S(2)}) async-start(), calls=%async_computation.30 | async-start | bytes 3244032 | tf_op jit(solution)/shard_map/all_gather | solution.py:458
  3162.3 1404.4 %reduce-scatter.7.cloned.1.call-start = ((), (), s32[]{:S(2)}) async-start(), calls=%async_computation.20 | async-start | bytes 25952256 | tf_op jit(solution)/shard_map/reduce_scatter | solution.py:424
  3172.3 7.3 copy-start.31
  3172.3 7.3 copy-start.39
  3176.9 45.4 copy-start.33
  3176.9 45.4 copy-start.35
  3213.0 1355.6 %all-to-all-start.3 = ((bf16[32,160,2048]{2,1,0:T(8,128)(2,1)}), bf16[32,160,2048]{2,1,0:T(8,128)(2,1)}, u32[]{:S(2)}, u32[]{:S(2)}) async-start(bf16[32,160,2048]{2,1,0:T(8,128)(2,1)} %bitcast.269), calls=%async_computation.3 | async-start | bytes 41943040 | tf_op jit(solution)/shard_map/all_to_all | solution.py:321
  3217.2 1499.8 %reduce-scatter.9.cloned.1.call-start = ((), (), s32[]{:S(2)}) async-start(), calls=%async_computation.22 | async-start | bytes 5406720 | tf_op jit(solution)/shard_map/reduce_scatter | solution.py:425
  3226.5 770.7 %copy-start.68 = (u32[32]{0:T(128)S(1)}, u32[32]{0:T(128)}, u32[]{:S(2)}) copy-start(u32[32]{0:T(128)} %constant.187) | copy-start | bytes 388
  3226.5 1508.0 %all-gather.29.cloned.1.call-start = ((), (), s32[]{:S(2)}) async-start(), calls=%async_computation.24 | async-start | bytes 1179648 | tf_op jit(solution)/shard_map/all_gather | solution.py:446
  3394.4 1385.3 %all-gather.33.cloned.1.call-start = ((), (), s32[]{:S(2)}) async-start(), calls=%async_computation.28 | async-start | bytes 6488064 | tf_op jit(solution)/shard_map/all_gather | solution.py:455
  3997.0 812.6 %all-gather.31.cloned.1.call-start = ((), (), s32[]{:S(2)}) async-start(), calls=%async_computation.26 | async-start | bytes 2359296 | tf_op jit(solution)/shard_map/all_gather | solution.py:449
  4281.9 561.9 %all-gather.27.cloned.1.call-start = ((), (), s32[]{:S(2)}) async-start(), calls=%async_computation.21 | async-start | bytes 3538944 | tf_op jit(solution)/shard_map/all_gather | solution.py:437
  4568.6 20.5 copy-start.44
  4608.8 15.1 copy-start.28
  4636.7 10.2 copy-start.20
  4653.9 59.0 %copy-start.60 = (f32[256]{0:T(256)S(1)}, f32[256]{0:T(256)}, u32[]{:S(2)}) copy-start(f32[256]{0:T(256)} %get-tuple-element.511) | copy-start | bytes 3076
  (62 other events, 253.8 us)
Sparse Core Ops, SparseCore 0:
  9.6 53.1 all-gather.16
  64.4 79.6 all-gather.18
  145.6 216.7 all-gather.14
  396.8 148.2 all-gather.20
  1103.9 799.2 all-gather.22
  2023.5 477.6 all-gather.24
  2523.7 284.0 reduce-scatter.16
  3130.0 262.7 reduce-scatter.10
  3395.1 599.4 reduce-scatter.14
  3996.8 283.2 reduce-scatter.12
  4282.0 32.9 all-gather.34
  4321.2 245.4 reduce-scatter.6
  4569.7 142.6 reduce-scatter.8
  4714.2 20.1 all-gather.28
  4736.3 43.3 all-gather.32
  4781.6 27.8 all-gather.30
  4811.4 32.3 all-gather.26
where the time goes:
time: 4870 us; the launch traced here: 4860 us
  waiting for transfers between devices  3610 us (74%)
  matrix products  511 us (10%)
  local copies, waits for them, and re-layouts  278 us (6%)
  other arithmetic  188 us (4%)
  blocking collectives  152 us (3%)
  starting transfers between devices  81.7 us (2%)
    all_to_all x1, waiting for transfers between devices, on_device(): lax.all_to_all(send_upstream, ('dp', 'seq'), split_axis=0, concat_axis=0,...  787 us
    reduce_scatter x1, waiting for transfers between devices, on_device(): lax.psum_scatter(local_grads[7], ('dp', 'seq'), scatter_dimension=0, tile...  600 us
    all_gather x1, waiting for transfers between devices, on_device(): lax.all_gather(w_shared_out, 'dp', axis=0, tiled=True)  466 us
    all_to_all x1, waiting for transfers between devices, on_device(): lax.all_to_all(send_rows, ('dp', 'seq'), split_axis=0, concat_axis=0, til...  421 us
    reduce_scatter x1, waiting for transfers between devices, on_device(): lax.psum_scatter(local_grads[1], ('dp', 'seq'), scatter_dimension=0, tile...  247 us
    reduce_scatter x1, waiting for transfers between devices, on_device(): lax.psum_scatter(local_grads[5], ('dp', 'seq'), scatter_dimension=0, tile...  240 us
    all_gather x1, waiting for transfers between devices, on_device(): lax.all_gather(w_query, 'dp', axis=0, tiled=True)  209 us
    all_to_all x1, waiting for transfers between devices, on_device(): lax.all_to_all(back_low.reshape(device_count, slot_count, feature_count),...  194 us
  transfers between devices with their start and end apart: 24, of which 18 were waited for; matrix products, arithmetic and copies ran while one was open for 18% of the time, Pallas kernels for 0%

commit v1 on v0

v1 whole, which is shorter than its diff:
```python
import math

import jax
import jax.numpy as jnp
from jax import lax
from jax.sharding import PartitionSpec as P

HEADS = 16
NOPE = 128
ROPE = 64
VDIM = 128
LATENT = 512
TOP = 6
QK = 192
SH_FF = 2816
HALF = 704
EPSILON = 1e-06
BF = jnp.bfloat16
F32 = jnp.float32


def rms_scale(entries):
    return lax.rsqrt(jnp.mean(entries * entries, axis=-1, keepdims=True) + EPSILON)


def rotary_angles(position_rows):
    steps_index = jnp.arange(ROPE // 2, dtype=F32)
    frequency = 10000.0 ** (-2.0 * steps_index / ROPE)
    return position_rows.astype(F32)[..., None] * frequency


def rotate(values, cosine_values, sine_values):
    half_width = values.shape[-1] // 2
    front_half = values[..., :half_width]
    back_half = values[..., half_width:]
    return jnp.concatenate(
        [
            front_half * cosine_values - back_half * sine_values,
            front_half * sine_values + back_half * cosine_values,
        ],
        axis=-1,
    )


def norm_backward(upstream, entries, inverse_scale, gain_row):
    scaled = upstream * gain_row
    return inverse_scale * scaled - entries * inverse_scale**3 * jnp.mean(
        scaled * entries, axis=-1, keepdims=True
    )


def dot(a, b):
    return jnp.dot(a, b, preferred_element_type=F32)


def dot_nt(a, b):
    return jnp.einsum("ik,jk->ij", a, b, preferred_element_type=F32)


def dot_tn(a, b):
    return jnp.einsum("ki,kj->ij", a, b, preferred_element_type=F32)


def attention_forward(queries, keys_all, values_all):
    length, head_count, head_width = queries.shape
    block_rows = min(512, length)
    scale_factor = 1.0 / math.sqrt(head_width)
    outs = []
    logs = []
    for start in range(0, length, block_rows):
        end = start + block_rows
        scores = (
            jnp.einsum(
                "qhd,khd->hqk", queries[start:end], keys_all[:end], preferred_element_type=F32
            )
            * scale_factor
        )
        allowed = jnp.arange(end)[None, :] <= (start + jnp.arange(block_rows))[:, None]
        scores = jnp.where(allowed[None], scores, -1e30)
        largest = jnp.max(scores, axis=-1, keepdims=True)
        weights = jnp.exp(scores - largest)
        totals = jnp.sum(weights, axis=-1, keepdims=True)
        shares = (weights / totals).astype(BF)
        attended = jnp.einsum("hqk,khd->qhd", shares, values_all[:end], preferred_element_type=F32)
        outs.append(attended.astype(BF))
        logs.append((largest + jnp.log(totals))[..., 0])
    return jnp.concatenate(outs, axis=0), logs


def attention_backward(queries, keys_all, values_all, logs, upstream_heads):
    length, head_count, head_width = queries.shape
    block_rows = min(512, length)
    scale_factor = 1.0 / math.sqrt(head_width)
    key_sums = jnp.zeros((length, head_count, head_width), F32)
    value_sums = jnp.zeros((length, head_count, VDIM), F32)
    query_grads = []
    for index, start in enumerate(range(0, length, block_rows)):
        end = start + block_rows
        query_rows = queries[start:end]
        upstream = upstream_heads[start:end]
        scores = (
            jnp.einsum("qhd,khd->hqk", query_rows, keys_all[:end], preferred_element_type=F32)
            * scale_factor
        )
        allowed = jnp.arange(end)[None, :] <= (start + jnp.arange(block_rows))[:, None]
        scores = jnp.where(allowed[None], scores, -1e30)
        shares = jnp.exp(scores - logs[index][..., None])
        share_grad = jnp.einsum(
            "qhd,khd->hqk", upstream, values_all[:end], preferred_element_type=F32
        )
        centre = jnp.sum(shares * share_grad, axis=-1, keepdims=True)
        score_grad = (shares * (share_grad - centre)).astype(BF)
        query_grads.append(
            jnp.einsum("hqk,khd->qhd", score_grad, keys_all[:end], preferred_element_type=F32)
            * scale_factor
        )
        key_sums = key_sums.at[:end].add(
            jnp.einsum("hqk,qhd->khd", score_grad, query_rows, preferred_element_type=F32)
            * scale_factor
        )
        value_sums = value_sums.at[:end].add(
            jnp.einsum("hqk,qhd->khd", shares.astype(BF), upstream, preferred_element_type=F32)
        )
    return (
        jnp.concatenate(query_grads, axis=0).astype(BF),
        key_sums.astype(BF),
        value_sums.astype(BF),
    )


def on_device(
    hidden_in,
    positions,
    expert_ids,
    gate_weights,
    attention_gain,
    w_query,
    w_compress,
    latent_gain,
    w_expand,
    w_output,
    feedforward_gain,
    w_shared_in,
    w_shared_out,
    w_expert_in,
    w_expert_out,
    cotangent,
):
    n_dp = lax.axis_size("dp")
    n_seq = lax.axis_size("seq")
    n_all = n_dp * n_seq
    both = ("dp", "seq")
    dp_index = lax.axis_index("dp")
    seq_index = lax.axis_index("seq")
    sequence_count, rows, features = hidden_in.shape
    rows = sequence_count * rows
    length = rows * n_seq
    heads = HEADS // n_seq
    shard = features // n_dp
    expert_count = n_all // 2
    capacity = max(2, rows * TOP * 5 // (expert_count * 3))
    units = SH_FF // n_all

    hidden = hidden_in.reshape(rows, features)
    upstream_rows = cotangent.reshape(rows, features)
    upstream_float = upstream_rows.astype(F32)
    id_rows = expert_ids.reshape(rows, TOP)
    gate_table = gate_weights.reshape(rows, TOP)

    hidden_all = lax.all_gather(hidden, "seq", axis=0, tiled=True)
    gains = lax.all_gather(
        jnp.concatenate([attention_gain, feedforward_gain, latent_gain]), "dp", axis=0
    ).astype(F32)
    first_gain = gains[:, :shard].reshape(features)
    second_gain = gains[:, shard : 2 * shard].reshape(features)
    latent_gain_row = gains[:, 2 * shard :].reshape(LATENT)
    positions_all = lax.all_gather(positions.reshape(rows), "seq", axis=0, tiled=True)
    query_part = lax.dynamic_slice_in_dim(w_query, seq_index * heads * QK, heads * QK, 1)
    expand_part = lax.dynamic_slice_in_dim(
        w_expand, seq_index * heads * (NOPE + VDIM), heads * (NOPE + VDIM), 1
    )
    query_weight = lax.all_gather(query_part, "dp", axis=0, tiled=True)
    compress_weight = lax.all_gather(w_compress, "dp", axis=0, tiled=True)
    expand_weight = lax.all_gather(expand_part, "dp", axis=0, tiled=True)
    output_weight = lax.all_gather(w_output, "dp", axis=0, tiled=True)
    shared_part = lax.dynamic_index_in_dim(
        w_shared_in.reshape(shard, 2, n_dp, n_seq, units), seq_index, 3, keepdims=False
    )
    shared_in = (
        lax.all_to_all(
            shared_part.transpose(2, 0, 1, 3), "dp", split_axis=0, concat_axis=0, tiled=True
        )
        .reshape(features, 2 * units)
    )
    shared_out = lax.dynamic_slice_in_dim(w_shared_out, seq_index * units, units, 0)
    upstream_all = lax.all_gather(upstream_rows, both, axis=0, tiled=True)
    ids_all = lax.all_gather(id_rows.T, both, axis=0)
    gates_all = lax.all_gather(gate_table.T, both, axis=0)

    hidden_all_float = hidden_all.astype(F32)
    normed_all = (hidden_all_float * rms_scale(hidden_all_float) * first_gain).astype(BF)
    angles = rotary_angles(positions_all)
    cosine_all, sine_all = jnp.cos(angles), jnp.sin(angles)
    query_raw = dot(normed_all, query_weight).reshape(length, heads, QK)
    queries = jnp.concatenate(
        [
            query_raw[..., :NOPE],
            rotate(query_raw[..., NOPE:], cosine_all[:, None], sine_all[:, None]),
        ],
        axis=-1,
    ).astype(BF)
    compressed = dot(normed_all, compress_weight)
    latent = compressed[:, :LATENT]
    key_rotary = rotate(compressed[:, LATENT:], cosine_all, sine_all)
    latent_scale = rms_scale(latent)
    latent_normed = (latent * latent_scale * latent_gain_row).astype(BF)
    expanded = dot(latent_normed, expand_weight).reshape(length, heads, NOPE + VDIM)
    keys_all = jnp.concatenate(
        [expanded[..., :NOPE], jnp.broadcast_to(key_rotary[:, None, :], (length, heads, ROPE))],
        axis=-1,
    ).astype(BF)
    values_all = expanded[..., NOPE:].astype(BF)
    attended_heads, logs = attention_forward(queries, keys_all, values_all)
    attended = lax.all_to_all(
        attended_heads.reshape(length, heads * VDIM), "seq", split_axis=0, concat_axis=1, tiled=True
    )
    hidden_float = hidden.astype(F32)
    middle = hidden_float + dot(attended, output_weight)
    second_scale = rms_scale(middle)
    moe_rows = (middle * second_scale * second_gain).astype(BF)

    rows_all = lax.all_gather(moe_rows, both, axis=0, tiled=True)
    attended_all = lax.all_gather(attended, "seq", axis=0, tiled=True)
    expert = (dp_index * n_seq + seq_index) // 2
    named = ids_all == expert
    chosen = jnp.any(named, axis=1)
    gate_rows = jnp.sum(jnp.where(named, gates_all, 0.0), axis=1)
    before = (jnp.arange(rows)[:, None] < jnp.arange(rows)[None, :]).astype(BF)
    place = dot(chosen.astype(BF), before).astype(jnp.int32)
    picked = chosen[:, None, :] & (
        place[:, None, :] == jnp.arange(capacity, dtype=jnp.int32)[None, :, None]
    )
    pick = picked.astype(BF)
    gate_slots = jnp.sum(jnp.where(picked, gate_rows[:, None, :], 0.0), axis=2)[..., None]
    rows_blocks = rows_all.reshape(n_all, rows, features)
    upstream_blocks = upstream_all.reshape(n_all, rows, features)
    slot_rows = jnp.einsum("bst,btd->bsd", pick, rows_blocks, preferred_element_type=F32)
    slot_rows = slot_rows.astype(BF).reshape(n_all * capacity, features)
    slot_cot = jnp.einsum("bst,btd->bsd", pick, upstream_blocks, preferred_element_type=F32)
    slot_upstream = (slot_cot * gate_slots).astype(BF).reshape(n_all * capacity, features)
    weight_in, weight_out = w_expert_in[0], w_expert_out[0]

    def gated(rows_in, upstream, w_in, w_out, width):
        gate_up = dot(rows_in, w_in)
        gate, up = gate_up[:, :width], gate_up[:, width:]
        sigmoid = 1.0 / (1.0 + jnp.exp(-gate))
        active = gate * sigmoid
        hidden_units = (active * up).astype(BF)
        hidden_back = dot_nt(upstream, w_out)
        gate_back = hidden_back * up * sigmoid * (1.0 + gate * (1.0 - sigmoid))
        both_back = jnp.concatenate([gate_back, hidden_back * active], axis=-1).astype(BF)
        return hidden_units, both_back, dot_tn(rows_in, both_back), dot_tn(hidden_units, upstream)

    hidden_units, both_back, expert_in_grad, expert_out_grad = gated(
        slot_rows, slot_upstream, weight_in, weight_out, HALF
    )
    slot_result = dot(hidden_units, weight_out).astype(BF)
    slot_back = dot_nt(both_back, weight_in).astype(BF)
    shared_units, shared_both_back, shared_in_grad, shared_out_grad = gated(
        rows_all, upstream_all, shared_in, shared_out, units
    )
    slot_back = slot_back.reshape(n_all, capacity, features)
    back_part = jnp.einsum("bst,bsd->btd", pick, slot_back, preferred_element_type=F32)
    back_part = back_part.reshape(n_all * rows, features) + dot_nt(shared_both_back, shared_in)
    back_sum = lax.psum_scatter(back_part.astype(BF), both, scatter_dimension=0, tiled=True)

    slot_float = slot_result.astype(F32).reshape(n_all, capacity, features)
    slot_gate_grad = jnp.sum(slot_float * slot_cot, axis=-1)
    weighted = (slot_float * gate_slots).astype(BF)
    out_part = jnp.einsum("bst,bsd->btd", pick, weighted, preferred_element_type=F32)
    out_part = out_part.reshape(n_all * rows, features) + dot(shared_units, shared_out)
    out_sum = lax.psum_scatter(out_part.astype(BF), both, scatter_dimension=0, tiled=True)
    token_gate_grad = jnp.sum(jnp.where(picked, slot_gate_grad[..., None], 0.0), axis=1)
    gate_grads = lax.all_to_all(token_gate_grad, both, split_axis=0, concat_axis=0, tiled=True)
    gate_grads = jnp.sum(gate_grads.reshape(expert_count, 2, rows), axis=1)
    gate_gradient = jnp.sum(
        jnp.where(
            id_rows[:, :, None] == jnp.arange(expert_count, dtype=jnp.int32),
            gate_grads.T[:, None, :],
            0.0,
        ),
        axis=-1,
    )
    block_out = (middle + out_sum.astype(F32)).astype(BF)

    moe_back = back_sum.astype(F32)
    second_gain_grad = jnp.sum(moe_back * middle * second_scale, axis=0)
    middle_back = upstream_float + norm_backward(moe_back, middle, second_scale, second_gain)
    middle_low = middle_back.astype(BF)
    middle_columns = lax.all_to_all(middle_low, "seq", split_axis=1, concat_axis=0, tiled=True)
    output_grad = dot_tn(attended_all, middle_columns)
    attended_back = dot_nt(middle_low, output_weight).astype(BF)
    upstream_heads = lax.all_to_all(
        attended_back, "seq", split_axis=1, concat_axis=0, tiled=True
    ).reshape(length, heads, VDIM)
    query_back, key_back, value_back = attention_backward(
        queries, keys_all, values_all, logs, upstream_heads
    )
    query_raw_back = (
        jnp.concatenate(
            [
                query_back[..., :NOPE].astype(F32),
                rotate(query_back[..., NOPE:].astype(F32), cosine_all[:, None], -sine_all[:, None]),
            ],
            axis=-1,
        )
        .astype(BF)
        .reshape(length, heads * QK)
    )
    expanded_back = jnp.concatenate([key_back[..., :NOPE], value_back], axis=-1).reshape(
        length, heads * (NOPE + VDIM)
    )
    query_grad = dot_tn(normed_all, query_raw_back)
    expand_grad = dot_tn(latent_normed, expanded_back)
    partial_back = jnp.concatenate(
        [
            dot_nt(query_raw_back, query_weight),
            dot_nt(expanded_back, expand_weight),
            jnp.sum(key_back[..., NOPE:].astype(F32), axis=1),
        ],
        axis=-1,
    ).astype(BF)
    summed_back = lax.psum_scatter(partial_back, "seq", scatter_dimension=0, tiled=True).astype(F32)
    latent_normed_back = summed_back[:, features : features + LATENT]
    own = seq_index * rows

    def mine(array):
        return lax.dynamic_slice_in_dim(array, own, rows, 0)

    latent_own, latent_scale_own = mine(latent), mine(latent_scale)
    latent_gain_grad = jnp.sum(latent_normed_back * latent_own * latent_scale_own, axis=0)
    latent_back = norm_backward(latent_normed_back, latent_own, latent_scale_own, latent_gain_row)
    rotary_back = rotate(summed_back[:, features + LATENT :], mine(cosine_all), -mine(sine_all))
    compressed_back = jnp.concatenate([latent_back, rotary_back], axis=-1).astype(BF)
    compressed_back_all = lax.all_gather(compressed_back, "seq", axis=0, tiled=True)
    width = (LATENT + ROPE) // n_seq
    compress_grad = dot_tn(
        normed_all, lax.dynamic_slice_in_dim(compressed_back_all, seq_index * width, width, 1)
    )
    normed_back = summed_back[:, :features] + dot_nt(compressed_back, compress_weight)
    first_scale = rms_scale(hidden_float)
    first_gain_grad = jnp.sum(normed_back * hidden_float * first_scale, axis=0)
    hidden_gradient = (
        middle_back + norm_backward(normed_back, hidden_float, first_scale, first_gain)
    ).astype(BF)

    gain_grads = lax.psum(
        jnp.concatenate([first_gain_grad, second_gain_grad, latent_gain_grad]), both
    )
    latent_shard = LATENT // n_dp

    def gain_part(start, size):
        return lax.dynamic_slice_in_dim(gain_grads, start + dp_index * size, size, 0)

    def over_dp(grad):
        return lax.psum_scatter(grad, "dp", scatter_dimension=0, tiled=True).astype(BF)

    def columns(part):
        return lax.all_gather(part, "seq", axis=1, tiled=True).astype(F32)

    shared_in_out = lax.all_to_all(
        shared_in_grad.astype(BF).reshape(n_dp, shard, 2, units),
        "dp",
        split_axis=0,
        concat_axis=0,
        tiled=True,
    )
    shared_in_out = lax.all_gather(shared_in_out, "seq", axis=0)
    shared_in_out = shared_in_out.transpose(2, 3, 1, 0, 4).reshape(shard, 2 * SH_FF).astype(F32)
    shared_out_out = lax.all_gather(
        shared_out_grad.astype(BF), "seq", axis=0, tiled=True
    ).astype(F32)
    return (
        block_out.reshape(hidden_in.shape),
        hidden_gradient.reshape(hidden_in.shape),
        gate_gradient.reshape(gate_weights.shape),
        gain_part(0, shard),
        columns(over_dp(query_grad)),
        columns(over_dp(compress_grad)),
        gain_part(2 * features, latent_shard),
        columns(over_dp(expand_grad)),
        columns(over_dp(output_grad)),
        gain_part(features, shard),
        shared_in_out,
        shared_out_out,
        expert_in_grad[None],
        expert_out_grad[None],
    )


def solution(mesh):
    token = P("dp", "seq", None)
    row = P("dp", None)
    half = P(("dp", "seq"), None, None)
    return jax.shard_map(
        on_device,
        mesh=mesh,
        in_specs=(
            token, P("dp", "seq"), token, token, P("dp"), row, row, P("dp"), row, row,
            P("dp"), row, row, half, half, token,
        ),
        out_specs=(
            token, token, token, P("dp"), row, row, P("dp"), row, row, P("dp"), row, row,
            half, half,
        ),
        check_vma=False,
    )
```

time: 4870 us -> 2330 us (0.48)
  waiting for transfers between devices: 3610 us -> 1100 us
  blocking collectives: 152 us -> 233 us
  starting transfers between devices: 81.7 us -> 23 us
  matrix products: 511 us -> 560 us
    all_to_all x7 -> x5, waiting for transfers between devices: 1460 us -> 39.5 us  [the longest x1 24.5 us: on_device(): lax.all_to_all(attended_back, 'seq', split_axis=1, concat_axis=0, tiled=T...]
    all_gather x11 -> x13, waiting for transfers between devices: 891 us -> 329 us  [the longest x1 110 us: on_device(): output_weight = lax.all_gather(w_output, 'dp', axis=0, tiled=True)]
    reduce_scatter x6 -> x7, waiting for transfers between devices: 1250 us -> 725 us  [the longest x1 350 us: on_device(): lax.psum_scatter(back_part.astype(BF), both, scatter_dimension=0, tiled=T...]
    reshape x5 -> x6, local copies, waits for them, and re-layouts: 46.4 us -> 171 us  [the longest x1 62.9 us: on_device(): out_part.reshape(n_all * rows, features) + dot(shared_units, shared_out)]
    all_gather x4 -> x6, blocking collectives: 45.7 us -> 146 us  [the longest x1 57.4 us: on_device(): gates_all = lax.all_gather(gate_table.T, both, axis=0)]
    reduce_sum x10 -> x11, other arithmetic: 74.9 us -> 13.5 us  [the longest x1 3.85 us: on_device(): jnp.sum(jnp.where(picked, slot_gate_grad[..., None], 0.0), axis=1)]
    all_to_all x7 -> x5, starting transfers between devices: 79.9 us -> 21.2 us  [the longest x1 7.95 us: on_device(): lax.all_to_all(attended_back, 'seq', split_axis=1, concat_axis=0, tiled=T...]
    unnamed x2 -> x0, blocking collectives: 53.8 us -> none
  transfers between devices with their start and end apart: 24 -> 25, of which waited for: 18 -> 11; matrix products, arithmetic and copies ran while one was open for 18% -> 27% of each run, Pallas kernels for 0% -> 0%
where the time goes in v1:
time: 2330 us
  waiting for transfers between devices  1100 us (47%)
  matrix products  560 us (24%)
  local copies, waits for them, and re-layouts  249 us (11%)
  blocking collectives  233 us (10%)
  other arithmetic  146 us (6%)
    reduce_scatter x1, waiting for transfers between devices, on_device(): lax.psum_scatter(back_part.astype(BF), both, scatter_dimension=0, tiled=T...  350 us
    reduce_scatter x1, waiting for transfers between devices, on_device(): lax.psum_scatter(out_part.astype(BF), both, scatter_dimension=0, tiled=True)  294 us
    dot_general x8, matrix products, dot_nt(): return jnp.einsum('ik,jk->ij', a, b, preferred_element_type=F32)  151 us
    dot_general x9, matrix products, dot(): return jnp.dot(a, b, preferred_element_type=F32)  136 us
    dot_general x8, matrix products, dot_tn(): return jnp.einsum('ki,kj->ij', a, b, preferred_element_type=F32)  118 us
    all_gather x1, waiting for transfers between devices, on_device(): output_weight = lax.all_gather(w_output, 'dp', axis=0, tiled=True)  110 us
    all_gather x1, waiting for transfers between devices, on_device(): rows_all = lax.all_gather(moe_rows, both, axis=0, tiled=True)  92.6 us
    reduce_scatter x1, waiting for transfers between devices, on_device(): lax.psum_scatter(partial_back, 'seq', scatter_dimension=0, tiled=True)  80.6 us
  transfers between devices with their start and end apart: 25, of which 11 were waited for; matrix products, arithmetic and copies ran while one was open for 27% of the time, Pallas kernels for 0%

profile of v1, /device:TPU:0, one launch (start us, length us, event | category | flops | bytes accessed | tf_op | source)
XLA Modules:
  0.0 2325.1 jit_solution(17709987286968380500)
XLA Ops:
  11.3 14.8 all-gather.7
  26.2 8.9 all-gather.2
  36.1 16.1 all_gather.73
  58.3 8.8 all-gather.44.cloned.1.call-done
  67.1 5.1 fusion.9
  72.2 8.6 fusion.11
  80.8 25.5 %all-gather.26.cloned.1.call-done = bf16[2048,384]{1,0:T(8,128)(2,1)} async-done(((bf16[512,384]{1,0:T(8,128)(2,1)}), bf16[2048,384]{1,0:T(8,128)(2,1)}) %all-gather.26.cloned.1.call-update) | async-done | bytes 1572880 | tf_op jit(solution)/shard_map/all_gather | solution.py:182
  106.4 6.4 fusion.190
  114.5 42.7 %all-gather.24.cloned.1.call-done = bf16[2048,576]{0,1:T(8,128)(2,1)} async-done(((bf16[512,576]{0,1:T(8,128)(2,1)}), bf16[2048,576]{0,1:T(8,128)(2,1)}) %all-gather.24.cloned.1.call-update) | async-done | bytes 2359312 | tf_op jit(solution)/shard_map/all_gather | solution.py:183
  157.3 8.2 fusion.189
  193.2 3.7 all-to-all-start
  197.5 109.7 %all-gather.28.cloned.1.call-done = bf16[2048,2048]{1,0:T(8,128)(2,1)} async-done(((bf16[512,2048]{1,0:T(8,128)(2,1)}), bf16[2048,2048]{1,0:T(8,128)(2,1)}) %all-gather.28.cloned.1.call-update) | async-done | bytes 8388624 | tf_op jit(solution)/shard_map/all_gather | solution.py:185
  308.2 7.1 multiply_reduce_fusion.5
  317.9 8.5 copy.206
  332.1 57.4 %all-gather.9 = f32[32,6,256]{2,1,0:T(8,128)S(1)} all-gather(f32[1,6,256]{2,1,0:T(8,128)S(1)} %bitcast.295), channel_id=6, replica_groups=mesh['dp'=4,'seq'=8] {'dp','seq'}, dimensions={0}, use_global_device_ids=true | all-gather | bytes 202752 | tf_op jit(solution)/shard_map/all_gather | solution.py:198
  389.5 38.1 %all-gather.8 = s32[32,6,256]{2,1,0:T(8,128)S(1)} all-gather(s32[1,6,256]{2,1,0:T(8,128)S(1)} %bitcast.290), channel_id=5, replica_groups=mesh['dp'=4,'seq'=8] {'dp','seq'}, dimensions={0}, use_global_device_ids=true | all-gather | bytes 202752 | tf_op jit(solution)/shard_map/all_gather | solution.py:197
  430.2 92.6 %all-gather.30.cloned.1.call-done = bf16[8192,2048]{0,1:T(8,128)(2,1)} async-done(((bf16[256,2048]{0,1:T(8,128)(2,1)}), bf16[8192,2048]{0,1:T(8,128)(2,1)}) %all-gather.30.cloned.1.call-update) | async-done | bytes 33554448 | tf_op jit(solution)/shard_map/all_gather | solution.py:232
  522.8 44.7 %copy.249 = bf16[8192,2048]{1,0:T(8,128)(2,1)} copy(bf16[8192,2048]{0,1:T(8,128)(2,1)} %all-gather.30.cloned.1.call-done) | data formatting | bytes 67108864 | tf_op jit(solution)/shard_map/reshape | solution.py:245
  567.5 26.7 %convolution_convert_fusion.2 = bf16[32,160,2048]{2,1,0:T(8,128)(2,1)} fusion(bf16[32,256,2048]{2,1,0:T(8,128)(2,1)} %bitcast.236, s32[32,256]{1,0:T(8,128)S(1)} %convolution_convert_fusion.9, pred[32,256]{1,0:T(8,128)(4,1)S(1)} %reduce_or.9), kind=kOutput, calls=%fused_computation.26 | convolution fusion | flops 5381816320 | bytes 54566912 | tf_op jit(solution)/shard_map/bst,btd->bsd/dot_general | solution.py:247
  594.1 37.6 %fusion.21 = f32[5120,1408]{0,1:T(8,128)} fusion(bf16[5120,2048]{1,0:T(8,128)(2,1)} %bitcast.246, bf16[1,2048,1408]{2,1,0:T(8,128)(2,1)} %param.49), kind=kOutput, calls=%fused_computation.48 | convolution fusion | flops 29527900160 | bytes 55574528 | tf_op jit(solution)/shard_map/dot_general | solution.py:53
  631.7 13.2 multiply_convert_fusion.3
  644.9 24.1 %convolution_convert_fusion = bf16[5120,2048]{1,0:T(8,128)(2,1)} fusion(bf16[5120,704]{0,1:T(8,128)(2,1)} %multiply_convert_fusion.3, bf16[1,704,2048]{2,1,0:T(8,128)(2,1)} %param.50), kind=kOutput, calls=%fused_computation.15 | convolution fusion | flops 14774435840 | bytes 31064064 | tf_op jit(solution)/shard_map/dot_general | solution.py:53
  669.0 49.7 %all-gather.46.cloned.1.call-done = bf16[1,8192,2048]{2,1,0:T(8,128)(2,1)} async-done(((bf16[1,256,2048]{2,1,0:T(8,128)(2,1)}), bf16[1,8192,2048]{2,1,0:T(8,128)(2,1)}) %all-gather.46.cloned.1.call-update) | async-done | bytes 33554448 | tf_op jit(solution)/shard_map/all_gather | solution.py:196
  718.7 32.0 %fusion.1 = (f32[32,160]{1,0:T(8,128)S(1)}, f32[32,160,2048]{2,1,0:T(8,128)}) fusion(bf16[32,160,2048]{2,1,0:T(8,128)(2,1)} %bitcast.241, bf16[32,256,2048]{2,1,0:T(8,128)(2,1)} %bitcast.235, s32[32,256]{1,0:T(8,128)S(1)} %convolution_convert_fusion.9, pred[32,256]{1,0:T(8,128)(4,1)S(1)} %reduce_or.9), kind=kOutput, calls=%fused_computation.5 | convolution fusion | flops 5402782720 | bytes 96530432 | tf_op jit(solution)/shard_map/bst,btd->bsd/dot_general | solution.py:249
  750.7 3.9 select_reduce_fusion
  754.6 23.4 %multiply_convert_fusion = bf16[32,160,2048]{2,1,0:T(8,128)(2,1)} fusion(f32[32,160,2048]{2,1,0:T(8,128)} %get-tuple-element.265, f32[32,160]{1,0:T(8,128)S(1)} %get-tuple-element.217), kind=kLoop, calls=%fused_computation.6 | loop fusion | flops 20971520 | bytes 62935040 | tf_op jit(solution)/shard_map/convert_element_type | solution.py:250
  778.0 41.6 %multiply_convert_fusion.2 = (bf16[5120,704]{0,1:T(8,128)(2,1)}, bf16[5120,704]{0,1:T(8,128)(2,1)}) fusion(f32[5120,1408]{0,1:T(8,128)} %fusion.21, bf16[5120,2048]{1,0:T(8,128)(2,1)} %bitcast.249, bf16[1,704,2048]{2,1,0:T(8,128)(2,1)S(1)} %copy-done.122), kind=kOutput, calls=%fused_computation.22 | convolution fusion | flops 14810808320 | bytes 67108864 | tf_op jit(solution)/shard_map/ik,jk->ij/dot_general | solution.py:57
  819.6 37.7 %convolution_convert_fusion.1 = bf16[5120,2048]{1,0:T(8,128)(2,1)} fusion(bf16[5120,704]{0,1:T(8,128)(2,1)} %get-tuple-element.221, bf16[5120,704]{0,1:T(8,128)(2,1)} %get-tuple-element.220, bf16[1,2048,1408]{2,1,0:T(8,128)(2,1)S(1)} %bitcast.300), kind=kOutput, calls=%fused_computation.16 | convolution fusion | flops 29567221760 | bytes 41156608 | tf_op jit(solution)/shard_map/ik,jk->ij/dot_general | solution.py:57
  857.3 31.2 %fusion.25 = f32[32,256,2048]{2,1,0:T(8,128)} fusion(bf16[32,160,2048]{2,1,0:T(8,128)(2,1)} %bitcast.248, s32[32,256]{1,0:T(8,128)S(1)} %convolution_convert_fusion.9, pred[32,256]{1,0:T(8,128)(4,1)S(1)} %reduce_or.9), kind=kOutput, calls=%fused_computation.55 | convolution fusion | flops 5371330560 | bytes 88121344 | tf_op jit(solution)/shard_map/bst,bsd->btd/dot_general | solution.py:273
  888.4 61.3 %copy.251 = f32[8192,2048]{0,1:T(8,128)} copy(f32[8192,2048]{1,0:T(8,128)} %bitcast.31) | data formatting | bytes 134217728 | tf_op jit(solution)/shard_map/reshape | solution.py:274
  949.7 16.3 fusion.193
  966.0 18.6 multiply_convert_fusion.9
  984.6 33.8 %add_convert_fusion = bf16[8192,2048]{0,1:T(8,128)(2,1)} fusion(f32[8192,2048]{0,1:T(8,128)} %copy.251, bf16[2048,176]{0,1:T(8,128)(2,1)S(1)} %bitcast.252, bf16[8192,88]{0,1:T(8,128)(2,1)} %get-tuple-element.223, bf16[8192,88]{0,1:T(8,128)(2,1)S(1)} %get-tuple-element.222), kind=kOutput, calls=%fused_computation | convolution fusion | flops 5944901632 | bytes 104267776 | tf_op jit(solution)/shard_map/ik,jk->ij/dot_general | solution.py:57
  1020.6 350.4 %reduce-scatter.10.cloned.1.call-done = bf16[256,2048]{0,1:T(8,128)(2,1)} async-done(((bf16[8192,2048]{0,1:T(8,128)(2,1)}), bf16[256,2048]{0,1:T(8,128)(2,1)}) %reduce-scatter.10.cloned.1.call-update) | async-done | bytes 1048592 | tf_op jit(solution)/shard_map/reduce_scatter | solution.py:275
  1375.1 6.2 convolution_convert_fusion.6
  1382.4 7.9 all-to-all-start.2
  1390.6 24.5 %all-to-all-done.2 = bf16[256,8,256]{2,0,1:T(8,128)(2,1)S(1)} async-done(((bf16[256,8,256]{2,0,1:T(8,128)(2,1)}), bf16[256,8,256]{2,0,1:T(8,128)(2,1)S(1)}, u32[]{:S(2)}, u32[]{:S(2)}) %all-to-all-start.2) | async-done | bytes 1048608 | tf_op jit(solution)/shard_map/all_to_all | solution.py:303
  1454.7 3.6 all-to-all-start.4
  1458.5 15.1 all-to-all-done.4
  1474.6 7.5 fusion.192
  1492.6 6.2 fusion.191
  1503.5 4.7 convolution_convert_fusion.3
  1508.2 17.6 pad_maximum_fusion.1
  1527.2 14.8 fusion.78
  1542.3 18.4 convolution_convert_fusion.7
  1563.0 39.4 %all_to_all.73 = bf16[4,512,2,88]{1,3,2,0:T(8,128)(2,1)} all-to-all(bf16[4,512,2,88]{1,3,2,0:T(8,128)(2,1)S(1)} %copy.231), channel_id=1, replica_groups=mesh['dp'=4,'seq'=8] {'dp'}, dimensions={0} | all-to-all | bytes 1441792 | tf_op jit(solution)/shard_map/all_to_all | solution.py:371
  1608.2 80.6 %reduce-scatter.12.cloned.1.call-done = bf16[256,2624]{0,1:T(8,128)(2,1)} async-done(((bf16[2048,2624]{0,1:T(8,128)(2,1)}), bf16[256,2624]{0,1:T(8,128)(2,1)}) %reduce-scatter.12.cloned.1.call-update) | async-done | bytes 1343504 | tf_op jit(solution)/shard_map/reduce_scatter | solution.py:333
  1695.5 30.3 %fusion.6 = f32[32,256,2048]{2,1,0:T(8,128)} fusion(bf16[32,160,2048]{2,1,0:T(8,128)(2,1)} %bitcast.242, f32[32,160]{1,0:T(8,128)S(1)} %copy-done.70, s32[32,256]{1,0:T(8,128)S(1)} %copy-done.44, pred[32,256]{1,0:T(8,128)(4,1)S(1)} %copy-done.67), kind=kOutput, calls=%fused_computation.13 | convolution fusion | flops 5402787840 | bytes 88141824 | tf_op jit(solution)/shard_map/bst,bsd->btd/dot_general | solution.py:280
  1725.8 62.9 %copy.250 = f32[8192,2048]{0,1:T(8,128)} copy(f32[8192,2048]{1,0:T(8,128)} %bitcast.22) | data formatting | bytes 134217728 | tf_op jit(solution)/shard_map/reshape | solution.py:281
  1788.7 34.9 %add_convert_fusion.1 = bf16[8192,2048]{0,1:T(8,128)(2,1)} fusion(f32[8192,2048]{0,1:T(8,128)} %copy.250, bf16[8192,88]{0,1:T(8,128)(2,1)S(1)} %copy-done.25, bf16[704,2048]{1,0:T(8,128)(2,1)} %param.48, s32[]{:T(128)S(6)} %select_n.82), kind=kOutput, calls=%fused_computation.1 | convolution fusion | flops 2986344448 | bytes 102465536 | tf_op jit(solution)/shard_map/dot_general | solution.py:53
  1828.7 41.5 %fusion.17 = f32[1,2048,1408]{2,1,0:T(8,128)} fusion(bf16[5120,2048]{1,0:T(8,128)(2,1)} %bitcast.247, bf16[5120,704]{0,1:T(8,128)(2,1)} %get-tuple-element.221, bf16[5120,704]{0,1:T(8,128)(2,1)} %get-tuple-element.220), kind=kOutput, calls=%fused_computation.31 | convolution fusion | flops 29556736000 | bytes 46923776 | tf_op jit(solution)/shard_map/ki,kj->ij/dot_general | solution.py:61
  1870.1 21.5 convolution_bitcast_fusion
  1892.5 5.1 convert_element_type.270
  1897.6 9.4 convert_bitcast_fusion
  1907.0 10.7 copy.232
  1917.7 12.0 copy.236
  1932.4 4.2 convert_element_type.264
  1936.6 5.4 convert_element_type.258
  1942.1 5.9 fusion.156
  1948.1 5.4 fusion.95
  1953.5 294.3 %reduce-scatter.8.cloned.1.call-done = bf16[256,2048]{0,1:T(8,128)(2,1)} async-done(((bf16[8192,2048]{0,1:T(8,128)(2,1)}), bf16[256,2048]{0,1:T(8,128)(2,1)}) %reduce-scatter.8.cloned.1.call-update) | async-done | bytes 1048592 | tf_op jit(solution)/shard_map/reduce_scatter | solution.py:282
  2247.8 4.1 fusion.129
  2256.6 47.3 %psum.7 = f32[4608]{0:T(1024)S(1)} all-reduce(f32[4608]{0:T(1024)S(1)} %pad_maximum_fusion.23), channel_id=1, replica_groups=mesh['dp'=4,'seq'=8] {'dp','seq'}, use_global_device_ids=true, to_apply=%region_33.34 | all-reduce | flops 4608 | bytes 36864 | tf_op jit(solution)/shard_map/psum | solution.py:357
  2306.0 10.8 all_gather.85
  (468 shorter events, 148.3 us)
Async XLA Ops:
  7.2 19.0 copy-start.118
  7.2 59.9 %all-gather.44.cloned.1.call-start = ((), (), s32[]{:S(2)}) async-start(), calls=%async_computation.30 | async-start | bytes 9437184 | tf_op jit(solution)/shard_map/all_gather | solution.py:170
  8.0 98.4 %all-gather.26.cloned.1.call-start = ((), (), s32[]{:S(2)}) async-start(), calls=%async_computation.14 | async-start | bytes 1966080 | tf_op jit(solution)/shard_map/all_gather | solution.py:182
  9.9 147.4 %all-gather.24.cloned.1.call-start = ((), (), s32[]{:S(2)}) async-start(), calls=%async_computation.13 | async-start | bytes 2949120 | tf_op jit(solution)/shard_map/all_gather | solution.py:183
  10.6 296.6 %all-gather.28.cloned.1.call-start = ((), (), s32[]{:S(2)}) async-start(), calls=%async_computation.15 | async-start | bytes 10485760 | tf_op jit(solution)/shard_map/all_gather | solution.py:185
  26.1 142.5 %copy-start.93 = (f32[512]{0:T(512)}, f32[512]{0:T(512)S(1)}, u32[]{:S(2)}) copy-start(f32[512]{0:T(512)S(1)} %slice_bitcast_fusion.2) | copy-start | bytes 6148
  35.2 37.0 %copy-start.79 = (f32[1,4,4,128]{3,1,2,0:T(4,128)}, f32[1,4,4,128]{3,1,2,0:T(4,128)S(1)}, u32[]{:S(2)}) copy-start(f32[1,4,4,128]{3,1,2,0:T(4,128)S(1)} %copy.257) | copy-start | bytes 24580
  52.2 116.4 %copy-start.71 = (bf16[512,512]{1,0:T(8,128)(2,1)}, bf16[512,512]{1,0:T(8,128)(2,1)S(1)}, u32[]{:S(2)}) copy-start(bf16[512,512]{1,0:T(8,128)(2,1)S(1)} %all_gather.73) | copy-start | bytes 1572868
  58.3 113.3 %copy-start.45 = (f32[2048,32]{0,1:T(8,128)}, f32[2048,32]{0,1:T(8,128)S(1)}, u32[]{:S(2)}) copy-start(f32[2048,32]{0,1:T(8,128)S(1)} %get-tuple-element.247) | copy-start | bytes 786436
  58.3 113.3 %copy-start.59 = (f32[2048,32]{0,1:T(8,128)}, f32[2048,32]{0,1:T(8,128)S(1)}, u32[]{:S(2)}) copy-start(f32[2048,32]{0,1:T(8,128)S(1)} %get-tuple-element.246) | copy-start | bytes 786436
  170.1 18.9 copy-start.29
  193.2 114.0 %all-to-all-start = ((bf16[8,256,256]{1,2,0:T(8,128)(2,1)}), bf16[8,256,256]{1,2,0:T(8,128)(2,1)S(1)}, u32[]{:S(2)}, u32[]{:S(2)}) async-start(bf16[8,256,256]{1,2,0:T(8,128)(2,1)} %copy.202), calls=%async_computation | async-start | bytes 2097152 | tf_op jit(solution)/shard_map/all_to_all | solution.py:224
  196.9 325.9 %all-gather.30.cloned.1.call-start = ((), (), s32[]{:S(2)}) async-start(), calls=%async_computation.16 | async-start | bytes 34603008 | tf_op jit(solution)/shard_map/all_gather | solution.py:232
  197.5 117.8 %copy-start.20 = (bf16[1,256,2048]{1,2,0:T(8,128)(2,1)}, bf16[1,256,2048]{1,2,0:T(8,128)(2,1)S(1)}, u32[]{:S(2)}) copy-start(bf16[1,256,2048]{1,2,0:T(8,128)(2,1)S(1)} %copy.200) | copy-start | bytes 3145732
  197.5 119.7 %copy-start.74 = (f32[1,4,4,128]{3,1,2,0:T(4,128)}, f32[1,4,4,128]{3,1,2,0:T(4,128)S(1)}, u32[]{:S(2)}) copy-start(f32[1,4,4,128]{3,1,2,0:T(4,128)S(1)} %copy.259) | copy-start | bytes 24580
  317.3 401.4 %all-gather.46.cloned.1.call-start = ((), (), s32[]{:S(2)}) async-start(), calls=%async_computation.31 | async-start | bytes 34603008 | tf_op jit(solution)/shard_map/all_gather | solution.py:196
  328.5 100.1 %all-to-all-start.1 = ((bf16[4,512,2,88]{1,3,2,0:T(8,128)(2,1)}), bf16[4,512,2,88]{1,3,2,0:T(8,128)(2,1)S(1)}, u32[]{:S(2)}, u32[]{:S(2)}) async-start(bf16[4,512,2,88]{1,3,2,0:T(8,128)(2,1)} %copy.207), calls=%async_computation.1 | async-start | bytes 1441792 | tf_op jit(solution)/shard_map/all_to_all | solution.py:190
  332.0 1039.1 %reduce-scatter.10.cloned.1.call-start = ((), (), s32[]{:S(2)}) async-start(), calls=%async_computation.18 | async-start | bytes 34603008 | tf_op jit(solution)/shard_map/reduce_scatter | solution.py:275
  332.1 96.3 %copy-start.81 = (s32[1,256,6]{1,2,0:T(8,128)}, s32[1,256,6]{1,2,0:T(8,128)S(1)}, u32[]{:S(2)}) copy-start(s32[1,256,6]{1,2,0:T(8,128)S(1)} %copy.268) | copy-start | bytes 18436
  428.4 428.8 %copy-start.66 = (pred[32,256]{1,0:T(8,128)(4,1)}, pred[32,256]{1,0:T(8,128)(4,1)S(1)}, u32[]{:S(2)}) copy-start(pred[32,256]{1,0:T(8,128)(4,1)S(1)} %reduce_or.9) | copy-start | bytes 24580
  428.6 428.7 %copy-start.43 = (s32[32,256]{1,0:T(8,128)}, s32[32,256]{1,0:T(8,128)S(1)}, u32[]{:S(2)}) copy-start(s32[32,256]{1,0:T(8,128)S(1)} %convolution_convert_fusion.9) | copy-start | bytes 98308
  718.7 32.0 %copy-start.77 = (f32[32,256]{1,0:T(8,128)S(1)}, f32[32,256]{1,0:T(8,128)}, u32[]{:S(2)}) copy-start(f32[32,256]{1,0:T(8,128)} %get-tuple-element.218) | copy-start | bytes 98308
  754.6 23.4 %copy-start.69 = (f32[32,160]{1,0:T(8,128)}, f32[32,160]{1,0:T(8,128)S(1)}, u32[]{:S(2)}) copy-start(f32[32,160]{1,0:T(8,128)S(1)} %get-tuple-element.217) | copy-start | bytes 61444
  754.6 23.4 %copy-start.122 = (bf16[1,704,2048]{2,1,0:T(8,128)(2,1)S(1)}, bf16[1,704,2048]{2,1,0:T(8,128)(2,1)}, u32[]{:S(2)}) copy-start(bf16[1,704,2048]{2,1,0:T(8,128)(2,1)} %param.50) | copy-start | bytes 8650756
  754.6 65.0 %slice-start.9 = ((s8[5767168]{0:T(1024)(128)(4,1)}), s8[4194304]{0:T(1024)(128)(4,1)S(1)}, s32[]{:S(2)}) async-start(s8[5767168]{0:T(1024)(128)(4,1)} %bitcast.299), calls=%async_computation.42 | async-start | bytes 8388608
  778.0 41.6 %slice-start.10 = ((s8[5767168]{0:T(1024)(128)(4,1)}), s8[1572864]{0:T(1024)(128)(4,1)S(1)}, s32[]{:S(2)}) async-start(s8[5767168]{0:T(1024)(128)(4,1)} %bitcast.299), calls=%async_computation.43 | async-start | bytes 3145728
  888.4 61.3 %copy-start.28 = (bf16[22,8,4,512]{3,1,2,0:T(8,128)(2,1)S(1)}, bf16[22,8,4,512]{3,1,2,0:T(8,128)(2,1)}, u32[]{:S(2)}) copy-start(bf16[22,8,4,512]{3,1,2,0:T(8,128)(2,1)} %copy.260) | copy-start | bytes 2162692
  984.6 33.8 %copy-start.56 = (bf16[8192,88]{0,1:T(8,128)(2,1)}, bf16[8192,88]{0,1:T(8,128)(2,1)S(1)}, u32[]{:S(2)}) copy-start(bf16[8192,88]{0,1:T(8,128)(2,1)S(1)} %get-tuple-element.222) | copy-start | bytes 4325380
  1018.4 352.7 %copy-start.9 = (f32[256,2048]{0,1:T(8,128)S(1)}, f32[256,2048]{0,1:T(8,128)}, u32[]{:S(2)}) copy-start(f32[256,2048]{0,1:T(8,128)} %copy-done.8) | copy-start | bytes 6291460
  1018.4 352.7 %copy-start.75 = (f32[1,4,4,128]{3,1,2,0:T(4,128)S(1)}, f32[1,4,4,128]{3,1,2,0:T(4,128)}, u32[]{:S(2)}) copy-start(f32[1,4,4,128]{3,1,2,0:T(4,128)} %copy-done.74) | copy-start | bytes 24580
  1018.4 352.7 %copy-start.91 = (f32[256]{0:T(256)S(1)}, f32[256]{0:T(256)}, u32[]{:S(2)}) copy-start(f32[256]{0:T(256)} %copy-done.90) | copy-start | bytes 3076
  1018.4 356.1 %copy-start.111 = (f32[256]{0:T(256)S(1)}, f32[256]{0:T(256)}, u32[]{:S(2)}) copy-start(f32[256]{0:T(256)} %get-tuple-element.252) | copy-start | bytes 3076
  1018.4 440.1 %all-gather.38.cloned.1.call-start = ((), (), s32[]{:S(2)}) async-start(), calls=%async_computation.26 | async-start | bytes 9437184 | tf_op jit(solution)/shard_map/all_gather | solution.py:233
  1020.6 354.5 %copy-start.22 = (bf16[1,256,2048]{1,2,0:T(8,128)(2,1)}, bf16[1,256,2048]{1,2,0:T(8,128)(2,1)S(1)}, u32[]{:S(2)}) copy-start(bf16[1,256,2048]{1,2,0:T(8,128)(2,1)S(1)} %copy.210) | copy-start | bytes 3145732
  1382.4 32.6 %all-to-all-start.2 = ((bf16[256,8,256]{2,0,1:T(8,128)(2,1)}), bf16[256,8,256]{2,0,1:T(8,128)(2,1)S(1)}, u32[]{:S(2)}, u32[]{:S(2)}) async-start(bf16[256,8,256]{2,0,1:T(8,128)(2,1)} %bitcast.231), calls=%async_computation.4 | async-start | bytes 2097152 | tf_op jit(solution)/shard_map/all_to_all | solution.py:303
  1390.4 212.1 %reduce-scatter.18.cloned.1.call-start = ((), (), s32[]{:S(2)}) async-start(), calls=%async_computation.24 | async-start | bytes 1310720 | tf_op jit(solution)/shard_map/reduce_scatter | solution.py:366
  1418.1 11.9 copy-start.49
  1454.7 18.9 all-to-all-start.4
  1458.3 145.9 %reduce-scatter.20.cloned.1.call-start = ((), (), s32[]{:S(2)}) async-start(), calls=%async_computation.27 | async-start | bytes 2621440 | tf_op jit(solution)/shard_map/reduce_scatter | solution.py:366
  1482.1 124.0 %reduce-scatter.14.cloned.1.call-start = ((), (), s32[]{:S(2)}) async-start(), calls=%async_computation.20 | async-start | bytes 3932160 | tf_op jit(solution)/shard_map/reduce_scatter | solution.py:366
  1498.9 189.8 %reduce-scatter.12.cloned.1.call-start = ((), (), s32[]{:S(2)}) async-start(), calls=%async_computation.19 | async-start | bytes 12091392 | tf_op jit(solution)/shard_map/reduce_scatter | solution.py:333
  1525.8 366.6 %all-gather.42.cloned.1.call-start = ((), (), s32[]{:S(2)}) async-start(), calls=%async_computation.29 | async-start | bytes 3244032 | tf_op jit(solution)/shard_map/all_gather | solution.py:380
  1527.2 15.1 copy-start.57
  1542.0 355.6 %all-gather.48.cloned.1.call-start = ((), (), s32[]{:S(2)}) async-start(), calls=%async_computation.32 | async-start | bytes 6488064 | tf_op jit(solution)/shard_map/all_gather | solution.py:378
  1602.4 327.3 %all-gather.36.cloned.1.call-start = ((), (), s32[]{:S(2)}) async-start(), calls=%async_computation.25 | async-start | bytes 1179648 | tf_op jit(solution)/shard_map/all_gather | solution.py:369
  1604.1 328.3 %all-gather.40.cloned.1.call-start = ((), (), s32[]{:S(2)}) async-start(), calls=%async_computation.28 | async-start | bytes 2359296 | tf_op jit(solution)/shard_map/all_gather | solution.py:369
  1606.0 330.6 %all-gather.32.cloned.1.call-start = ((), (), s32[]{:S(2)}) async-start(), calls=%async_computation.21 | async-start | bytes 3538944 | tf_op jit(solution)/shard_map/all_gather | solution.py:369
  1608.0 334.0 %all-gather.34.cloned.1.call-start = ((), (), s32[]{:S(2)}) async-start(), calls=%async_computation.22 | async-start | bytes 2654208 | tf_op jit(solution)/shard_map/all_gather | solution.py:345
  1608.2 87.3 %copy-start.44 = (s32[32,256]{1,0:T(8,128)S(1)}, s32[32,256]{1,0:T(8,128)}, u32[]{:S(2)}) copy-start(s32[32,256]{1,0:T(8,128)} %copy-done.43) | copy-start | bytes 98308
  1608.2 87.3 %copy-start.67 = (pred[32,256]{1,0:T(8,128)(4,1)S(1)}, pred[32,256]{1,0:T(8,128)(4,1)}, u32[]{:S(2)}) copy-start(pred[32,256]{1,0:T(8,128)(4,1)} %copy-done.66) | copy-start | bytes 24580
  1608.2 87.3 %copy-start.70 = (f32[32,160]{1,0:T(8,128)S(1)}, f32[32,160]{1,0:T(8,128)}, u32[]{:S(2)}) copy-start(f32[32,160]{1,0:T(8,128)} %copy-done.69) | copy-start | bytes 61444
  1693.4 32.4 %copy-start.83 = (bf16[256,32]{0,1:T(8,128)(2,1)}, bf16[256,32]{0,1:T(8,128)(2,1)S(1)}, u32[]{:S(2)}) copy-start(bf16[256,32]{0,1:T(8,128)(2,1)S(1)} %get-tuple-element.231) | copy-start | bytes 49156
  1693.4 32.4 %copy-start.85 = (bf16[256,32]{0,1:T(8,128)(2,1)}, bf16[256,32]{0,1:T(8,128)(2,1)S(1)}, u32[]{:S(2)}) copy-start(bf16[256,32]{0,1:T(8,128)(2,1)S(1)} %get-tuple-element.232) | copy-start | bytes 49156
  1694.6 31.2 %copy-start.62 = (bf16[256,512]{0,1:T(8,128)(2,1)}, bf16[256,512]{0,1:T(8,128)(2,1)S(1)}, u32[]{:S(2)}) copy-start(bf16[256,512]{0,1:T(8,128)(2,1)S(1)} %subtract_convert_fusion) | copy-start | bytes 786436
  1695.4 552.4 %reduce-scatter.8.cloned.1.call-start = ((), (), s32[]{:S(2)}) async-start(), calls=%async_computation.17 | async-start | bytes 34603008 | tf_op jit(solution)/shard_map/reduce_scatter | solution.py:282
  1825.8 65.8 %all-to-all-start.3 = ((f32[32,1,256]{2,1,0:T(1,128)}), f32[32,1,256]{2,1,0:T(1,128)S(1)}, u32[]{:S(2)}, u32[]{:S(2)}) async-start(f32[32,1,256]{2,1,0:T(1,128)} %all_to_all.60), calls=%async_computation.6 | async-start | bytes 65536 | tf_op jit(solution)/shard_map/all_to_all | solution.py:284
  1828.4 476.7 %reduce-scatter.16.cloned.1.call-start = ((), (), s32[]{:S(2)}) async-start(), calls=%async_computation.23 | async-start | bytes 737280 | tf_op jit(solution)/shard_map/reduce_scatter | solution.py:366
  1870.1 21.7 copy-start.82
  1948.0 299.8 %copy-start.10 = (f32[256,2048]{0,1:T(8,128)S(1)}, f32[256,2048]{0,1:T(8,128)}, u32[]{:S(2)}) copy-start(f32[256,2048]{0,1:T(8,128)} %copy-done.8) | copy-start | bytes 6291460
  1948.0 299.8 %copy-start.76 = (f32[1,4,4,128]{3,1,2,0:T(4,128)S(1)}, f32[1,4,4,128]{3,1,2,0:T(4,128)}, u32[]{:S(2)}) copy-start(f32[1,4,4,128]{3,1,2,0:T(4,128)} %copy-done.74) | copy-start | bytes 24580
  1948.0 299.8 %copy-start.92 = (f32[256]{0:T(256)S(1)}, f32[256]{0:T(256)}, u32[]{:S(2)}) copy-start(f32[256]{0:T(256)} %copy-done.90) | copy-start | bytes 3076
  1948.1 299.8 %copy-start.112 = (f32[256]{0:T(256)S(1)}, f32[256]{0:T(256)}, u32[]{:S(2)}) copy-start(f32[256]{0:T(256)} %get-tuple-element.252) | copy-start | bytes 3076
  1948.1 299.7 %copy-start.114 = (f32[256]{0:T(256)S(1)}, f32[256]{0:T(256)}, u32[]{:S(2)}) copy-start(f32[256]{0:T(256)} %copy-done.113) | copy-start | bytes 3076
  2251.9 66.1 %copy-start.1 = (bf16[512,3072]{1,0:T(8,128)(2,1)S(1)}, bf16[512,3072]{1,0:T(8,128)(2,1)}, u32[]{:S(2)}) copy-start(bf16[512,3072]{1,0:T(8,128)(2,1)} %param.41) | copy-start | bytes 9437188
  (96 other events, 420.0 us)
Sparse Core Ops, SparseCore 0:
  10.0 57.0 all-gather.43
  69.2 37.0 all-gather.25
  107.9 49.2 all-gather.23
  158.7 148.4 all-gather.27
  317.4 205.3 all-gather.29
  525.5 193.1 all-gather.45
  1018.5 352.5 reduce-scatter.9
  1373.5 74.8 all-gather.37
  1453.5 26.4 reduce-scatter.17
  1482.8 42.5 reduce-scatter.19
  1528.3 71.0 reduce-scatter.13
  1603.3 85.3 reduce-scatter.11
  1691.4 31.1 all-gather.41
  1724.5 43.3 all-gather.47
  1770.3 23.5 all-gather.35
  1796.3 28.1 all-gather.39
  1827.0 32.8 all-gather.31
  1861.8 29.3 all-gather.33
  1893.5 354.2 reduce-scatter.7
  2250.0 29.7 reduce-scatter.15

commit v2 on v1

--- a/solution.py
+++ b/solution.py
@@ -1,8 +1,11 @@
+import functools
 import math
 
 import jax
 import jax.numpy as jnp
 from jax import lax
+from jax.experimental import pallas as pl
+from jax.experimental.pallas import tpu as pltpu
 from jax.sharding import PartitionSpec as P
 
 HEADS = 16
@@ -126,6 +129,910 @@
         key_sums.astype(BF),
         value_sums.astype(BF),
     )
+
+
+def copy_kernel(places_ref, in_ref, out_ref):
+    out_ref[...] = in_ref[...]
+
+
+def reorder(stack, places):
+    count = stack.shape[0]
+    if stack.size * stack.dtype.itemsize < 2**20 or stack.ndim != 3:
+        return jnp.stack(
+            [lax.dynamic_index_in_dim(stack, places[j], 0, keepdims=False) for j in range(count)]
+        )
+    block = (1, *stack.shape[1:])
+    return pl.pallas_call(
+        copy_kernel,
+        grid_spec=pltpu.PrefetchScalarGridSpec(
+            num_scalar_prefetch=1,
+            grid=(count,),
+            in_specs=[pl.BlockSpec(block, lambda j, order: (order[j], 0, 0))],
+            out_specs=pl.BlockSpec(block, lambda j, order: (j, 0, 0)),
+        ),
+        out_shape=jax.ShapeDtypeStruct(stack.shape, stack.dtype),
+        compiler_params=params(40),
+        cost_estimate=pl.CostEstimate(
+            flops=0, bytes_accessed=2 * stack.size * stack.dtype.itemsize, transcendentals=0
+        ),
+    )(places.astype(jnp.int32), stack)
+
+
+def small_take(table, index):
+    table = jnp.array(table, jnp.int32)
+    hit = index[:, None] == jnp.arange(table.shape[0])[None, :]
+    return jnp.sum(jnp.where(hit, table[None, :], 0), axis=1)
+
+
+def params(limit=60):
+    return pltpu.CompilerParams(
+        vmem_limit_bytes=limit * 2**20, dimension_semantics=("arbitrary",)
+    )
+
+
+MESH_ID = pl.DeviceIdType.MESH
+
+
+def neighbours():
+    dp = lax.axis_index("dp")
+    seq = lax.axis_index("seq")
+    core = {"dp": dp, "seq": seq + 1 - 2 * (seq % 2)}
+    across_x = {"dp": dp, "seq": seq + 2 - 4 * ((seq // 2) % 2)}
+    across_y = {"dp": dp, "seq": seq + 4 - 8 * (seq // 4)}
+    following = {"dp": (dp + 1) % 4, "seq": seq}
+    previous = {"dp": (dp + 3) % 4, "seq": seq}
+    return core, across_x, across_y, following, previous
+
+
+def greet(devices):
+    barrier = pltpu.get_barrier_semaphore()
+    for device in devices:
+        pl.semaphore_signal(barrier, inc=1, device_id=device, device_id_type=MESH_ID)
+    pl.semaphore_wait(barrier, len(devices))
+
+
+class Courier:
+    def __init__(self, send_sems, recv_sems):
+        self.send_sems, self.recv_sems = send_sems, recv_sems
+        self.sent, self.open = [], []
+
+    def send(self, source, target, device):
+        index = len(self.sent)
+        copy = pltpu.make_async_remote_copy(
+            src_ref=source,
+            dst_ref=target,
+            send_sem=self.send_sems.at[index],
+            recv_sem=self.recv_sems.at[index],
+            device_id=device,
+            device_id_type=MESH_ID,
+        )
+        copy.start()
+        self.sent.append(copy)
+        self.open.append(copy)
+        return copy
+
+    def take(self, copy):
+        copy.wait_recv()
+        self.open = [other for other in self.open if other is not copy]
+
+    def finish(self):
+        for copy in list(self.open):
+            self.take(copy)
+        for copy in self.sent:
+            copy.wait_send()
+
+
+def gather_all_kernel(in_ref, out_ref, send_sems, recv_sems, local_sem):
+    core, across_x, across_y, following, previous = neighbours()
+    greet((core, across_x, across_y, following, previous))
+    half = in_ref.shape[0] // 2
+    top, bottom = pl.ds(0, half), pl.ds(half, half)
+    own = pltpu.make_async_copy(in_ref, out_ref.at[0], local_sem)
+    own.start()
+    post = Courier(send_sems, recv_sems)
+    ring = late = None
+    for i in range(4):
+        base = 8 * i
+        block = in_ref if i == 0 else out_ref.at[base]
+        if ring is not None:
+            post.take(ring)
+        if i < 3:
+            ring = post.send(block, out_ref.at[base + 8], following)
+        by_x = post.send(block, out_ref.at[base + 1], across_x)
+        by_y = post.send(block, out_ref.at[base + 2], across_y)
+        post.send(block, out_ref.at[base + 4], core)
+        post.take(by_x)
+        far_top = post.send(out_ref.at[base + 1, top], out_ref.at[base + 3, top], across_y)
+        post.send(out_ref.at[base + 1], out_ref.at[base + 5], core)
+        post.take(by_y)
+        far_bottom = post.send(
+            out_ref.at[base + 2, bottom], out_ref.at[base + 3, bottom], across_x
+        )
+        post.send(out_ref.at[base + 2], out_ref.at[base + 6], core)
+        if late is not None:
+            post.take(late[0])
+            post.take(late[1])
+            post.send(out_ref.at[base - 5], out_ref.at[base - 1], core)
+        late = (far_top, far_bottom)
+    post.take(late[0])
+    post.take(late[1])
+    post.send(out_ref.at[27], out_ref.at[31], core)
+    own.wait()
+    post.finish()
+
+
+def gather_all(block, collective_id):
+    rows, columns = block.shape
+    return pl.pallas_call(
+        gather_all_kernel,
+        out_shape=jax.ShapeDtypeStruct((32, rows, columns), block.dtype),
+        in_specs=[pl.BlockSpec(memory_space=pl.ANY)],
+        out_specs=pl.BlockSpec(memory_space=pl.ANY),
+        scratch_shapes=[
+            pltpu.SemaphoreType.DMA((39,)),
+            pltpu.SemaphoreType.DMA((39,)),
+            pltpu.SemaphoreType.DMA,
+        ],
+        compiler_params=pltpu.CompilerParams(
+            collective_id=collective_id, has_side_effects=True, vmem_limit_bytes=16 * 2**20
+        ),
+        cost_estimate=pl.CostEstimate(
+            flops=0, bytes_accessed=64 * rows * columns * 2, transcendentals=0
+        ),
+    )(block)
+
+
+def accumulate(target, *sources):
+    rows = target.shape[0]
+    step = 16
+
+    def body(k, carry):
+        part = pl.ds(pl.multiple_of(k * step, step), step)
+        total = target[part].astype(F32)
+        for source in sources:
+            total = total + source[part].astype(F32)
+        target[part] = total.astype(target.dtype)
+        return carry
+
+    lax.fori_loop(0, rows // step, body, 0)
+
+
+def scatter_all_kernel(
+    in_ref, out_ref, held, far, near, ring, stage, send_sems, recv_sems, local_sems
+):
+    core, across_x, across_y, following, previous = neighbours()
+    greet((core, across_x, across_y, following, previous))
+    rows = out_ref.shape[0]
+    half = rows // 2
+    top, bottom = pl.ds(0, half), pl.ds(half, half)
+    post = Courier(send_sems, recv_sems)
+    order = (1, 2, 3, 0)
+    by_core, by_far, by_near, loads = {}, {}, {}, {}
+    by_ring = None
+
+    def load(n):
+        i = order[n]
+        loads[i] = pltpu.make_async_copy(
+            in_ref.at[pl.ds(8 * i, 4)], stage.at[n % 2], local_sems.at[n % 2]
+        )
+        loads[i].start()
+
+    load(0)
+    for i in order:
+        by_core[i] = post.send(in_ref.at[pl.ds(8 * i + 4, 4)], held.at[i], core)
+
+    def first(n):
+        i = order[n]
+        if n < 3:
+            load(n + 1)
+        loads[i].wait()
+        post.take(by_core[i])
+        accumulate(held.at[i, 3], stage.at[n % 2, 3])
+        by_far[i] = (
+            post.send(held.at[i, 3, top], far.at[i, 0], across_y),
+            post.send(held.at[i, 3, bottom], far.at[i, 1], across_x),
+        )
+        for k in (1, 2, 0):
+            accumulate(held.at[i, k], stage.at[n % 2, k])
+
+    def second(n):
+        i = order[n]
+        post.take(by_far[i][0])
+        accumulate(held.at[i, 1, top], far.at[i, 0])
+        to_x = post.send(held.at[i, 1], near.at[i, 0], across_x)
+        post.take(by_far[i][1])
+        accumulate(held.at[i, 2, bottom], far.at[i, 1])
+        to_y = post.send(held.at[i, 2], near.at[i, 1], across_y)
+        by_near[i] = (to_x, to_y)
+
+    def third(n, before):
+        i = order[n]
+        post.take(by_near[i][0])
+        post.take(by_near[i][1])
+        sources = [near.at[i, 0], near.at[i, 1]]
+        if before is not None:
+            post.take(before)
+            sources.append(ring.at[n - 1])
+        accumulate(held.at[i, 0], *sources)
+        if n < 3:
+            return post.send(held.at[i, 0], ring.at[n], following)
+        return None
+
+    first(0)
+    first(1)
+    second(0)
+    first(2)
+    second(1)
+    by_ring = third(0, by_ring)
+    first(3)
+    second(2)
+    by_ring = third(1, by_ring)
+    second(3)
+    by_ring = third(2, by_ring)
+    third(3, by_ring)
+    out_ref[...] = held[0, 0]
+    post.finish()
+
+
+def scatter_all(parts, collective_id):
+    _, rows, columns = parts.shape
+    dtype = parts.dtype
+    return pl.pallas_call(
+        scatter_all_kernel,
+        out_shape=jax.ShapeDtypeStruct((rows, columns), dtype),
+        in_specs=[pl.BlockSpec(memory_space=pl.ANY)],
+        out_specs=pl.BlockSpec(memory_space=pltpu.VMEM),
+        scratch_shapes=[
+            pltpu.VMEM((4, 4, rows, columns), dtype),
+            pltpu.VMEM((4, 2, rows // 2, columns), dtype),
+            pltpu.VMEM((4, 2, rows, columns), dtype),
+            pltpu.VMEM((3, rows, columns), dtype),
+            pltpu.VMEM((2, 4, rows, columns), dtype),
+            pltpu.SemaphoreType.DMA((23,)),
+            pltpu.SemaphoreType.DMA((23,)),
+            pltpu.SemaphoreType.DMA((2,)),
+        ],
+        compiler_params=pltpu.CompilerParams(
+            collective_id=collective_id, has_side_effects=True, vmem_limit_bytes=56 * 2**20
+        ),
+        cost_estimate=pl.CostEstimate(
+            flops=32 * rows * columns, bytes_accessed=64 * rows * columns * 2, transcendentals=0
+        ),
+    )(parts)
+
+
+def gather_start_kernel(
+    hidden, named, gains, query, expand, compress, hidden_all, named_all, gains_all, query_all,
+    expand_all, compress_all, send_sems, recv_sems, local_sems
+):
+    dp = lax.axis_index("dp")
+    seq = lax.axis_index("seq")
+    core, across_x, across_y, following, previous = neighbours()
+    greet((core, across_x, across_y, following, previous))
+    post = Courier(send_sems, recv_sems)
+    rows = hidden.shape[0]
+    top, bottom = pl.ds(0, rows // 2), pl.ds(rows // 2, rows // 2)
+    by_x = seq + 2 - 4 * ((seq // 2) % 2)
+    by_y = seq + 4 - 8 * (seq // 4)
+    by_both = by_x + 4 - 8 * (seq // 4)
+    x_copy = post.send(hidden, hidden_all.at[seq], across_x)
+    y_copy = post.send(hidden, hidden_all.at[seq], across_y)
+    core_half = compress.shape[0] // 2
+    mine = pl.ds(pl.multiple_of((seq % 2) * core_half, core_half), core_half)
+    locals_ = [
+        pltpu.make_async_copy(source, target, local_sems.at[n])
+        for n, (source, target) in enumerate(
+            (
+                (hidden, hidden_all.at[seq]),
+                (named, named_all.at[0, 0]),
+                (gains, gains_all.at[dp]),
+                (query, query_all.at[dp]),
+                (expand, expand_all.at[dp]),
+                (compress, compress_all.at[dp]),
+            )
+        )
+    ]
+    for copy in locals_:
+        copy.start()
+
+    def hop(i):
+        at = (dp + 5 - i) % 4
+        first = i == 1
+        return [
+            post.send(gains if first else gains_all.at[at], gains_all.at[at], following),
+            post.send(named if first else named_all.at[0, i - 1], named_all.at[0, i], following),
+            post.send(query if first else query_all.at[at], query_all.at[at], following),
+            post.send(expand if first else expand_all.at[at], expand_all.at[at], following),
+            post.send(
+                compress.at[mine] if first else compress_all.at[at, mine],
+                compress_all.at[at, mine],
+                following,
+            ),
+        ]
+
+    ring = hop(1)
+    post.send(hidden, hidden_all.at[seq], core)
+    post.take(x_copy)
+    far_top = post.send(hidden_all.at[by_x, top], hidden_all.at[by_x, top], across_y)
+    post.send(hidden_all.at[by_x], hidden_all.at[by_x], core)
+    post.take(y_copy)
+    far_bottom = post.send(hidden_all.at[by_y, bottom], hidden_all.at[by_y, bottom], across_x)
+    post.send(hidden_all.at[by_y], hidden_all.at[by_y], core)
+    for i in (2, 3, 4):
+        for copy in ring:
+            post.take(copy)
+        at = (dp + 5 - i) % 4
+        if i < 4:
+            ring = hop(i)
+        post.send(compress_all.at[at, mine], compress_all.at[at, mine], core)
+        if i == 3:
+            post.take(far_top)
+            post.take(far_bottom)
+            post.send(hidden_all.at[by_both], hidden_all.at[by_both], core)
+    locals_[1].wait()
+    post.take(post.send(named_all.at[0], named_all.at[1], across_x))
+    post.take(post.send(named_all.at[pl.ds(0, 2)], named_all.at[pl.ds(2, 2)], across_y))
+    post.send(named_all.at[pl.ds(0, 4)], named_all.at[pl.ds(4, 4)], core)
+    for n, copy in enumerate(locals_):
+        if n != 1:
+            copy.wait()
+    post.finish()
+
+
+def gather_start(hidden, named, gains, query, expand, compress, collective_id):
+    anywhere = pl.BlockSpec(memory_space=pl.ANY)
+    total = 8 + 5 * 3 + 3 + 3
+    return pl.pallas_call(
+        gather_start_kernel,
+        out_shape=[
+            jax.ShapeDtypeStruct((8, *hidden.shape), hidden.dtype),
+            jax.ShapeDtypeStruct((8, 4, *named.shape), named.dtype),
+        ]
+        + [jax.ShapeDtypeStruct((4, *x.shape), x.dtype) for x in (gains, query, expand, compress)],
+        in_specs=[anywhere] * 6,
+        out_specs=[anywhere] * 6,
+        scratch_shapes=[
+            pltpu.SemaphoreType.DMA((total,)),
+            pltpu.SemaphoreType.DMA((total,)),
+            pltpu.SemaphoreType.DMA((6,)),
+        ],
+        compiler_params=pltpu.CompilerParams(
+            collective_id=collective_id, has_side_effects=True, vmem_limit_bytes=16 * 2**20
+        ),
+        cost_estimate=pl.CostEstimate(flops=0, bytes_accessed=2**26, transcendentals=0),
+    )(hidden, named, gains, query, expand, compress)
+
+
+PADDED_HALF = 768
+TILE = 256
+
+
+def flip(value, change):
+    return value + change - 2 * value * change
+
+
+def experts_kernel(
+    remote, capacity, rows_in, place_ref, gate_ref, weight_in, weight_out, shared_in,
+    shared_out, rows_all, slot_rows, slot_up, hidden_ref, back_ref, units_ref, part_ref,
+    in_grad, out_grad, rows_buffer, cot_buffer, load_sems, *sems
+):
+    step = pl.program_id(0)
+    steps = pl.num_programs(0)
+    rows = place_ref.shape[2]
+    features = slot_rows.shape[1]
+    slot = step % 2
+    gathered = rows_all if remote else rows_in
+
+    def loads(at, into):
+        found = []
+        for b in range(2):
+            block = 2 * at + b
+            part = pl.ds(b * rows, rows)
+            for kind, buffer in enumerate((rows_buffer, cot_buffer)):
+                found.append(
+                    pltpu.make_async_copy(
+                        gathered.at[block, kind],
+                        buffer.at[into, part],
+                        load_sems.at[into, 2 * b + kind],
+                    )
+                )
+        return found
+
+    if remote:
+        send_sems, recv_sems, own_sem = sems
+        core, across_x, across_y, following, previous = neighbours()
+        half = rows // 2
+        top, bottom = pl.ds(0, half), pl.ds(half, half)
+
+        def copy(index, source, target, device):
+            return pltpu.make_async_remote_copy(
+                src_ref=source,
+                dst_ref=target,
+                send_sem=send_sems.at[index],
+                recv_sem=recv_sems.at[index],
+                device_id=device,
+                device_id_type=MESH_ID,
+            )
+
+        def block_of(i):
+            return rows_in if i == 0 else rows_all.at[8 * i]
+
+        def along(i):
+            return copy(9 * i, block_of(i), rows_all.at[8 * i + 8], following)
+
+        def by_x(i):
+            return copy(9 * i + 1, block_of(i), rows_all.at[8 * i + 1], across_x)
+
+        def by_y(i):
+            return copy(9 * i + 2, block_of(i), rows_all.at[8 * i + 2], across_y)
+
+        def far(i, which):
+            if which == 0:
+                return copy(
+                    9 * i + 3, rows_all.at[8 * i + 1, :, top], rows_all.at[8 * i + 3, :, top], across_y
+                )
+            return copy(
+                9 * i + 4, rows_all.at[8 * i + 2, :, bottom], rows_all.at[8 * i + 3, :, bottom], across_x
+            )
+
+        def to_core(i, k):
+            source = block_of(i) if k == 0 else rows_all.at[8 * i + k]
+            return copy(9 * i + 5 + k, source, rows_all.at[8 * i + 4 + k], core)
+
+        def begin(i):
+            if i < 3:
+                along(i).start()
+            by_x(i).start()
+            by_y(i).start()
+            to_core(i, 0).start()
+
+        def ready(i, m):
+            if m == 0:
+                by_x(i).wait_recv()
+                far(i, 0).start()
+                to_core(i, 1).start()
+                by_y(i).wait_recv()
+                far(i, 1).start()
+                to_core(i, 2).start()
+                if i < 3:
+                    along(i).wait_recv()
+                    begin(i + 1)
+            elif m == 1:
+                far(i, 0).wait_recv()
+                far(i, 1).wait_recv()
+                to_core(i, 3).start()
+            elif m == 2:
+                to_core(i, 0).wait_recv()
+                to_core(i, 1).wait_recv()
+            else:
+                to_core(i, 2).wait_recv()
+                to_core(i, 3).wait_recv()
+
+        @pl.when(step == 0)
+        def _():
+            greet((core, across_x, across_y, following, previous))
+            own = pltpu.make_async_copy(rows_in, rows_all.at[0], own_sem)
+            own.start()
+            begin(0)
+            own.wait()
+            ready(0, 0)
+            for load in loads(0, 0):
+                load.start()
+    else:
+
+        @pl.when(step == 0)
+        def _():
+            for load in loads(0, 0):
+                load.start()
+
+    @pl.when(step == 0)
+    def _():
+        in_grad[...] = jnp.zeros_like(in_grad)
+        out_grad[...] = jnp.zeros_like(out_grad)
+
+    for load in loads(step, slot):
+        load.wait()
+
+    picks = []
+    for b in range(2):
+        chosen = one_hot(place_ref, 2 * step + b, capacity)
+        pick = chosen.astype(F32)
+        picks.append(pick.T.astype(BF))
+        pick = pick.astype(BF)
+        gates = jnp.sum(jnp.where(chosen, gate_ref[2 * step + b], 0.0), axis=1, keepdims=True)
+        part = pl.ds(b * rows, rows)
+        slots = pl.ds(b * capacity, capacity)
+        slot_rows[slots] = dot(pick, rows_buffer[slot, part]).astype(BF)
+        slot_up[slots] = (dot(pick, cot_buffer[slot, part]) * gates).astype(BF)
+
+    def gated(gate, up, hidden_back):
+        sigmoid = 1.0 / (1.0 + jnp.exp(-gate))
+        active = gate * sigmoid
+        gate_back = hidden_back * up * sigmoid * (1.0 + gate * (1.0 - sigmoid))
+        return (active * up).astype(BF), gate_back.astype(BF), (hidden_back * active).astype(BF)
+
+    def hidden_tile(t, carry):
+        part = pl.ds(pl.multiple_of(t * TILE, TILE), TILE)
+        second = pl.ds(pl.multiple_of(PADDED_HALF + t * TILE, TILE), TILE)
+        gate = dot(slot_rows[...], weight_in[:, part])
+        up = dot(slot_rows[...], weight_in[:, second])
+        hidden_back = dot_nt(slot_up[...], weight_out[part])
+        hidden_ref[:, part], back_ref[:, part], back_ref[:, second] = gated(gate, up, hidden_back)
+        return carry
+
+    lax.fori_loop(0, PADDED_HALF // TILE, hidden_tile, 0)
+
+    width = shared_out.shape[0]
+    rows_pair, cot_pair = rows_buffer[slot], cot_buffer[slot]
+    gate_up = dot(rows_pair, shared_in[...])
+    hidden_back = dot_nt(cot_pair, shared_out[...])
+    units, gate_back, up_back = gated(gate_up[:, :width], gate_up[:, width:], hidden_back)
+    units_ref[...] = units
+    shared_back = jnp.concatenate([gate_back, up_back], axis=1)
+    in_grad[...] += dot_tn(shared_back, rows_pair)
+    out_grad[...] += dot_tn(units, cot_pair)
+
+    if remote:
+        for m in range(4):
+            for i in range(4):
+                if i == 0 and m == 0:
+                    continue
+
+                @pl.when(step + 1 == 4 * i + m)
+                def _():
+                    ready(i, m)
+
+    @pl.when(step + 1 < steps)
+    def _():
+        for load in loads(step + 1, 1 - slot):
+            load.start()
+
+    def back_tile(t, carry):
+        part = pl.ds(pl.multiple_of(t * 2 * TILE, 2 * TILE), 2 * TILE)
+        slot_back = dot_nt(back_ref[...], weight_in[part]).astype(BF)
+        shared_part = dot_nt(shared_back, shared_in[part])
+        for b in range(2):
+            tokens = slice(b * rows, (b + 1) * rows)
+            total = dot(picks[b], slot_back[b * capacity : (b + 1) * capacity])
+            part_ref[b, :, part] = (total + shared_part[tokens]).astype(BF)
+        return carry
+
+    lax.fori_loop(0, features // (2 * TILE), back_tile, 0)
+
+    if remote:
+
+        @pl.when(step + 1 == steps)
+        def _():
+            for i in range(4):
+                if i < 3:
+                    along(i).wait_send()
+                by_x(i).wait_send()
+                by_y(i).wait_send()
+                far(i, 0).wait_send()
+                far(i, 1).wait_send()
+                for k in range(4):
+                    to_core(i, k).wait_send()
+
+
+def one_hot(place_ref, block, capacity):
+    place = place_ref[block]
+    rows = place.shape[1]
+    return lax.broadcasted_iota(jnp.int32, (capacity, rows), 0) == place
+
+
+def experts(
+    remote, capacity, rows_in, places, gates, weight_in, weight_out, shared_in, shared_out
+):
+    blocks, _, rows = places.shape
+    features = weight_in.shape[0]
+    width = shared_out.shape[0]
+    steps = blocks // 2
+
+    def whole(array):
+        return pl.BlockSpec(
+            array.shape, lambda j: (0,) * array.ndim, pipeline_mode=pl.Buffered(1)
+        )
+
+    def tiled(height, columns):
+        return pl.BlockSpec((height, columns), lambda j: (j, 0))
+
+    anywhere = pl.BlockSpec(memory_space=pl.ANY)
+    slots = 2 * capacity
+    scratch = [
+        pltpu.VMEM((2, 2 * rows, features), BF),
+        pltpu.VMEM((2, 2 * rows, features), BF),
+        pltpu.SemaphoreType.DMA((2, 4)),
+    ]
+    if remote:
+        scratch += [
+            pltpu.SemaphoreType.DMA((36,)),
+            pltpu.SemaphoreType.DMA((36,)),
+            pltpu.SemaphoreType.DMA,
+        ]
+    found = pl.pallas_call(
+        functools.partial(experts_kernel, remote, capacity),
+        grid=(steps,),
+        in_specs=[anywhere]
+        + [whole(x) for x in (places, gates, weight_in, weight_out, shared_in, shared_out)],
+        out_specs=[
+            anywhere,
+            tiled(slots, features),
+            tiled(slots, features),
+            tiled(slots, PADDED_HALF),
+            tiled(slots, 2 * PADDED_HALF),
+            tiled(2 * rows, width),
+            pl.BlockSpec((2, rows, features), lambda j: (j, 0, 0)),
+            pl.BlockSpec((2 * width, features), lambda j: (0, 0)),
+            pl.BlockSpec((width, features), lambda j: (0, 0)),
+        ],
+        out_shape=[
+            jax.ShapeDtypeStruct((blocks if remote else 1, 2, rows, features), BF),
+            jax.ShapeDtypeStruct((steps * slots, features), BF),
+            jax.ShapeDtypeStruct((steps * slots, features), BF),
+            jax.ShapeDtypeStruct((steps * slots, PADDED_HALF), BF),
+            jax.ShapeDtypeStruct((steps * slots, 2 * PADDED_HALF), BF),
+            jax.ShapeDtypeStruct((blocks * rows, width), BF),
+            jax.ShapeDtypeStruct((blocks, rows, features), BF),
+            jax.ShapeDtypeStruct((2 * width, features), F32),
+            jax.ShapeDtypeStruct((width, features), F32),
+        ],
+        scratch_shapes=scratch,
+        compiler_params=pltpu.CompilerParams(
+            vmem_limit_bytes=60 * 2**20,
+            dimension_semantics=("arbitrary",),
+            **({"collective_id": 3, "has_side_effects": True} if remote else {}),
+        ),
+        cost_estimate=pl.CostEstimate(
+            flops=steps * slots * features * 2 * 3 * 2 * PADDED_HALF,
+            bytes_accessed=blocks * features * 8 * rows,
+            transcendentals=0,
+        ),
+    )(rows_in, places, gates, weight_in, weight_out, shared_in, shared_out)
+    return found[1:]
+
+
+def plane_scatter_kernel(
+    in_ref, out_ref, held, far, near, stage, send_sems, recv_sems, local_sems
+):
+    core, across_x, across_y, _, _ = neighbours()
+    greet((core, across_x, across_y))
+    seq = lax.axis_index("seq")
+    rows = out_ref.shape[0]
+    top, bottom = pl.ds(0, rows // 2), pl.ds(rows // 2, rows // 2)
+    post = Courier(send_sems, recv_sems)
+    x_seq = seq + 2 - 4 * ((seq // 2) % 2)
+    y_seq = seq + 4 - 8 * (seq // 4)
+    xy_seq = x_seq + 4 - 8 * (seq // 4)
+    core_step = 1 - 2 * (seq % 2)
+    loads, arriving = {}, {}
+    for k, place in ((3, xy_seq), (1, x_seq), (2, y_seq), (0, seq)):
+        arriving[k] = post.send(in_ref.at[place + core_step], held.at[k], core)
+        loads[k] = pltpu.make_async_copy(in_ref.at[place], stage.at[k], local_sems.at[k])
+        loads[k].start()
+
+    def join(k):
+        loads[k].wait()
+        post.take(arriving[k])
+        accumulate(held.at[k], stage.at[k])
+
+    join(3)
+    far_top = post.send(held.at[3, top], far.at[0], across_y)
+    far_bottom = post.send(held.at[3, bottom], far.at[1], across_x)
+    join(1)
+    x_bottom = post.send(held.at[1, bottom], near.at[0, bottom], across_x)
+    join(2)
+    y_top = post.send(held.at[2, top], near.at[1, top], across_y)
+    join(0)
+    post.take(far_top)
+    accumulate(held.at[1, top], far.at[0])
+    x_top = post.send(held.at[1, top], near.at[0, top], across_x)
+    post.take(far_bottom)
+    accumulate(held.at[2, bottom], far.at[1])
+    y_bottom = post.send(held.at[2, bottom], near.at[1, bottom], across_y)
+    for copy in (x_bottom, y_top, x_top, y_bottom):
+        post.take(copy)
+    accumulate(held.at[0], near.at[0], near.at[1])
+    out_ref[...] = held[0]
+    post.finish()
+
+
+def plane_scatter(parts, collective_id):
+    _, rows, columns = parts.shape
+    return pl.pallas_call(
+        plane_scatter_kernel,
+        out_shape=jax.ShapeDtypeStruct((rows, columns), parts.dtype),
+        in_specs=[pl.BlockSpec(memory_space=pl.ANY)],
+        out_specs=pl.BlockSpec(memory_space=pltpu.VMEM),
+        scratch_shapes=[
+            pltpu.VMEM((4, rows, columns), parts.dtype),
+            pltpu.VMEM((2, rows // 2, columns), parts.dtype),
+            pltpu.VMEM((2, rows, columns), parts.dtype),
+            pltpu.VMEM((4, rows, columns), parts.dtype),
+            pltpu.SemaphoreType.DMA((10,)),
+            pltpu.SemaphoreType.DMA((10,)),
+            pltpu.SemaphoreType.DMA((4,)),
+        ],
+        compiler_params=pltpu.CompilerParams(
+            collective_id=collective_id, has_side_effects=True, vmem_limit_bytes=32 * 2**20
+        ),
+        cost_estimate=pl.CostEstimate(
+            flops=8 * rows * columns, bytes_accessed=16 * rows * columns, transcendentals=0
+        ),
+    )(parts)
+
+
+def spread(post, source, found, n, core, across_x, across_y):
+    seq = lax.axis_index("seq")
+    rows = source.shape[0]
+    top, bottom = pl.ds(0, rows // 2), pl.ds(rows // 2, rows // 2)
+    x_seq = seq + 2 - 4 * ((seq // 2) % 2)
+    y_seq = seq + 4 - 8 * (seq // 4)
+    xy_seq = x_seq + 4 - 8 * (seq // 4)
+    x_copy = post.send(source, found.at[seq], across_x)
+    y_copy = post.send(source, found.at[seq], across_y)
+    post.send(source, found.at[seq], core)
+    yield
+    post.take(x_copy)
+    far_top = post.send(found.at[x_seq, top], found.at[x_seq, top], across_y)
+    post.send(found.at[x_seq], found.at[x_seq], core)
+    post.take(y_copy)
+    far_bottom = post.send(found.at[y_seq, bottom], found.at[y_seq, bottom], across_x)
+    post.send(found.at[y_seq], found.at[y_seq], core)
+    yield
+    post.take(far_top)
+    post.take(far_bottom)
+    post.send(found.at[xy_seq], found.at[xy_seq], core)
+
+
+def plane_gather_kernel(in_ref, out_ref, send_sems, recv_sems, local_sem):
+    core, across_x, across_y, _, _ = neighbours()
+    greet((core, across_x, across_y))
+    own = pltpu.make_async_copy(in_ref, out_ref.at[lax.axis_index("seq")], local_sem)
+    own.start()
+    post = Courier(send_sems, recv_sems)
+    for _ in spread(post, in_ref, out_ref, 0, core, across_x, across_y):
+        pass
+    own.wait()
+    post.finish()
+
+
+def plane_gather(block, collective_id):
+    anywhere = pl.BlockSpec(memory_space=pl.ANY)
+    return pl.pallas_call(
+        plane_gather_kernel,
+        out_shape=jax.ShapeDtypeStruct((8, *block.shape), block.dtype),
+        in_specs=[anywhere],
+        out_specs=anywhere,
+        scratch_shapes=[
+            pltpu.SemaphoreType.DMA((8,)),
+            pltpu.SemaphoreType.DMA((8,)),
+            pltpu.SemaphoreType.DMA,
+        ],
+        compiler_params=pltpu.CompilerParams(
+            collective_id=collective_id, has_side_effects=True, vmem_limit_bytes=16 * 2**20
+        ),
+        cost_estimate=pl.CostEstimate(
+            flops=0, bytes_accessed=32 * block.size, transcendentals=0
+        ),
+    )(block)
+
+
+def grads_kernel(in_ref, out_ref, total, ring, send_sems, recv_sems, local_sems):
+    dp = lax.axis_index("dp")
+    core, across_x, across_y, following, previous = neighbours()
+    greet((core, across_x, across_y, following, previous))
+    post = Courier(send_sems, recv_sems)
+    loads = []
+    for n, i in enumerate((1, 2, 3, 0)):
+        load = pltpu.make_async_copy(in_ref.at[(dp + 4 - i) % 4], total.at[n], local_sems.at[n])
+        load.start()
+        loads.append(load)
+    loads[0].wait()
+    before = post.send(total.at[0], ring.at[0], following)
+    for n in (1, 2, 3):
+        loads[n].wait()
+        post.take(before)
+        accumulate(total.at[n], ring.at[n - 1])
+        if n < 3:
+            before = post.send(total.at[n], ring.at[n], following)
+    own = pltpu.make_async_copy(total.at[3], out_ref.at[lax.axis_index("seq")], local_sems.at[0])
+    own.start()
+    for _ in spread(post, total.at[3], out_ref, 0, core, across_x, across_y):
+        pass
+    own.wait()
+    post.finish()
+
+
+def sum_grads(parts, collective_id):
+    _, rows, columns = parts.shape
+    anywhere = pl.BlockSpec(memory_space=pl.ANY)
+    return pl.pallas_call(
+        grads_kernel,
+        out_shape=jax.ShapeDtypeStruct((8, rows, columns), parts.dtype),
+        in_specs=[anywhere],
+        out_specs=anywhere,
+        scratch_shapes=[
+            pltpu.VMEM((4, rows, columns), parts.dtype),
+            pltpu.VMEM((3, rows, columns), parts.dtype),
+            pltpu.SemaphoreType.DMA((11,)),
+            pltpu.SemaphoreType.DMA((11,)),
+            pltpu.SemaphoreType.DMA((4,)),
+        ],
+        compiler_params=pltpu.CompilerParams(
+            collective_id=collective_id, has_side_effects=True, vmem_limit_bytes=32 * 2**20
+        ),
+        cost_estimate=pl.CostEstimate(
+            flops=0, bytes_accessed=32 * rows * columns, transcendentals=0
+        ),
+    )(parts)
+
+
+def out_kernel(
+    capacity, order_ref, place_ref, gate_ref, hidden_ref, up_ref, units_ref, weight_ref, shared_ref,
+    gate_grad_ref, part_ref
+):
+    rows = place_ref.shape[2]
+    features = part_ref.shape[2]
+    chosen = one_hot(place_ref, 0, capacity)
+    pick = chosen.astype(F32).T.astype(BF)
+    gates = jnp.sum(jnp.where(chosen, gate_ref[0], 0.0), axis=1, keepdims=True)
+
+    def tile(t, slot_grad):
+        part = pl.ds(pl.multiple_of(t * 2 * TILE, 2 * TILE), 2 * TILE)
+        result = dot(hidden_ref[...], weight_ref[:, part]).astype(BF).astype(F32)
+        slot_grad += jnp.sum(result * up_ref[:, part].astype(F32), axis=1, keepdims=True)
+        total = dot(pick, (result * gates).astype(BF)) + dot(units_ref[...], shared_ref[:, part])
+        part_ref[0, :, part] = total.astype(BF)
+        return slot_grad
+
+    slot_grad = lax.fori_loop(
+        0, features // (2 * TILE), tile, jnp.zeros((capacity, 1), F32)
+    )
+    slot_grad = slot_grad / jnp.where(gates > 0.0, gates, 1.0)
+    gate_grad_ref[0] = jnp.sum(jnp.where(chosen, slot_grad, 0.0), axis=0, keepdims=True)
+
+
+def out_side(capacity, order, places, gates, hidden, up, units, weight_out, shared_out):
+    blocks, _, rows = places.shape
+    features = up.shape[1]
+    one = pl.BlockSpec((1, 1, rows), lambda j, order: (j, 0, 0))
+
+    def tiled(height, columns):
+        return pl.BlockSpec((height, columns), lambda j, order: (j, 0))
+
+    def whole(array):
+        return pl.BlockSpec(array.shape, lambda j, order: (0, 0))
+
+    return pl.pallas_call(
+        functools.partial(out_kernel, capacity),
+        grid_spec=pltpu.PrefetchScalarGridSpec(
+            num_scalar_prefetch=1,
+            grid=(blocks,),
+            in_specs=[
+                one,
+                one,
+                tiled(capacity, PADDED_HALF),
+                tiled(capacity, features),
+                tiled(rows, units.shape[1]),
+                whole(weight_out),
+                whole(shared_out),
+            ],
+            out_specs=[
+                pl.BlockSpec((1, 1, rows), lambda j, order: (order[j], 0, 0)),
+                pl.BlockSpec((1, rows, features), lambda j, order: (order[j], 0, 0)),
+            ],
+        ),
+        out_shape=[
+            jax.ShapeDtypeStruct((blocks, 1, rows), F32),
+            jax.ShapeDtypeStruct((blocks, rows, features), BF),
+        ],
+        compiler_params=params(48),
+        cost_estimate=pl.CostEstimate(
+            flops=blocks * 2 * features * (capacity * PADDED_HALF + rows * 2 * capacity),
+            bytes_accessed=blocks * features * 2 * (rows + capacity),
+            transcendentals=0,
+        ),
+    )(order, places, gates, hidden, up, units, weight_out, shared_out)
 
 
 def on_device(
@@ -149,6 +1056,7 @@
     n_dp = lax.axis_size("dp")
     n_seq = lax.axis_size("seq")
     n_all = n_dp * n_seq
+    fast = (n_dp, n_seq) == (4, 8)
     both = ("dp", "seq")
     dp_index = lax.axis_index("dp")
     seq_index = lax.axis_index("seq")
@@ -159,7 +1067,10 @@
     shard = features // n_dp
     expert_count = n_all // 2
     capacity = max(2, rows * TOP * 5 // (expert_count * 3))
+    capacity = (capacity + 15) // 16 * 16
     units = SH_FF // n_all
+    padded_units = (units + 127) // 128 * 128
+    expand_width = heads * (NOPE + VDIM)
 
     hidden = hidden_in.reshape(rows, features)
     upstream_rows = cotangent.reshape(rows, features)
@@ -167,39 +1078,70 @@
     id_rows = expert_ids.reshape(rows, TOP)
     gate_table = gate_weights.reshape(rows, TOP)
 
-    hidden_all = lax.all_gather(hidden, "seq", axis=0, tiled=True)
-    gains = lax.all_gather(
-        jnp.concatenate([attention_gain, feedforward_gain, latent_gain]), "dp", axis=0
-    ).astype(F32)
+    gains_own = jnp.concatenate([attention_gain, feedforward_gain, latent_gain])
+    named_own = jnp.concatenate(
+        [id_rows.T.astype(F32), gate_table.T, positions.reshape(1, rows).astype(F32)]
+    )
+    query_part = lax.dynamic_slice_in_dim(w_query, seq_index * heads * QK, heads * QK, 1)
+    expand_part = lax.dynamic_slice_in_dim(w_expand, seq_index * expand_width, expand_width, 1)
+    if fast:
+        named_own = jnp.pad(named_own, ((0, 16 - named_own.shape[0]), (0, 0)))
+        gains_size = gains_own.shape[0]
+        gains_own = jnp.pad(gains_own, (0, 2048 - gains_size)).reshape(16, 128)
+        hidden_all, named_all, gains, query_weight, expand_weight, compress_weight = gather_start(
+            hidden, named_own, gains_own, query_part, expand_part, w_compress, 1
+        )
+        gains = gains.reshape(n_dp, 2048)[:, :gains_size]
+        plane_places = seq_index ^ jnp.array([0, 2, 4, 6, 1, 3, 5, 7], jnp.int32)
+        dp_places = (dp_index - jnp.arange(n_dp)) % n_dp
+        block_places = (dp_places[:, None] * n_seq + plane_places[None, :]).reshape(n_all)
+        slot_of_seq = small_take([0, 4, 1, 5, 2, 6, 3, 7], seq_index ^ jnp.arange(n_seq))
+        positions_all = reorder(named_all[:, 0, 2 * TOP], slot_of_seq)
+        named_all = named_all.swapaxes(0, 1).reshape(n_all, 16, rows)
+    else:
+        hidden_all = lax.all_gather(hidden, "seq", axis=0)
+        named_all = lax.all_gather(named_own, both, axis=0)
+        positions_all = lax.dynamic_slice_in_dim(named_all, dp_index * n_seq, n_seq, 0)[:, 2 * TOP]
+        gains = lax.all_gather(gains_own, "dp", axis=0)
+        query_weight = lax.all_gather(query_part, "dp", axis=0)
+        expand_weight = lax.all_gather(expand_part, "dp", axis=0)
+        compress_weight = lax.all_gather(w_compress, "dp", axis=0)
+        block_places = jnp.arange(n_all, dtype=jnp.int32)
+    hidden_all = hidden_all.reshape(length, features)
+    query_weight = query_weight.reshape(features, heads * QK)
+    expand_weight = expand_weight.reshape(LATENT, expand_width)
+    compress_weight = compress_weight.reshape(features, LATENT + ROPE)
+    gains = gains.astype(F32)
     first_gain = gains[:, :shard].reshape(features)
     second_gain = gains[:, shard : 2 * shard].reshape(features)
     latent_gain_row = gains[:, 2 * shard :].reshape(LATENT)
-    positions_all = lax.all_gather(positions.reshape(rows), "seq", axis=0, tiled=True)
-    query_part = lax.dynamic_slice_in_dim(w_query, seq_index * heads * QK, heads * QK, 1)
-    expand_part = lax.dynamic_slice_in_dim(
-        w_expand, seq_index * heads * (NOPE + VDIM), heads * (NOPE + VDIM), 1
-    )
-    query_weight = lax.all_gather(query_part, "dp", axis=0, tiled=True)
-    compress_weight = lax.all_gather(w_compress, "dp", axis=0, tiled=True)
-    expand_weight = lax.all_gather(expand_part, "dp", axis=0, tiled=True)
     output_weight = lax.all_gather(w_output, "dp", axis=0, tiled=True)
     shared_part = lax.dynamic_index_in_dim(
         w_shared_in.reshape(shard, 2, n_dp, n_seq, units), seq_index, 3, keepdims=False
     )
-    shared_in = (
-        lax.all_to_all(
-            shared_part.transpose(2, 0, 1, 3), "dp", split_axis=0, concat_axis=0, tiled=True
-        )
-        .reshape(features, 2 * units)
-    )
+    shared_in = lax.all_to_all(
+        shared_part.transpose(2, 0, 1, 3), "dp", split_axis=0, concat_axis=0, tiled=True
+    ).reshape(features, 2, units)
+    pad = padded_units - units
+    shared_in = jnp.pad(shared_in, ((0, 0), (0, 0), (0, pad))).reshape(features, 2 * padded_units)
     shared_out = lax.dynamic_slice_in_dim(w_shared_out, seq_index * units, units, 0)
-    upstream_all = lax.all_gather(upstream_rows, both, axis=0, tiled=True)
-    ids_all = lax.all_gather(id_rows.T, both, axis=0)
-    gates_all = lax.all_gather(gate_table.T, both, axis=0)
+    shared_out = jnp.pad(shared_out, ((0, pad), (0, 0)))
+    pad = PADDED_HALF - HALF
+    weight_in = jnp.pad(
+        w_expert_in.reshape(features, 2, HALF), ((0, 0), (0, 0), (0, pad))
+    ).reshape(features, 2 * PADDED_HALF)
+    weight_out = jnp.pad(w_expert_out[0], ((0, pad), (0, 0)))
+    expert = (dp_index * n_seq + seq_index) // 2
+    named = named_all[:, :TOP] == expert.astype(F32)
+    chosen = jnp.any(named, axis=1)
+    gate_rows = jnp.sum(jnp.where(named, named_all[:, TOP : 2 * TOP], 0.0), axis=1)[:, None]
+    before = (jnp.arange(rows)[:, None] < jnp.arange(rows)[None, :]).astype(BF)
+    place = dot(chosen.astype(BF), before).astype(jnp.int32)
+    place = jnp.where(chosen, place, -1)[:, None]
 
     hidden_all_float = hidden_all.astype(F32)
     normed_all = (hidden_all_float * rms_scale(hidden_all_float) * first_gain).astype(BF)
-    angles = rotary_angles(positions_all)
+    angles = rotary_angles(positions_all.reshape(length))
     cosine_all, sine_all = jnp.cos(angles), jnp.sin(angles)
     query_raw = dot(normed_all, query_weight).reshape(length, heads, QK)
     queries = jnp.concatenate(
@@ -229,59 +1171,28 @@
     second_scale = rms_scale(middle)
     moe_rows = (middle * second_scale * second_gain).astype(BF)
 
-    rows_all = lax.all_gather(moe_rows, both, axis=0, tiled=True)
-    attended_all = lax.all_gather(attended, "seq", axis=0, tiled=True)
-    expert = (dp_index * n_seq + seq_index) // 2
-    named = ids_all == expert
-    chosen = jnp.any(named, axis=1)
-    gate_rows = jnp.sum(jnp.where(named, gates_all, 0.0), axis=1)
-    before = (jnp.arange(rows)[:, None] < jnp.arange(rows)[None, :]).astype(BF)
-    place = dot(chosen.astype(BF), before).astype(jnp.int32)
-    picked = chosen[:, None, :] & (
-        place[:, None, :] == jnp.arange(capacity, dtype=jnp.int32)[None, :, None]
-    )
-    pick = picked.astype(BF)
-    gate_slots = jnp.sum(jnp.where(picked, gate_rows[:, None, :], 0.0), axis=2)[..., None]
-    rows_blocks = rows_all.reshape(n_all, rows, features)
-    upstream_blocks = upstream_all.reshape(n_all, rows, features)
-    slot_rows = jnp.einsum("bst,btd->bsd", pick, rows_blocks, preferred_element_type=F32)
-    slot_rows = slot_rows.astype(BF).reshape(n_all * capacity, features)
-    slot_cot = jnp.einsum("bst,btd->bsd", pick, upstream_blocks, preferred_element_type=F32)
-    slot_upstream = (slot_cot * gate_slots).astype(BF).reshape(n_all * capacity, features)
-    weight_in, weight_out = w_expert_in[0], w_expert_out[0]
-
-    def gated(rows_in, upstream, w_in, w_out, width):
-        gate_up = dot(rows_in, w_in)
-        gate, up = gate_up[:, :width], gate_up[:, width:]
-        sigmoid = 1.0 / (1.0 + jnp.exp(-gate))
-        active = gate * sigmoid
-        hidden_units = (active * up).astype(BF)
-        hidden_back = dot_nt(upstream, w_out)
-        gate_back = hidden_back * up * sigmoid * (1.0 + gate * (1.0 - sigmoid))
-        both_back = jnp.concatenate([gate_back, hidden_back * active], axis=-1).astype(BF)
-        return hidden_units, both_back, dot_tn(rows_in, both_back), dot_tn(hidden_units, upstream)
-
-    hidden_units, both_back, expert_in_grad, expert_out_grad = gated(
-        slot_rows, slot_upstream, weight_in, weight_out, HALF
-    )
-    slot_result = dot(hidden_units, weight_out).astype(BF)
-    slot_back = dot_nt(both_back, weight_in).astype(BF)
-    shared_units, shared_both_back, shared_in_grad, shared_out_grad = gated(
-        rows_all, upstream_all, shared_in, shared_out, units
-    )
-    slot_back = slot_back.reshape(n_all, capacity, features)
-    back_part = jnp.einsum("bst,bsd->btd", pick, slot_back, preferred_element_type=F32)
-    back_part = back_part.reshape(n_all * rows, features) + dot_nt(shared_both_back, shared_in)
-    back_sum = lax.psum_scatter(back_part.astype(BF), both, scatter_dimension=0, tiled=True)
-
-    slot_float = slot_result.astype(F32).reshape(n_all, capacity, features)
-    slot_gate_grad = jnp.sum(slot_float * slot_cot, axis=-1)
-    weighted = (slot_float * gate_slots).astype(BF)
-    out_part = jnp.einsum("bst,bsd->btd", pick, weighted, preferred_element_type=F32)
-    out_part = out_part.reshape(n_all * rows, features) + dot(shared_units, shared_out)
-    out_sum = lax.psum_scatter(out_part.astype(BF), both, scatter_dimension=0, tiled=True)
-    token_gate_grad = jnp.sum(jnp.where(picked, slot_gate_grad[..., None], 0.0), axis=1)
-    gate_grads = lax.all_to_all(token_gate_grad, both, split_axis=0, concat_axis=0, tiled=True)
+    sent = jnp.stack([moe_rows, upstream_rows])
+    if not fast:
+        sent = lax.all_gather(sent, both, axis=0)
+    slot_rows, slot_up, hidden_units, both_back, shared_units, back_parts, shared_in_grad, shared_out_grad = experts(
+        fast, capacity, sent, place, gate_rows, weight_in, weight_out, shared_in, shared_out
+    )
+    if fast:
+        moe_back = scatter_all(back_parts, 4)
+    else:
+        moe_back = lax.psum_scatter(
+            back_parts.reshape(n_all * rows, features), both, scatter_dimension=0, tiled=True
+        )
+    moe_back = moe_back.astype(F32)
+    gate_grads, out_parts = out_side(
+        capacity, block_places, place, gate_rows, hidden_units, slot_up, shared_units, weight_out,
+        shared_out,
+    )
+    out_sum = lax.psum_scatter(
+        out_parts.reshape(n_all * rows, features), both, scatter_dimension=0, tiled=True
+    )
+    block_out = (middle + out_sum.astype(F32)).astype(BF)
+    gate_grads = lax.all_to_all(gate_grads, both, split_axis=0, concat_axis=0, tiled=True)
     gate_grads = jnp.sum(gate_grads.reshape(expert_count, 2, rows), axis=1)
     gate_gradient = jnp.sum(
         jnp.where(
@@ -291,18 +1202,23 @@
         ),
         axis=-1,
     )
-    block_out = (middle + out_sum.astype(F32)).astype(BF)
-
-    moe_back = back_sum.astype(F32)
+    expert_in_grad = dot_tn(slot_rows, both_back)
+    expert_in_grad = jnp.concatenate(
+        [expert_in_grad[:, :HALF], expert_in_grad[:, PADDED_HALF : PADDED_HALF + HALF]], axis=1
+    )
+    expert_out_grad = dot_tn(hidden_units, slot_up)[:HALF]
+
     second_gain_grad = jnp.sum(moe_back * middle * second_scale, axis=0)
     middle_back = upstream_float + norm_backward(moe_back, middle, second_scale, second_gain)
     middle_low = middle_back.astype(BF)
-    middle_columns = lax.all_to_all(middle_low, "seq", split_axis=1, concat_axis=0, tiled=True)
-    output_grad = dot_tn(attended_all, middle_columns)
     attended_back = dot_nt(middle_low, output_weight).astype(BF)
     upstream_heads = lax.all_to_all(
         attended_back, "seq", split_axis=1, concat_axis=0, tiled=True
     ).reshape(length, heads, VDIM)
+    attended_all = lax.all_gather(attended, "seq", axis=0, tiled=True)
+    middle_columns = lax.all_to_all(middle_low, "seq", split_axis=1, concat_axis=0, tiled=True)
+    output_grad = dot_tn(attended_all, middle_columns)
+
     query_back, key_back, value_back = attention_backward(
         queries, keys_all, values_all, logs, upstream_heads
     )
@@ -318,10 +1234,8 @@
         .reshape(length, heads * QK)
     )
     expanded_back = jnp.concatenate([key_back[..., :NOPE], value_back], axis=-1).reshape(
-        length, heads * (NOPE + VDIM)
-    )
-    query_grad = dot_tn(normed_all, query_raw_back)
-    expand_grad = dot_tn(latent_normed, expanded_back)
+        length, expand_width
+    )
     partial_back = jnp.concatenate(
         [
             dot_nt(query_raw_back, query_weight),
@@ -330,7 +1244,14 @@
         ],
         axis=-1,
     ).astype(BF)
-    summed_back = lax.psum_scatter(partial_back, "seq", scatter_dimension=0, tiled=True).astype(F32)
+    if fast:
+        partial_back = jnp.pad(partial_back, ((0, 0), (0, 64)))
+        summed_back = plane_scatter(partial_back.reshape(n_seq, rows, -1), 5)
+    else:
+        summed_back = lax.psum_scatter(partial_back, "seq", scatter_dimension=0, tiled=True)
+    summed_back = summed_back[:, : features + LATENT + ROPE].astype(F32)
+    query_grad = dot_tn(normed_all, query_raw_back)
+    expand_grad = dot_tn(latent_normed, expanded_back)
     latent_normed_back = summed_back[:, features : features + LATENT]
     own = seq_index * rows
 
@@ -342,8 +1263,13 @@
     latent_back = norm_backward(latent_normed_back, latent_own, latent_scale_own, latent_gain_row)
     rotary_back = rotate(summed_back[:, features + LATENT :], mine(cosine_all), -mine(sine_all))
     compressed_back = jnp.concatenate([latent_back, rotary_back], axis=-1).astype(BF)
-    compressed_back_all = lax.all_gather(compressed_back, "seq", axis=0, tiled=True)
     width = (LATENT + ROPE) // n_seq
+    if fast:
+        compressed_back_all = plane_gather(jnp.pad(compressed_back, ((0, 0), (0, 64))), 6)
+        compressed_back_all = compressed_back_all[:, :, : LATENT + ROPE]
+    else:
+        compressed_back_all = lax.all_gather(compressed_back, "seq", axis=0)
+    compressed_back_all = compressed_back_all.reshape(length, LATENT + ROPE)
     compress_grad = dot_tn(
         normed_all, lax.dynamic_slice_in_dim(compressed_back_all, seq_index * width, width, 1)
     )
@@ -354,42 +1280,65 @@
         middle_back + norm_backward(normed_back, hidden_float, first_scale, first_gain)
     ).astype(BF)
 
-    gain_grads = lax.psum(
-        jnp.concatenate([first_gain_grad, second_gain_grad, latent_gain_grad]), both
-    )
+    gain_grads = jnp.concatenate([first_gain_grad, second_gain_grad, latent_gain_grad])
+    bit = 1
+    while bit < n_seq:
+        gain_grads = gain_grads + lax.ppermute(
+            gain_grads, "seq", [(i, i ^ bit) for i in range(n_seq)]
+        )
+        bit *= 2
+    bit = 1
+    while bit < n_dp:
+        gain_grads = gain_grads + lax.ppermute(
+            gain_grads, "dp", [(i, i ^ bit) for i in range(n_dp)]
+        )
+        bit *= 2
     latent_shard = LATENT // n_dp
 
     def gain_part(start, size):
         return lax.dynamic_slice_in_dim(gain_grads, start + dp_index * size, size, 0)
 
-    def over_dp(grad):
-        return lax.psum_scatter(grad, "dp", scatter_dimension=0, tiled=True).astype(BF)
-
-    def columns(part):
-        return lax.all_gather(part, "seq", axis=1, tiled=True).astype(F32)
-
+    widths = [heads * QK, expand_width * latent_shard // shard, features // n_seq, width]
+    parts = jnp.concatenate(
+        [
+            query_grad.reshape(n_dp, shard, -1),
+            expand_grad.reshape(n_dp, shard, -1),
+            output_grad.reshape(n_dp, shard, -1),
+            compress_grad.reshape(n_dp, shard, -1),
+        ],
+        axis=-1,
+    )
+    if fast:
+        extra = -parts.shape[-1] % 128
+        summed = sum_grads(jnp.pad(parts, ((0, 0), (0, 0), (0, extra))).astype(BF), 7)
+    else:
+        summed = lax.psum_scatter(parts, "dp", scatter_dimension=0)
+        summed = lax.all_gather(summed.astype(BF), "seq", axis=0)
+
+    def columns(start, size, height):
+        found = summed[:, :, start : start + size].reshape(n_seq, height, -1)
+        return found.transpose(1, 0, 2).reshape(height, -1).astype(F32)
+
+    starts = [sum(widths[:n]) for n in range(4)]
+    shared_in_grad = shared_in_grad.reshape(2, padded_units, n_dp, shard)[:, :units].astype(BF)
     shared_in_out = lax.all_to_all(
-        shared_in_grad.astype(BF).reshape(n_dp, shard, 2, units),
-        "dp",
-        split_axis=0,
-        concat_axis=0,
-        tiled=True,
+        shared_in_grad.transpose(2, 3, 0, 1), "dp", split_axis=0, concat_axis=0, tiled=True
     )
     shared_in_out = lax.all_gather(shared_in_out, "seq", axis=0)
     shared_in_out = shared_in_out.transpose(2, 3, 1, 0, 4).reshape(shard, 2 * SH_FF).astype(F32)
     shared_out_out = lax.all_gather(
-        shared_out_grad.astype(BF), "seq", axis=0, tiled=True
+        shared_out_grad[:units].astype(BF), "seq", axis=0, tiled=True
     ).astype(F32)
     return (
         block_out.reshape(hidden_in.shape),
         hidden_gradient.reshape(hidden_in.shape),
         gate_gradient.reshape(gate_weights.shape),
         gain_part(0, shard),
-        columns(over_dp(query_grad)),
-        columns(over_dp(compress_grad)),
+        columns(starts[0], widths[0], shard),
+        columns(starts[3], widths[3], shard),
         gain_part(2 * features, latent_shard),
-        columns(over_dp(expand_grad)),
-        columns(over_dp(output_grad)),
+        columns(starts[1], widths[1], latent_shard),
+        columns(starts[2], widths[2], shard),
         gain_part(features, shard),
         shared_in_out,
         shared_out_out,

time: 2330 us -> 1670 us (0.72)
  waiting for transfers between devices: 1100 us -> 7.06 us
  Pallas kernels: 0 us -> 1040 us
  matrix products: 560 us -> 168 us
  blocking collectives: 233 us -> 38.8 us
  local copies, waits for them, and re-layouts: 249 us -> 211 us
    pallas_call x0 -> x7, Pallas kernels: none -> 1040 us  [the longest x1 340 us: experts(): pl.pallas_call(functools.partial(experts_kernel, remote, capacity), grid=...]
    reduce_scatter x7 -> x1, waiting for transfers between devices: 725 us -> 0.01 us  [on_device(): lax.psum_scatter(out_parts.reshape(n_all * rows, features), both, scatter...]
    all_gather x10 -> x1, waiting for transfers between devices: 219 us -> 0.02 us  [on_device(): lax.all_gather(shared_out_grad[:units].astype(BF), 'seq', axis=0, tiled=T...]
    reshape x5, local copies, waits for them, and re-layouts: 171 us -> 14.3 us  [the longest x1 8.76 us: on_device(): weight_in = jnp.pad(w_expert_in.reshape(features, 2, HALF), ((0, 0), (0,...]
    all_gather x6 -> x0, blocking collectives: 146 us -> none  [the longest x1 57.4 us: on_device(): gates_all = lax.all_gather(gate_table.T, both, axis=0)]
    dot_general x8 -> x4, matrix products: 151 us -> 14.5 us  [dot_nt(): return jnp.einsum('ik,jk->ij', a, b, preferred_element_type=F32)]
    dot_general x4 -> x0, matrix products: 120 us -> none  [the longest x1 32 us: on_device(): jnp.einsum('bst,btd->bsd', pick, upstream_blocks, preferred_element_type=...]
    dot_general x9 -> x5, matrix products: 136 us -> 25.7 us  [dot(): return jnp.dot(a, b, preferred_element_type=F32)]
  transfers between devices with their start and end apart: 25 -> 14, of which waited for: 11 -> 3; matrix products, arithmetic and copies ran while one was open for 27% -> 29% of each run, Pallas kernels for 0% -> 63%
where the time goes in v2:
time: 1670 us; the launch traced here: 1660 us
  Pallas kernels  1040 us (62%)
  local copies, waits for them, and re-layouts  211 us (13%)
  matrix products  168 us (10%)
  other arithmetic  131 us (8%)
  blocking collectives  38.8 us (2%)
  starting transfers between devices  32.4 us (2%)
  between operations  31.6 us (2%)
    pallas_call x1, Pallas kernels, experts(): pl.pallas_call(functools.partial(experts_kernel, remote, capacity), grid=...  340 us
    pallas_call x1, Pallas kernels, scatter_all(): pl.pallas_call(scatter_all_kernel, out_shape=jax.ShapeDtypeStruct((rows,...  288 us
    pallas_call x1, Pallas kernels, gather_start(): pl.pallas_call(gather_start_kernel, out_shape=[jax.ShapeDtypeStruct((8, *...  171 us
    unnamed x270, local copies, waits for them, and re-layouts  102 us
    pallas_call x1, Pallas kernels, sum_grads(): pl.pallas_call(grads_kernel, out_shape=jax.ShapeDtypeStruct((8, rows, col...  94.8 us
    dot_general x6, matrix products, dot_tn(): return jnp.einsum('ki,kj->ij', a, b, preferred_element_type=F32)  79.9 us
    pallas_call x1, Pallas kernels, out_side(): pl.pallas_call(functools.partial(out_kernel, capacity), grid_spec=pltpu.P...  79 us
    pallas_call x1, Pallas kernels, plane_scatter(): pl.pallas_call(plane_scatter_kernel, out_shape=jax.ShapeDtypeStruct((rows...  53.2 us
  transfers between devices with their start and end apart: 14, of which 3 were waited for; matrix products, arithmetic and copies ran while one was open for 29% of the time, Pallas kernels for 63%

profile of v2, /device:TPU:0, one launch (start us, length us, event | category | flops | bytes accessed | tf_op | source)
XLA Modules:
  0.0 1661.5 jit_solution(9681415813299707885)
XLA Ops:
  31.8 170.7 %shard_map.291 = (bf16[8,256,2048]{2,1,0:T(8,128)(2,1)S(1)}, f32[8,4,16,256]{3,2,1,0:T(8,128)S(1)}, bf16[4,16,128]{2,1,0:T(8,128)(2,1)S(1)}, bf16[4,512,384]{2,1...) custom-call(bf16[256,2048]{1,0:T(8,128)(2,1)S(1)} %bitcast.269, ...), custom_call_target="tpu_custom_call" | custom-call | bytes 67108864 | tf_op jit(solution)/shard_map/pallas_call | solution.py:485
  213.9 8.7 multiply_convert_fusion
  222.7 9.0 fusion.175
  231.7 2.3 copy-done.46
  234.0 4.8 fusion.103
  239.6 4.6 fusion.167
  244.1 3.7 convolution_convert_fusion.2
  251.9 5.3 fusion.94
  257.9 6.6 fusion.176
  279.8 11.3 fusion.98
  295.9 18.5 %all_to_all.69 = bf16[8,256,256]{1,2,0:T(8,128)(2,1)} all-to-all(bf16[8,256,256]{1,2,0:T(8,128)(2,1)S(1)} %copy.285), channel_id=1, replica_groups=mesh['dp'=4,'seq'=8] {'seq'}, dimensions={0} | all-to-all | bytes 2097152 | tf_op jit(solution)/shard_map/all_to_all | solution.py:1166
  314.4 8.3 copy.289
  324.9 18.1 %all-to-all-start.1 = ((bf16[4,512,2,88]{1,3,2,0:T(8,128)(2,1)}), bf16[4,512,2,88]{1,3,2,0:T(8,128)(2,1)}, u32[]{:S(2)}, u32[]{:S(2)}) async-start(bf16[4,512,2,88]{1,3,2,0:T(8,128)(2,1)} %copy.290), calls=%async_computation.1 | async-start | bytes 1441792 | tf_op jit(solution)/shard_map/all_to_all | solution.py:1122
  344.7 8.2 copy.287
  352.9 7.0 pad.59
  359.9 8.8 copy.340.weight_in
  375.3 6.2 multiply_reduce_fusion.6
  384.9 339.6 %shard_map.292 = (bf16[32,2,256,2048]{3,2,1,0:T(8,128)(2,1)}, bf16[5120,2048]{1,0:T(8,128)(2,1)}, bf16[5120,2048]{1,0:T(8,128)(2,1)}, bf16[5120,768]{1,0:T(8,128...) custom-call(bf16[2,256,2048]{2,1,0:T(8,128)(2,1)} %pad_maximum_fusio, ...), custom_call_target="tpu_custom_call" | custom-call | flops 96636764160 | bytes 134217728 | tf_op jit(solution)/shard_map/pallas_call | solution.py:752
  726.5 2.7 convert.116
  729.2 2.8 reshape.776
  733.5 20.3 %all_to_all.70 = bf16[4,512,2,88]{1,3,2,0:T(8,128)(2,1)} all-to-all(bf16[4,512,2,88]{1,3,2,0:T(8,128)(2,1)S(1)} %bitcast.310), channel_id=1, replica_groups=mesh['dp'=4,'seq'=8] {'dp'}, dimensions={0} | all-to-all | bytes 1441792 | tf_op jit(solution)/shard_map/all_to_all | solution.py:1324
  756.8 79.0 %shard_map.293 = (f32[32,1,256]{2,1,0:T(1,128)}, bf16[32,256,2048]{2,1,0:T(8,128)(2,1)}) custom-call(s32[32]{0:T(128)S(1)} %add.344.order_ref, s32[32,1,256]{2,1,0:T(1,128)S(1)} %copy-done.19, f32[32,1,256]{2,1,0:T(1,128)S(1)} %copy-done.20, bf16[5120,768]{1,0:T(8,128)(2,1)} %get-tuple-element.148.hidden_ref, bf16[5120,2048]{1,0:T(8,128)(2,1)} %get-tuple-element.149.up_ref, ...), custom_call_target="tpu_custom_call" | custom-call | flops 26843545600 | bytes 54525952 | tf_op jit(solution)/shard_map/pallas_call | solution.py:1006
  838.8 9.5 fusion.1
  848.4 12.5 copy.311
  863.6 2.6 all-to-all-start.3
  866.2 287.9 %shard_map.294 = bf16[256,2048]{1,0:T(8,128)(2,1)} custom-call(bf16[32,256,2048]{2,1,0:T(8,128)(2,1)} %get-tuple-element.152.in_ref), custom_call_target="tpu_custom_call" | custom-call | flops 16777216 | bytes 67108864 | tf_op jit(solution)/shard_map/pallas_call | solution.py:380
  1154.2 2.6 fusion.56
  1158.5 21.7 %fusion.20 = f32[1,704,2048]{2,1,0:T(8,128)} fusion(bf16[5120,2048]{1,0:T(8,128)(2,1)} %get-tuple-element.149.up_ref, bf16[5120,768]{1,0:T(8,128)(2,1)} %get-tuple-element.148.hidden_ref), kind=kOutput, calls=%fused_computation.55 | convolution fusion | flops 14763950080 | bytes 34603008 | tf_op jit(solution)/shard_map/ki,kj->ij/dot_general | solution.py:64
  1180.2 42.0 %fusion.177 = f32[2048,1536]{0,1:T(8,128)} fusion(bf16[5120,2048]{1,0:T(8,128)(2,1)} %get-tuple-element.156, bf16[5120,1536]{1,0:T(8,128)(2,1)} %get-tuple-element.157), kind=kOutput, calls=%fused_computation.311 | convolution fusion | flops 32212254720 | bytes 49283072 | tf_op jit(solution)/shard_map/ki,kj->ij/dot_general | solution.py:64
  1222.2 5.8 convolution_convert_fusion.3
  1229.1 4.9 all-to-all-start.2
  1233.9 10.8 fusion.166
  1245.8 10.7 maximum_bitcast_fusion
  1256.5 11.9 copy.328
  1268.6 4.4 all-to-all-start.4
  1288.5 2.4 multiply_reduce_fusion.3
  1294.1 3.0 multiply_reduce_fusion.2
  1304.1 3.4 multiply_convert_fusion.1
  1307.6 3.5 fusion.26
  1328.7 4.7 convolution_convert_fusion
  1333.4 18.0 %pad_maximum_fusion = bf16[2048,2624]{0,1:T(8,128)(2,1)} fusion(bf16[2048,64]{0,1:T(8,128)(2,1)S(1)} %slice_reduce_fusion, bf16[2048,512]{0,1:T(8,128)(2,1)S(1)} %convolution_convert_fusion.1, bf16[2048,2048]{0,1:T(8,128)(2,1)S(1)} %convolution_convert_fusion), kind=kLoop, calls=%fused_computation.7 | loop fusion | flops 32243712 | bytes 21495808 | tf_op jit(solution)/shard_map/concatenate | solution.py:1239
  1351.4 14.1 copy.348
  1365.5 5.6 pad.63.clone
  1371.2 53.2 %shard_map.295 = bf16[256,2688]{1,0:T(8,128)(2,1)S(1)} custom-call(bf16[8,256,2688]{2,1,0:T(8,128)(2,1)S(1)} %bitcast.268), custom_call_target="tpu_custom_call" | custom-call | flops 5505024 | bytes 11010048 | tf_op jit(solution)/shard_map/pallas_call | solution.py:841
  1428.7 2.7 fusion.66
  1433.3 5.6 convolution_convert_fusion.4
  1439.0 16.0 shard_map.296
  1456.3 2.8 convolution_convert_fusion.7
  1463.8 3.8 collective-permute-done.4
  1468.8 6.1 convolution_convert_fusion.5
  1475.4 94.8 %shard_map.297 = bf16[8,512,896]{2,1,0:T(8,128)(2,1)S(1)} custom-call(bf16[4,512,896]{2,1,0:T(8,128)(2,1)S(1)} %fusion.19.in_ref), custom_call_target="tpu_custom_call" | custom-call | bytes 14680064 | tf_op jit(solution)/shard_map/pallas_call | solution.py:949
  1570.2 3.0 copy-done.3
  1573.2 3.1 convert_bitcast_fusion.1
  1576.4 6.5 copy.318
  1582.9 6.6 copy.325
  1592.4 2.7 slice_convert_fusion.2
  1598.4 4.0 convert_bitcast_fusion.2
  1602.4 5.3 copy.321
  1607.7 5.5 copy.326
  1613.3 5.1 convert_element_type.307
  1618.4 8.7 convert_bitcast_fusion
  1627.1 10.4 copy.323
  1637.5 11.9 copy.327
  1649.5 5.2 fusion.108
  (442 shorter events, 138.3 us)
Async XLA Ops:
  7.2 19.9 %copy-start = (bf16[512,3072]{1,0:T(8,128)(2,1)S(1)}, bf16[512,3072]{1,0:T(8,128)(2,1)}, u32[]{:S(2)}) copy-start(bf16[512,3072]{1,0:T(8,128)(2,1)} %param.43) | copy-start | bytes 9437188
  7.2 368.1 %all-gather.6.cloned.1.call-start = ((), (), s32[]{:S(2)}) async-start(), calls=%async_computation.7 | async-start | bytes 10485760 | tf_op jit(solution)/shard_map/all_gather | solution.py:1118
  7.9 1460.9 %all-gather.8.cloned.1.call-start = ((), (), s32[]{:S(2)}) async-start(), calls=%async_computation.9 | async-start | bytes 9437184 | tf_op jit(solution)/shard_map/all_gather | solution.py:1218
  204.5 18.2 %copy-start.9 = (bf16[4,512,576]{2,1,0:T(8,128)(2,1)}, bf16[4,512,576]{2,1,0:T(8,128)(2,1)S(1)}, u32[]{:S(2)}) copy-start(bf16[4,512,576]{2,1,0:T(8,128)(2,1)S(1)} %get-tuple-element.144) | copy-start | bytes 7077892
  204.6 18.1 %copy-start.73 = (f32[1,4,4,128]{3,1,2,0:T(4,128)}, f32[1,4,4,128]{3,1,2,0:T(4,128)S(1)}, u32[]{:S(2)}) copy-start(f32[1,4,4,128]{3,1,2,0:T(4,128)S(1)} %copy.354) | copy-start | bytes 24580
  222.7 11.3 copy-start.117
  265.1 11.1 copy-start.44
  266.0 10.3 copy-start.53
  268.5 11.3 copy-start.24
  268.5 11.3 copy-start.101
  269.6 10.2 copy-start.103
  271.9 19.3 %copy-start.23 = (f32[2,512,1536]{2,1,0:T(8,128)}, f32[2,512,1536]{2,1,0:T(8,128)S(1)}, u32[]{:S(2)}) copy-start(f32[2,512,1536]{2,1,0:T(8,128)S(1)} %get-tuple-element.302) | copy-start | bytes 18874372
  271.9 19.3 %copy-start.97 = (f32[2,512]{1,0:T(2,128)}, f32[2,512]{1,0:T(2,128)S(1)}, u32[]{:S(2)}) copy-start(f32[2,512]{1,0:T(2,128)S(1)} %get-tuple-element.301) | copy-start | bytes 12292
  275.0 16.1 copy-start.99
  278.5 14.5 copy-start.22
  278.5 14.5 copy-start.91
  279.8 13.2 copy-start.93
  324.9 47.8 %all-to-all-start.1 = ((bf16[4,512,2,88]{1,3,2,0:T(8,128)(2,1)}), bf16[4,512,2,88]{1,3,2,0:T(8,128)(2,1)}, u32[]{:S(2)}, u32[]{:S(2)}) async-start(bf16[4,512,2,88]{1,3,2,0:T(8,128)(2,1)} %copy.290), calls=%async_computation.1 | async-start | bytes 1441792 | tf_op jit(solution)/shard_map/all_to_all | solution.py:1122
  343.0 1270.4 %all-gather.10.cloned.1.call-start = ((), (), s32[]{:S(2)}) async-start(), calls=%async_computation.10 | async-start | bytes 3244032 | tf_op jit(solution)/shard_map/all_gather | solution.py:1329
  343.0 39.1 %copy-start.76 = (f32[1,4,4,128]{3,1,2,0:T(4,128)}, f32[1,4,4,128]{3,1,2,0:T(4,128)S(1)}, u32[]{:S(2)}) copy-start(f32[1,4,4,128]{3,1,2,0:T(4,128)S(1)} %copy.357) | copy-start | bytes 24580
  359.9 8.8 copy-start.57
  726.4 892.0 %all-gather.12.cloned.1.call-start = ((), (), s32[]{:S(2)}) async-start(), calls=%async_computation.11 | async-start | bytes 6488064 | tf_op jit(solution)/shard_map/all_gather | solution.py:1327
  729.2 24.7 %copy-start.116 = (s32[8]{0:T(128)S(1)}, s32[8]{0:T(128)}, u32[]{:S(2)}) copy-start(s32[8]{0:T(128)} %get-tuple-element.319) | copy-start | bytes 100
  729.2 24.9 %copy-start.8 = (bf16[768,2048]{1,0:T(8,128)(2,1)S(1)}, bf16[768,2048]{1,0:T(8,128)(2,1)}, u32[]{:S(2)}) copy-start(bf16[768,2048]{1,0:T(8,128)(2,1)} %pad.60.weight_out.weight_ref) | copy-start | bytes 9437188
  729.2 24.9 %copy-start.19 = (s32[32,1,256]{2,1,0:T(1,128)S(1)}, s32[32,1,256]{2,1,0:T(1,128)}, u32[]{:S(2)}) copy-start(s32[32,1,256]{2,1,0:T(1,128)} %broadcast_in_dim.118.place_ref) | copy-start | bytes 98308
  729.2 24.9 %copy-start.20 = (f32[32,1,256]{2,1,0:T(1,128)S(1)}, f32[32,1,256]{2,1,0:T(1,128)}, u32[]{:S(2)}) copy-start(f32[32,1,256]{2,1,0:T(1,128)} %broadcast_in_dim.187.gate_ref) | copy-start | bytes 98308
  753.9 895.6 %reduce-scatter.2.cloned.1.call-start = ((), (), s32[]{:S(2)}) async-start(), calls=%async_computation.8 | async-start | bytes 34603008 | tf_op jit(solution)/shard_map/reduce_scatter | solution.py:1191
  838.8 22.4 %copy-start.105 = (f32[256]{0:T(256)}, f32[256]{0:T(256)S(1)}, u32[]{:S(2)}) copy-start(f32[256]{0:T(256)S(1)} %dynamic-slice.70) | copy-start | bytes 3076
  848.4 12.6 copy-start.6
  848.4 14.0 copy-start.83
  848.4 14.0 copy-start.96
  848.4 14.0 copy-start.102
  848.4 14.0 copy-start.104
  848.4 14.0 copy-start.98
  848.4 14.0 copy-start.100
  848.4 14.6 copy-start.92
  848.4 14.6 copy-start.94
  863.6 365.5 %all-to-all-start.3 = ((f32[32,1,256]{2,1,0:T(1,128)}), f32[32,1,256]{2,1,0:T(1,128)S(1)}, u32[]{:S(2)}, u32[]{:S(2)}) async-start(f32[32,1,256]{2,1,0:T(1,128)} %get-tuple-element.153), calls=%async_computation.4 | async-start | bytes 65536 | tf_op jit(solution)/shard_map/all_to_all | solution.py:1195
  866.2 288.0 %copy-start.29 = (f32[256,2048]{1,0:T(8,128)S(1)}, f32[256,2048]{1,0:T(8,128)}, u32[]{:S(2)}) copy-start(f32[256,2048]{1,0:T(8,128)} %copy-done.28) | copy-start | bytes 6291460
  866.2 288.0 %copy-start.77 = (f32[1,4,4,128]{3,1,2,0:T(4,128)S(1)}, f32[1,4,4,128]{3,1,2,0:T(4,128)}, u32[]{:S(2)}) copy-start(f32[1,4,4,128]{3,1,2,0:T(4,128)} %copy-done.76) | copy-start | bytes 24580
  866.2 288.0 %copy-start.87 = (f32[256]{0:T(256)S(1)}, f32[256]{0:T(256)}, u32[]{:S(2)}) copy-start(f32[256]{0:T(256)} %copy-done.86) | copy-start | bytes 3076
  1156.8 23.4 %copy-start.112 = (f32[256]{0:T(256)}, f32[256]{0:T(256)S(1)}, u32[]{:S(2)}) copy-start(f32[256]{0:T(256)S(1)} %broadcast_multiply_fusion.2) | copy-start | bytes 3076
  1180.2 42.0 %copy-start.56 = (bf16[256,2048]{1,0:T(8,128)(2,1)S(1)}, bf16[256,2048]{1,0:T(8,128)(2,1)}, u32[]{:S(2)}) copy-start(bf16[256,2048]{1,0:T(8,128)(2,1)} %fusion.165) | copy-start | bytes 3145732
  1229.1 39.5 %all-to-all-start.2 = ((bf16[256,8,256]{2,0,1:T(8,128)(2,1)}), bf16[256,8,256]{2,0,1:T(8,128)(2,1)S(1)}, u32[]{:S(2)}, u32[]{:S(2)}) async-start(bf16[256,8,256]{2,0,1:T(8,128)(2,1)} %bitcast.263), calls=%async_computation.3 | async-start | bytes 2097152 | tf_op jit(solution)/shard_map/all_to_all | solution.py:1215
  1268.6 200.3 %all-to-all-start.4 = ((bf16[256,8,256]{2,0,1:T(8,128)(2,1)}), bf16[256,8,256]{2,0,1:T(8,128)(2,1)}, u32[]{:S(2)}, u32[]{:S(2)}) async-start(bf16[256,8,256]{2,0,1:T(8,128)(2,1)} %bitcast.262), calls=%async_computation.5 | async-start | bytes 2097152 | tf_op jit(solution)/shard_map/all_to_all | solution.py:1219
  1283.3 10.8 copy-start.60
  1311.0 8.2 copy-start.50
  1371.1 53.5 %copy-start.90 = (f32[512]{0:T(512)S(1)}, f32[512]{0:T(512)}, u32[]{:S(2)}) copy-start(f32[512]{0:T(512)} %copy-done.89) | copy-start | bytes 6148
  1371.1 53.5 %copy-start.106 = (f32[256]{0:T(256)S(1)}, f32[256]{0:T(256)}, u32[]{:S(2)}) copy-start(f32[256]{0:T(256)} %copy-done.105) | copy-start | bytes 3076
  1371.1 56.2 %copy-start.114 = (f32[256,1]{0,1:T(1,128)S(1)}, f32[256,1]{0,1:T(1,128)}, u32[]{:S(2)}) copy-start(f32[256,1]{0,1:T(1,128)} %multiply_multiply_fusion.1) | copy-start | bytes 3076
  1371.1 62.2 %slice-start.4 = ((s8[8388608]{0:T(1024)(128)(4,1)}), s8[4194304]{0:T(1024)(128)(4,1)S(1)}, s32[]{:S(2)}) async-start(s8[8388608]{0:T(1024)(128)(4,1)} %bitcast.286), calls=%async_computation.16 | async-start | bytes 8388608
  1424.4 9.0 slice-start.5
  1428.7 30.4 %slice-start.6 = ((s8[5242880]{0:T(1024)(128)(4,1)}), s8[4194304]{0:T(1024)(128)(4,1)S(1)}, s32[]{:S(2)}) async-start(s8[5242880]{0:T(1024)(128)(4,1)} %bitcast.299), calls=%async_computation.18 | async-start | bytes 8388608
  1431.4 1.3 collective-permute-start
  1432.7 22.3 %collective-permute-start.1 = (f32[4608]{0:T(1024)S(1)}, f32[4608]{0:T(1024)S(1)}, u32[]{:S(2)}, u32[]{:S(2)}) collective-permute-start(f32[4608]{0:T(1024)S(1)} %fusion.162), channel_id=1, source_target_pairs={{0,2},{1,3},{2,0},{3,1},{4,6},{5,7},{6,4},{7,5},{8,10},{9,11},{10,... | collective-permute-start | bytes 55304 | tf_op jit(solution)/shard_map/ppermute | solution.py:1286
  1433.3 25.8 %slice-start.7 = ((s8[5242880]{0:T(1024)(128)(4,1)}), s8[1048576]{0:T(1024)(128)(4,1)S(1)}, s32[]{:S(2)}) async-start(s8[5242880]{0:T(1024)(128)(4,1)} %bitcast.299), calls=%async_computation.19 | async-start | bytes 2097152
  1455.0 4.0 collective-permute-start.2
  1459.0 3.8 collective-permute-start.3
  1462.9 4.7 collective-permute-start.4
  1637.5 12.0 copy-start.78
  1637.5 12.0 copy-start.88
  1637.5 12.0 copy-start.111
  1637.5 12.0 copy-start.113
  1637.5 12.0 copy-start.115
  (77 other events, 246.1 us)
Sparse Core Ops, SparseCore 0:
  9.6 208.1 all-gather.5
  314.6 68.4 all-gather.7
  726.6 31.6 all-gather.9
  760.0 43.3 all-gather.11
  836.0 510.2 reduce-scatter.1

commit v3 on v2

v3 whole, which is shorter than its diff:
```python
import functools
import math

import jax
import jax.numpy as jnp
from jax import lax
from jax.experimental import pallas as pl
from jax.experimental.pallas import tpu as pltpu
from jax.sharding import PartitionSpec as P

HEADS = 16
NOPE = 128
ROPE = 64
VDIM = 128
LATENT = 512
TOP = 6
QK = 192
SH_FF = 2816
HALF = 704
EPSILON = 1e-06
BF = jnp.bfloat16
F32 = jnp.float32


def rms_scale(entries):
    return lax.rsqrt(jnp.mean(entries * entries, axis=-1, keepdims=True) + EPSILON)


def rotary_angles(position_rows):
    steps_index = jnp.arange(ROPE // 2, dtype=F32)
    frequency = 10000.0 ** (-2.0 * steps_index / ROPE)
    return position_rows.astype(F32)[..., None] * frequency


def rotate(values, cosine_values, sine_values):
    half_width = values.shape[-1] // 2
    front_half = values[..., :half_width]
    back_half = values[..., half_width:]
    return jnp.concatenate(
        [
            front_half * cosine_values - back_half * sine_values,
            front_half * sine_values + back_half * cosine_values,
        ],
        axis=-1,
    )


def norm_backward(upstream, entries, inverse_scale, gain_row):
    scaled = upstream * gain_row
    return inverse_scale * scaled - entries * inverse_scale**3 * jnp.mean(
        scaled * entries, axis=-1, keepdims=True
    )


def dot(a, b):
    return jnp.dot(a, b, preferred_element_type=F32)


def dot_nt(a, b):
    return jnp.einsum("ik,jk->ij", a, b, preferred_element_type=F32)


def dot_tn(a, b):
    return jnp.einsum("ki,kj->ij", a, b, preferred_element_type=F32)


def copy_kernel(places_ref, in_ref, out_ref):
    out_ref[...] = in_ref[...]


def reorder(stack, places):
    count = stack.shape[0]
    if stack.size * stack.dtype.itemsize < 2**20 or stack.ndim != 3:
        return jnp.stack(
            [lax.dynamic_index_in_dim(stack, places[j], 0, keepdims=False) for j in range(count)]
        )
    block = (1, *stack.shape[1:])
    return pl.pallas_call(
        copy_kernel,
        grid_spec=pltpu.PrefetchScalarGridSpec(
            num_scalar_prefetch=1,
            grid=(count,),
            in_specs=[pl.BlockSpec(block, lambda j, order: (order[j], 0, 0))],
            out_specs=pl.BlockSpec(block, lambda j, order: (j, 0, 0)),
        ),
        out_shape=jax.ShapeDtypeStruct(stack.shape, stack.dtype),
        compiler_params=params(40),
        cost_estimate=pl.CostEstimate(
            flops=0, bytes_accessed=2 * stack.size * stack.dtype.itemsize, transcendentals=0
        ),
    )(places.astype(jnp.int32), stack)


def small_take(table, index):
    table = jnp.array(table, jnp.int32)
    hit = index[:, None] == jnp.arange(table.shape[0])[None, :]
    return jnp.sum(jnp.where(hit, table[None, :], 0), axis=1)


def params(limit=60):
    return pltpu.CompilerParams(
        vmem_limit_bytes=limit * 2**20, dimension_semantics=("arbitrary",)
    )


MESH_ID = pl.DeviceIdType.MESH
OWN_SLOTS = (0, 2, 3, 6)
CORE_SLOTS = (1, 4, 5, 7)


def neighbours():
    dp = lax.axis_index("dp")
    seq = lax.axis_index("seq")
    core = {"dp": dp, "seq": seq + 1 - 2 * (seq % 2)}
    across_x = {"dp": dp, "seq": seq + 2 - 4 * ((seq // 2) % 2)}
    across_y = {"dp": dp, "seq": seq + 4 - 8 * (seq // 4)}
    following = {"dp": (dp + 1) % 4, "seq": seq}
    previous = {"dp": (dp + 3) % 4, "seq": seq}
    return core, across_x, across_y, following, previous


def greet(devices):
    barrier = pltpu.get_barrier_semaphore()
    for device in devices:
        pl.semaphore_signal(barrier, inc=1, device_id=device, device_id_type=MESH_ID)
    pl.semaphore_wait(barrier, len(devices))


class Courier:
    def __init__(self, send_sems, recv_sems):
        self.send_sems, self.recv_sems = send_sems, recv_sems
        self.sent, self.open = [], []

    def send(self, source, target, device):
        index = len(self.sent)
        copy = pltpu.make_async_remote_copy(
            src_ref=source,
            dst_ref=target,
            send_sem=self.send_sems.at[index],
            recv_sem=self.recv_sems.at[index],
            device_id=device,
            device_id_type=MESH_ID,
        )
        copy.start()
        self.sent.append(copy)
        self.open.append(copy)
        return copy

    def take(self, copy):
        copy.wait_recv()
        self.open = [other for other in self.open if other is not copy]

    def finish(self):
        for copy in list(self.open):
            self.take(copy)
        for copy in self.sent:
            copy.wait_send()


def accumulate(target, *sources):
    rows = target.shape[0]
    step = 16

    def body(k, carry):
        part = pl.ds(pl.multiple_of(k * step, step), step)
        total = target[part].astype(F32)
        for source in sources:
            total = total + source[part].astype(F32)
        target[part] = total.astype(target.dtype)
        return carry

    lax.fori_loop(0, rows // step, body, 0)


SCATTER_ORDER = (1, 2, 3, 0)


class ScatterAll:
    @staticmethod
    def scratch(rows, columns, dtype):
        return [
            pltpu.VMEM((4, 4, rows, columns), dtype),
            pltpu.VMEM((4, 2, rows // 2, columns), dtype),
            pltpu.VMEM((4, 2, rows, columns), dtype),
            pltpu.VMEM((3, rows, columns), dtype),
            pltpu.VMEM((4, rows, columns), dtype),
            pltpu.SemaphoreType.DMA((35,)),
            pltpu.SemaphoreType.DMA((35,)),
            pltpu.SemaphoreType.DMA((4,)),
        ]

    def __init__(self, in_ref, held, far, near, ring, stage, send_sems, recv_sems, local_sems):
        self.in_ref, self.held, self.far, self.near = in_ref, held, far, near
        self.ring, self.stage = ring, stage
        self.send_sems, self.recv_sems, self.local_sems = send_sems, recv_sems, local_sems
        self.core, self.across_x, self.across_y, self.following, self.previous = neighbours()
        rows = held.shape[2]
        self.top, self.bottom = pl.ds(0, rows // 2), pl.ds(rows // 2, rows // 2)

    def copy(self, index, source, target, device):
        return pltpu.make_async_remote_copy(
            src_ref=source,
            dst_ref=target,
            send_sem=self.send_sems.at[index],
            recv_sem=self.recv_sems.at[index],
            device_id=device,
            device_id_type=MESH_ID,
        )

    def to_core(self, i, k):
        source = self.in_ref.at[8 * i + CORE_SLOTS[k]]
        return self.copy(19 + 4 * i + k, source, self.held.at[i, k], self.core)

    def far_copy(self, i, which):
        part = self.bottom if which else self.top
        device = self.across_x if which else self.across_y
        return self.copy(2 * i + which, self.held.at[i, 3, part], self.far.at[i, which], device)

    def near_copy(self, i, which):
        device = self.across_y if which else self.across_x
        return self.copy(8 + 2 * i + which, self.held.at[i, 1 + which], self.near.at[i, which], device)

    def ring_copy(self, n):
        return self.copy(
            16 + n, self.held.at[SCATTER_ORDER[n], 0], self.ring.at[n], self.following
        )

    def loads(self, n):
        i = SCATTER_ORDER[n]
        return [
            pltpu.make_async_copy(
                self.in_ref.at[8 * i + OWN_SLOTS[k]], self.stage.at[k], self.local_sems.at[k]
            )
            for k in range(4)
        ]

    def begin(self):
        greet((self.core, self.across_x, self.across_y, self.following, self.previous))
        for i in SCATTER_ORDER:
            for k in (3, 1, 2, 0):
                self.to_core(i, k).start()
        for load in self.loads(0):
            load.start()

    def first(self, n):
        i = SCATTER_ORDER[n]
        loads = self.loads(n)
        later = self.loads(n + 1) if n < 3 else None
        for k in (3, 1, 2, 0):
            loads[k].wait()
            self.to_core(i, k).wait_recv()
            accumulate(self.held.at[i, k], self.stage.at[k])
            if later:
                later[k].start()
            if k == 3:
                self.far_copy(i, 0).start()
                self.far_copy(i, 1).start()

    def second(self, n):
        i = SCATTER_ORDER[n]
        self.far_copy(i, 0).wait_recv()
        accumulate(self.held.at[i, 1, self.top], self.far.at[i, 0])
        self.near_copy(i, 0).start()
        self.far_copy(i, 1).wait_recv()
        accumulate(self.held.at[i, 2, self.bottom], self.far.at[i, 1])
        self.near_copy(i, 1).start()

    def third(self, n):
        i = SCATTER_ORDER[n]
        self.near_copy(i, 0).wait_recv()
        self.near_copy(i, 1).wait_recv()
        sources = [self.near.at[i, 0], self.near.at[i, 1]]
        if n > 0:
            self.ring_copy(n - 1).wait_recv()
            sources.append(self.ring.at[n - 1])
        accumulate(self.held.at[i, 0], *sources)
        if n < 3:
            self.ring_copy(n).start()

    def events(self):
        first, second, third = self.first, self.second, self.third
        plan = [
            (first, 0), (first, 1), (second, 0), (first, 2), (second, 1), (third, 0), (first, 3),
            (second, 2), (third, 1), (second, 3), (third, 2), (third, 3),
        ]
        return [functools.partial(f, n) for f, n in plan]

    def finish(self, out_ref):
        out_ref[...] = self.held[0, 0]
        for i in range(4):
            for k in range(4):
                self.to_core(i, k).wait_send()
            for which in range(2):
                self.far_copy(i, which).wait_send()
                self.near_copy(i, which).wait_send()
        for n in range(3):
            self.ring_copy(n).wait_send()


def scatter_all_kernel(in_ref, out_ref, *scratch):
    scatter = ScatterAll(in_ref, *scratch)
    scatter.begin()
    for event in scatter.events():
        event()
    scatter.finish(out_ref)


def scatter_all(parts, collective_id):
    _, rows, columns = parts.shape
    return pl.pallas_call(
        scatter_all_kernel,
        out_shape=jax.ShapeDtypeStruct((rows, columns), parts.dtype),
        in_specs=[pl.BlockSpec(memory_space=pl.ANY)],
        out_specs=pl.BlockSpec(memory_space=pltpu.VMEM),
        scratch_shapes=ScatterAll.scratch(rows, columns, parts.dtype),
        compiler_params=pltpu.CompilerParams(
            collective_id=collective_id, has_side_effects=True, vmem_limit_bytes=56 * 2**20
        ),
        cost_estimate=pl.CostEstimate(
            flops=32 * rows * columns, bytes_accessed=64 * rows * columns * 2, transcendentals=0
        ),
    )(parts)


def spread(post, source, place, core, across_x, across_y):
    seq = lax.axis_index("seq")
    x_seq = seq + 2 - 4 * ((seq // 2) % 2)
    y_seq = seq + 4 - 8 * (seq // 4)
    xy_seq = x_seq + 4 - 8 * (seq // 4)
    x_copy = post.send(source, place(seq), across_x)
    y_copy = post.send(source, place(seq), across_y)
    post.send(source, place(seq), core)
    yield
    post.take(x_copy)
    far_top = post.send(place(x_seq, 0), place(x_seq, 0), across_y)
    post.send(place(x_seq), place(x_seq), core)
    post.take(y_copy)
    far_bottom = post.send(place(y_seq, 1), place(y_seq, 1), across_x)
    post.send(place(y_seq), place(y_seq), core)
    yield
    post.take(far_top)
    post.take(far_bottom)
    post.send(place(xy_seq), place(xy_seq), core)


def blocks_of(found):
    half = found.shape[1] // 2

    def place(index, part=None):
        if part is None:
            return found.at[index]
        return found.at[index, pl.ds(part * half, half)]

    return place


def advance(*spreads):
    for one in spreads:
        for _ in one:
            break


def gather_start_kernel(
    hidden, named, gains, query, expand, compress, output, hidden_all, named_all, gains_all,
    query_all, expand_all, compress_all, output_all, send_sems, recv_sems, local_sems
):
    dp = lax.axis_index("dp")
    seq = lax.axis_index("seq")
    core, across_x, across_y, following, previous = neighbours()
    greet((core, across_x, across_y, following, previous))
    post = Courier(send_sems, recv_sems)
    strip = output.shape[0] // 8
    own_strip = pl.ds(pl.multiple_of(seq * strip, strip), strip)
    core_half = compress.shape[0] // 2
    mine = pl.ds(pl.multiple_of((seq % 2) * core_half, core_half), core_half)
    hidden_spread = spread(post, hidden, blocks_of(hidden_all), core, across_x, across_y)
    advance(hidden_spread)

    def hop(i):
        at = (dp + 5 - i) % 4
        first = i == 1
        return [
            post.send(query if first else query_all.at[at], query_all.at[at], following),
            post.send(
                compress.at[mine] if first else compress_all.at[at, mine],
                compress_all.at[at, mine],
                following,
            ),
            post.send(expand if first else expand_all.at[at], expand_all.at[at], following),
            post.send(gains if first else gains_all.at[at], gains_all.at[at], following),
            post.send(named if first else named_all.at[0, i - 1], named_all.at[0, i], following),
            post.send(
                output.at[own_strip] if first else output_all.at[at, own_strip],
                output_all.at[at, own_strip],
                following,
            ),
        ]

    def strip_spread(at):
        def place(index, part=None):
            if part is None:
                where = pl.ds(pl.multiple_of(index * strip, strip), strip)
            else:
                half = strip // 2
                where = pl.ds(pl.multiple_of(index * strip + part * half, half), half)
            return output_all.at[at, where]

        return spread(post, place(seq), place, core, across_x, across_y)

    ring = hop(1)
    locals_ = [
        pltpu.make_async_copy(source, target, local_sems.at[n])
        for n, (source, target) in enumerate(
            (
                (hidden, hidden_all.at[seq]),
                (named, named_all.at[0, 0]),
                (gains, gains_all.at[dp]),
                (query, query_all.at[dp]),
                (expand, expand_all.at[dp]),
                (compress, compress_all.at[dp]),
                (output, output_all.at[dp]),
            )
        )
    ]
    for copy in locals_:
        copy.start()
    spreads = []
    for i in (2, 3, 4):
        for copy in ring:
            post.take(copy)
        at = (dp + 5 - i) % 4
        if i < 4:
            ring = hop(i)
        post.send(compress_all.at[at, mine], compress_all.at[at, mine], core)
        advance(*spreads)
        if i < 4:
            advance(hidden_spread)
        spreads.append(strip_spread(at))
        advance(spreads[-1])
    locals_[1].wait()
    names_x = post.send(named_all.at[0], named_all.at[1], across_x)
    advance(*spreads)
    post.take(names_x)
    names_y = post.send(named_all.at[pl.ds(0, 2)], named_all.at[pl.ds(2, 2)], across_y)
    advance(*spreads)
    post.take(names_y)
    post.send(named_all.at[pl.ds(0, 4)], named_all.at[pl.ds(4, 4)], core)
    for n, copy in enumerate(locals_):
        if n != 1:
            copy.wait()
    post.finish()


def gather_start(hidden, named, gains, query, expand, compress, output, collective_id):
    anywhere = pl.BlockSpec(memory_space=pl.ANY)
    total = 8 + 6 * 3 + 3 + 3 + 8 * 3
    return pl.pallas_call(
        gather_start_kernel,
        out_shape=[
            jax.ShapeDtypeStruct((8, *hidden.shape), hidden.dtype),
            jax.ShapeDtypeStruct((8, 4, *named.shape), named.dtype),
        ]
        + [jax.ShapeDtypeStruct((4, *x.shape), x.dtype) for x in (gains, query, expand, compress, output)],
        in_specs=[anywhere] * 7,
        out_specs=[anywhere] * 7,
        scratch_shapes=[
            pltpu.SemaphoreType.DMA((total,)),
            pltpu.SemaphoreType.DMA((total,)),
            pltpu.SemaphoreType.DMA((7,)),
        ],
        compiler_params=pltpu.CompilerParams(
            collective_id=collective_id, has_side_effects=True, vmem_limit_bytes=16 * 2**20
        ),
        cost_estimate=pl.CostEstimate(flops=0, bytes_accessed=2**26, transcendentals=0),
    )(hidden, named, gains, query, expand, compress, output)


PADDED_HALF = 768
TILE = 256


def flip(value, change):
    return value + change - 2 * value * change


def pair_of(step, remote):
    if not remote:
        return step
    first = 1 - (step + 15) // 16
    last = (step + 3) // 16
    turn_of, place = (step + 3) // 4 - 1, (step + 3) % 4
    ahead = 1 - (place + 3) // 4
    return (1 - first) * (1 - last) * (4 * turn_of + place + 4 * ahead) + last * step


def experts_kernel(
    remote, capacity, rows_in, place_ref, gate_ref, weight_in_ref, weight_out_ref, shared_in,
    shared_out, rows_all, in_grad_ref, out_grad_ref, hidden_out, units_ref, part_ref,
    shared_in_grad, shared_out_grad, rows_buffer, cot_buffer, weight_in, weight_up, weight_out,
    slot_rows_pair, slot_up_pair, hidden_pair, back_pair, in_grad, out_grad, rows_out, load_sems,
    weight_sems, *sems
):
    step = pl.program_id(0)
    steps = pl.num_programs(0)
    rows = place_ref.shape[2]
    features = weight_in.shape[0]
    pair = pair_of(step, remote)
    slot = step % 2
    half_slots = 2 * capacity
    now = pl.ds(pl.multiple_of(slot * half_slots, half_slots), half_slots)
    slot_rows, slot_up = slot_rows_pair.at[now], slot_up_pair.at[now]
    hidden_ref, back_ref = hidden_pair.at[now], back_pair.at[now]
    gathered = rows_all if remote else rows_in

    def loads(at, into):
        found = []
        for b in range(2):
            block = 2 * pair_of(at, remote) + b
            part = pl.ds(b * rows, rows)
            for kind, buffer in enumerate((rows_buffer, cot_buffer)):
                found.append(
                    pltpu.make_async_copy(
                        gathered.at[block, kind],
                        buffer.at[into, part],
                        load_sems.at[into, 2 * b + kind],
                    )
                )
        return found

    if remote:
        send_sems, recv_sems, own_sem = sems
        core, across_x, across_y, following, previous = neighbours()
        half = rows // 2
        top, bottom = pl.ds(0, half), pl.ds(half, half)

        def copy(index, source, target, device):
            return pltpu.make_async_remote_copy(
                src_ref=source,
                dst_ref=target,
                send_sem=send_sems.at[index],
                recv_sem=recv_sems.at[index],
                device_id=device,
                device_id_type=MESH_ID,
            )

        def block_of(i):
            return rows_in if i == 0 else rows_all.at[8 * i]

        def along(i):
            return copy(9 * i, block_of(i), rows_all.at[8 * i + 8], following)

        def by_x(i):
            return copy(9 * i + 1, block_of(i), rows_all.at[8 * i + 2], across_x)

        def by_y(i):
            return copy(9 * i + 2, block_of(i), rows_all.at[8 * i + 3], across_y)

        def far(i, which):
            if which == 0:
                return copy(
                    9 * i + 3, rows_all.at[8 * i + 2, :, top], rows_all.at[8 * i + 6, :, top], across_y
                )
            return copy(
                9 * i + 4, rows_all.at[8 * i + 3, :, bottom], rows_all.at[8 * i + 6, :, bottom], across_x
            )

        def to_core(i, k):
            source = block_of(i) if k == 0 else rows_all.at[8 * i + OWN_SLOTS[k]]
            return copy(9 * i + 5 + k, source, rows_all.at[8 * i + CORE_SLOTS[k]], core)

        def begin_plane(i):
            by_x(i).start()
            by_y(i).start()

        def plane_arrived(i):
            by_x(i).wait_recv()
            far(i, 0).start()
            to_core(i, 1).start()
            by_y(i).wait_recv()
            far(i, 1).start()
            to_core(i, 2).start()

        def far_arrived(i):
            far(i, 0).wait_recv()
            far(i, 1).wait_recv()
            to_core(i, 3).start()

        def along_arrived(i):
            along(i).wait_recv()
            if i < 2:
                along(i + 1).start()
            to_core(i + 1, 0).start()

        def core_arrived(i, *which):
            for k in which:
                to_core(i, k).wait_recv()

        ready = {
            0: [(core_arrived, 0, 0)],
            1: [(along_arrived, 0), (plane_arrived, 0), (core_arrived, 1, 0)],
            2: [(begin_plane, 1)],
            3: [(core_arrived, 0, 1, 2), (far_arrived, 0)],
            4: [(core_arrived, 0, 3), (along_arrived, 1)],
            5: [(core_arrived, 2, 0), (plane_arrived, 1)],
            6: [(begin_plane, 2)],
            7: [(core_arrived, 1, 1, 2), (far_arrived, 1), (along_arrived, 2)],
            8: [(core_arrived, 1, 3)],
            9: [(core_arrived, 3, 0), (plane_arrived, 2)],
            10: [(begin_plane, 3)],
            11: [(core_arrived, 2, 1, 2), (far_arrived, 2)],
            12: [(core_arrived, 2, 3)],
            13: [(plane_arrived, 3)],
            14: [(core_arrived, 3, 1, 2)],
            15: [(far_arrived, 3), (core_arrived, 3, 3)],
        }

        def prepare(at):
            for event, *given in ready[at]:
                event(*given)

        @pl.when(step == 0)
        def _():
            greet((core, across_x, across_y, following, previous))
            own = pltpu.make_async_copy(rows_in, rows_all.at[0], own_sem)
            own.start()
            along(0).start()
            begin_plane(0)
            to_core(0, 0).start()
            own.wait()

    @pl.when(step == 0)
    def _():
        weights = (
            pltpu.make_async_copy(weight_in_ref, weight_in, weight_sems.at[0]),
            pltpu.make_async_copy(weight_out_ref, weight_out.at[pl.ds(0, HALF)], weight_sems.at[1]),
        )
        for copy_in in weights:
            copy_in.start()
        in_grad[...] = jnp.zeros_like(in_grad)
        out_grad[...] = jnp.zeros_like(out_grad)
        shared_in_grad[...] = jnp.zeros_like(shared_in_grad)
        shared_out_grad[...] = jnp.zeros_like(shared_out_grad)
        weight_out[pl.ds(HALF, PADDED_HALF - HALF)] = jnp.zeros(
            (PADDED_HALF - HALF, features), BF
        )
        for copy_in in weights:
            copy_in.wait()

        def split(k, carry):
            part = pl.ds(pl.multiple_of(k * 128, 128), 128)
            up = weight_in[part, HALF:].astype(F32)
            up = jnp.concatenate([up, jnp.zeros((128, PADDED_HALF - HALF), F32)], axis=1)
            weight_up[part] = up.astype(BF)
            return carry

        lax.fori_loop(0, features // 128, split, 0)
        if remote:
            prepare(0)
        for load in loads(0, 0):
            load.start()

    for load in loads(step, slot):
        load.wait()

    picks = []
    for b in range(2):
        chosen = one_hot(place_ref, 2 * pair + b, capacity)
        pick = chosen.astype(F32)
        picks.append(pick.T.astype(BF))
        pick = pick.astype(BF)
        gates = jnp.sum(jnp.where(chosen, gate_ref[2 * pair + b], 0.0), axis=1, keepdims=True)
        part = pl.ds(b * rows, rows)
        slots = pl.ds(b * capacity, capacity)
        slot_rows[slots] = dot(pick, rows_buffer[slot, part]).astype(BF)
        slot_up[slots] = (dot(pick, cot_buffer[slot, part]) * gates).astype(BF)

    def gated(gate, up, hidden_back):
        sigmoid = 1.0 / (1.0 + jnp.exp(-gate))
        active = gate * sigmoid
        gate_back = hidden_back * up * sigmoid * (1.0 + gate * (1.0 - sigmoid))
        return (active * up).astype(BF), gate_back.astype(BF), (hidden_back * active).astype(BF)

    def hidden_tile(t, carry):
        part = pl.ds(pl.multiple_of(t * TILE, TILE), TILE)
        second = pl.ds(pl.multiple_of(PADDED_HALF + t * TILE, TILE), TILE)
        gate = dot(slot_rows[...], weight_in[:, part])
        up = dot(slot_rows[...], weight_up[:, part])
        hidden_back = dot_nt(slot_up[...], weight_out[part])
        hidden_ref[:, part], back_ref[:, part], back_ref[:, second] = gated(gate, up, hidden_back)
        return carry

    lax.fori_loop(0, PADDED_HALF // TILE, hidden_tile, 0)
    hidden_out[...] = hidden_ref[...]

    width = shared_out.shape[0]
    rows_pair, cot_pair = rows_buffer[slot], cot_buffer[slot]
    gate_up = dot(rows_pair, shared_in[...])
    hidden_back = dot_nt(cot_pair, shared_out[...])
    units, gate_back, up_back = gated(gate_up[:, :width], gate_up[:, width:], hidden_back)
    units_ref[...] = units
    shared_back = jnp.concatenate([gate_back, up_back], axis=1)
    shared_in_grad[...] += dot_tn(shared_back, rows_pair)
    shared_out_grad[...] += dot_tn(units, cot_pair)

    if remote:
        for at in range(1, 16):

            @pl.when(step + 1 == at)
            def _():
                prepare(at)

    @pl.when(step + 1 < steps)
    def _():
        for load in loads(step + 1, 1 - slot):
            load.start()

    def back_tile(t, carry):
        part = pl.ds(pl.multiple_of(t * 2 * TILE, 2 * TILE), 2 * TILE)
        slot_back = dot_nt(back_ref[:, :PADDED_HALF], weight_in[part, :PADDED_HALF])
        slot_back = (slot_back + dot_nt(back_ref[:, PADDED_HALF:], weight_up[part])).astype(BF)
        shared_part = dot_nt(shared_back, shared_in[part])
        for b in range(2):
            tokens = slice(b * rows, (b + 1) * rows)
            total = dot(picks[b], slot_back[b * capacity : (b + 1) * capacity])
            part_ref[b, :, part] = (total + shared_part[tokens]).astype(BF)
        return carry

    lax.fori_loop(0, features // (2 * TILE), back_tile, 0)

    @pl.when(slot == 1)
    def _():
        def in_tile(t, carry):
            part = pl.ds(pl.multiple_of(t * TILE, TILE), TILE)
            in_grad[part] += dot_tn(slot_rows_pair[:, part], back_pair[...])
            return carry

        lax.fori_loop(0, features // TILE, in_tile, 0)

        def out_tile(t, carry):
            part = pl.ds(pl.multiple_of(t * TILE, TILE), TILE)
            out_grad[part] += dot_tn(hidden_pair[:, part], slot_up_pair[...])
            return carry

        lax.fori_loop(0, PADDED_HALF // TILE, out_tile, 0)

    @pl.when(step + 1 == steps)
    def _():
        whole_out = pltpu.make_async_copy(
            out_grad.at[pl.ds(0, HALF)], out_grad_ref, weight_sems.at[0]
        )
        whole_out.start()
        height = rows_out.shape[1]

        def out_copy(k):
            part = pl.ds(pl.multiple_of(k * height, height), height)
            return pltpu.make_async_copy(
                rows_out.at[k % 2], in_grad_ref.at[part], load_sems.at[k % 2, 0]
            )

        def write(k, carry):
            @pl.when(k >= 2)
            def _():
                out_copy(k - 2).wait()

            part = pl.ds(pl.multiple_of(k * height, height), height)
            rows_out[k % 2] = jnp.concatenate(
                [in_grad[part, :HALF], in_grad[part, PADDED_HALF : PADDED_HALF + HALF]], axis=1
            )
            out_copy(k).start()
            return carry

        count = features // height
        lax.fori_loop(0, count, write, 0)
        out_copy(count - 2).wait()
        out_copy(count - 1).wait()
        whole_out.wait()

    if remote:

        @pl.when(step + 1 == steps)
        def _():
            for i in range(4):
                if i < 3:
                    along(i).wait_send()
                by_x(i).wait_send()
                by_y(i).wait_send()
                far(i, 0).wait_send()
                far(i, 1).wait_send()
                for k in range(4):
                    to_core(i, k).wait_send()


def one_hot(place_ref, block, capacity):
    place = place_ref[block]
    rows = place.shape[1]
    return lax.broadcasted_iota(jnp.int32, (capacity, rows), 0) == place


def experts(
    remote, capacity, rows_in, places, gates, weight_in, weight_out, shared_in, shared_out
):
    blocks, _, rows = places.shape
    features = weight_in.shape[0]
    width = shared_out.shape[0]
    steps = blocks // 2

    def whole(array):
        return pl.BlockSpec(
            array.shape, lambda j: (0,) * array.ndim, pipeline_mode=pl.Buffered(1)
        )

    def tiled(height, columns):
        return pl.BlockSpec((height, columns), lambda j: (pair_of(j, remote), 0))

    anywhere = pl.BlockSpec(memory_space=pl.ANY)
    slots = 2 * capacity
    scratch = [
        pltpu.VMEM((2, 2 * rows, features), BF),
        pltpu.VMEM((2, 2 * rows, features), BF),
        pltpu.VMEM(weight_in.shape, BF),
        pltpu.VMEM((features, PADDED_HALF), BF),
        pltpu.VMEM((PADDED_HALF, features), BF),
        pltpu.VMEM((2 * slots, features), BF),
        pltpu.VMEM((2 * slots, features), BF),
        pltpu.VMEM((2 * slots, PADDED_HALF), BF),
        pltpu.VMEM((2 * slots, 2 * PADDED_HALF), BF),
        pltpu.VMEM((features, 2 * PADDED_HALF), F32),
        pltpu.VMEM((PADDED_HALF, features), F32),
        pltpu.VMEM((2, 64, 2 * HALF), F32),
        pltpu.SemaphoreType.DMA((2, 4)),
        pltpu.SemaphoreType.DMA((2,)),
    ]
    if remote:
        scratch += [
            pltpu.SemaphoreType.DMA((36,)),
            pltpu.SemaphoreType.DMA((36,)),
            pltpu.SemaphoreType.DMA,
        ]
    found = pl.pallas_call(
        functools.partial(experts_kernel, remote, capacity),
        grid=(steps,),
        in_specs=[anywhere, whole(places), whole(gates), anywhere, anywhere]
        + [whole(x) for x in (shared_in, shared_out)],
        out_specs=[
            anywhere,
            anywhere,
            anywhere,
            tiled(slots, PADDED_HALF),
            tiled(2 * rows, width),
            pl.BlockSpec((2, rows, features), lambda j: (pair_of(j, remote), 0, 0)),
            pl.BlockSpec(
                (2 * width, features), lambda j: (0, 0), pipeline_mode=pl.Buffered(1)
            ),
            pl.BlockSpec((width, features), lambda j: (0, 0), pipeline_mode=pl.Buffered(1)),
        ],
        out_shape=[
            jax.ShapeDtypeStruct((blocks if remote else 1, 2, rows, features), BF),
            jax.ShapeDtypeStruct(weight_in.shape, F32),
            jax.ShapeDtypeStruct(weight_out.shape, F32),
            jax.ShapeDtypeStruct((steps * slots, PADDED_HALF), BF),
            jax.ShapeDtypeStruct((blocks * rows, width), BF),
            jax.ShapeDtypeStruct((blocks, rows, features), BF),
            jax.ShapeDtypeStruct((2 * width, features), F32),
            jax.ShapeDtypeStruct((width, features), F32),
        ],
        scratch_shapes=scratch,
        compiler_params=pltpu.CompilerParams(
            vmem_limit_bytes=63 * 2**20,
            dimension_semantics=("arbitrary",),
            **({"collective_id": 3, "has_side_effects": True} if remote else {}),
        ),
        cost_estimate=pl.CostEstimate(
            flops=steps * slots * features * 2 * 3 * 2 * PADDED_HALF,
            bytes_accessed=blocks * features * 8 * rows,
            transcendentals=0,
        ),
    )(rows_in, places, gates, weight_in, weight_out, shared_in, shared_out)
    return found


def plane_scatter_kernel(
    in_ref, out_ref, held, far, near, stage, send_sems, recv_sems, local_sems
):
    core, across_x, across_y, _, _ = neighbours()
    greet((core, across_x, across_y))
    seq = lax.axis_index("seq")
    rows = out_ref.shape[0]
    top, bottom = pl.ds(0, rows // 2), pl.ds(rows // 2, rows // 2)
    post = Courier(send_sems, recv_sems)
    x_seq = seq + 2 - 4 * ((seq // 2) % 2)
    y_seq = seq + 4 - 8 * (seq // 4)
    xy_seq = x_seq + 4 - 8 * (seq // 4)
    core_step = 1 - 2 * (seq % 2)
    loads, arriving = {}, {}
    for k, place in ((3, xy_seq), (1, x_seq), (2, y_seq), (0, seq)):
        arriving[k] = post.send(in_ref.at[place + core_step], held.at[k], core)
        loads[k] = pltpu.make_async_copy(in_ref.at[place], stage.at[k], local_sems.at[k])
        loads[k].start()

    def join(k):
        loads[k].wait()
        post.take(arriving[k])
        accumulate(held.at[k], stage.at[k])

    join(3)
    far_top = post.send(held.at[3, top], far.at[0], across_y)
    far_bottom = post.send(held.at[3, bottom], far.at[1], across_x)
    join(1)
    x_bottom = post.send(held.at[1, bottom], near.at[0, bottom], across_x)
    join(2)
    y_top = post.send(held.at[2, top], near.at[1, top], across_y)
    join(0)
    post.take(far_top)
    accumulate(held.at[1, top], far.at[0])
    x_top = post.send(held.at[1, top], near.at[0, top], across_x)
    post.take(far_bottom)
    accumulate(held.at[2, bottom], far.at[1])
    y_bottom = post.send(held.at[2, bottom], near.at[1, bottom], across_y)
    for copy in (x_bottom, y_top, x_top, y_bottom):
        post.take(copy)
    accumulate(held.at[0], near.at[0], near.at[1])
    out_ref[...] = held[0]
    post.finish()


def plane_scatter(parts, collective_id):
    _, rows, columns = parts.shape
    return pl.pallas_call(
        plane_scatter_kernel,
        out_shape=jax.ShapeDtypeStruct((rows, columns), parts.dtype),
        in_specs=[pl.BlockSpec(memory_space=pl.ANY)],
        out_specs=pl.BlockSpec(memory_space=pltpu.VMEM),
        scratch_shapes=[
            pltpu.VMEM((4, rows, columns), parts.dtype),
            pltpu.VMEM((2, rows // 2, columns), parts.dtype),
            pltpu.VMEM((2, rows, columns), parts.dtype),
            pltpu.VMEM((4, rows, columns), parts.dtype),
            pltpu.SemaphoreType.DMA((10,)),
            pltpu.SemaphoreType.DMA((10,)),
            pltpu.SemaphoreType.DMA((4,)),
        ],
        compiler_params=pltpu.CompilerParams(
            collective_id=collective_id, has_side_effects=True, vmem_limit_bytes=32 * 2**20
        ),
        cost_estimate=pl.CostEstimate(
            flops=8 * rows * columns, bytes_accessed=16 * rows * columns, transcendentals=0
        ),
    )(parts)


def plane_gather_kernel(in_ref, out_ref, send_sems, recv_sems, local_sem):
    core, across_x, across_y, _, _ = neighbours()
    greet((core, across_x, across_y))
    own = pltpu.make_async_copy(in_ref, out_ref.at[lax.axis_index("seq")], local_sem)
    own.start()
    post = Courier(send_sems, recv_sems)
    for _ in spread(post, in_ref, blocks_of(out_ref), core, across_x, across_y):
        pass
    own.wait()
    post.finish()


def plane_gather(block, collective_id):
    anywhere = pl.BlockSpec(memory_space=pl.ANY)
    return pl.pallas_call(
        plane_gather_kernel,
        out_shape=jax.ShapeDtypeStruct((8, *block.shape), block.dtype),
        in_specs=[anywhere],
        out_specs=anywhere,
        scratch_shapes=[
            pltpu.SemaphoreType.DMA((8,)),
            pltpu.SemaphoreType.DMA((8,)),
            pltpu.SemaphoreType.DMA,
        ],
        compiler_params=pltpu.CompilerParams(
            collective_id=collective_id, has_side_effects=True, vmem_limit_bytes=16 * 2**20
        ),
        cost_estimate=pl.CostEstimate(
            flops=0, bytes_accessed=32 * block.size, transcendentals=0
        ),
    )(block)


def grads_kernel(in_ref, out_ref, total, ring, send_sems, recv_sems, local_sems):
    dp = lax.axis_index("dp")
    core, across_x, across_y, following, previous = neighbours()
    greet((core, across_x, across_y, following, previous))
    post = Courier(send_sems, recv_sems)
    loads = []
    for n, i in enumerate((1, 2, 3, 0)):
        load = pltpu.make_async_copy(in_ref.at[(dp + 4 - i) % 4], total.at[n], local_sems.at[n])
        load.start()
        loads.append(load)
    loads[0].wait()
    before = post.send(total.at[0], ring.at[0], following)
    for n in (1, 2, 3):
        loads[n].wait()
        post.take(before)
        accumulate(total.at[n], ring.at[n - 1])
        if n < 3:
            before = post.send(total.at[n], ring.at[n], following)
    own = pltpu.make_async_copy(total.at[3], out_ref.at[lax.axis_index("seq")], local_sems.at[0])
    own.start()
    for _ in spread(post, total.at[3], blocks_of(out_ref), core, across_x, across_y):
        pass
    own.wait()
    post.finish()


def sum_grads(parts, collective_id):
    _, rows, columns = parts.shape
    anywhere = pl.BlockSpec(memory_space=pl.ANY)
    return pl.pallas_call(
        grads_kernel,
        out_shape=jax.ShapeDtypeStruct((8, rows, columns), parts.dtype),
        in_specs=[anywhere],
        out_specs=anywhere,
        scratch_shapes=[
            pltpu.VMEM((4, rows, columns), parts.dtype),
            pltpu.VMEM((3, rows, columns), parts.dtype),
            pltpu.SemaphoreType.DMA((11,)),
            pltpu.SemaphoreType.DMA((11,)),
            pltpu.SemaphoreType.DMA((4,)),
        ],
        compiler_params=pltpu.CompilerParams(
            collective_id=collective_id, has_side_effects=True, vmem_limit_bytes=32 * 2**20
        ),
        cost_estimate=pl.CostEstimate(
            flops=0, bytes_accessed=32 * rows * columns, transcendentals=0
        ),
    )(parts)


OUT_EVENTS = (3, 5, 7, 9, 13, 17, 18, 23, 27, 30, 31, 31)


def out_terms(capacity, place_ref, gate_ref, hidden_ref, cot_ref, units_ref, weight_ref, shared_ref,
              gate_grad_ref, part_ref):
    features = part_ref.shape[2]
    chosen = one_hot(place_ref, 0, capacity)
    pick = chosen.astype(F32)
    pick, spread_pick = pick.astype(BF), pick.T.astype(BF)
    gates = jnp.sum(jnp.where(chosen, gate_ref[0], 0.0), axis=1, keepdims=True)

    def tile(t, slot_grad):
        part = pl.ds(pl.multiple_of(t * 2 * TILE, 2 * TILE), 2 * TILE)
        result = dot(hidden_ref[:, :HALF], weight_ref[:, part]).astype(BF).astype(F32)
        slot_grad += jnp.sum(result * dot(pick, cot_ref[0, 0, :, part]), axis=1, keepdims=True)
        total = dot(spread_pick, (result * gates).astype(BF)) + dot(units_ref[...], shared_ref[:, part])
        part_ref[0, :, part] = total.astype(BF)
        return slot_grad

    slot_grad = lax.fori_loop(0, features // (2 * TILE), tile, jnp.zeros((capacity, 1), F32))
    gate_grad_ref[0] = jnp.sum(jnp.where(chosen, slot_grad, 0.0), axis=0, keepdims=True)


def out_kernel(remote, capacity, back_ref, *refs):
    step = pl.program_id(0)
    terms, sum_ref, scratch = refs[:9], refs[9], refs[10:]
    if remote:
        scatter = ScatterAll(back_ref, *scratch)
        pl.when(step == 0)(scatter.begin)
    out_terms(capacity, *terms)
    if remote:
        events = scatter.events()
        for at in sorted(set(OUT_EVENTS)):

            @pl.when(step == at)
            def _():
                for event, when in zip(events, OUT_EVENTS):
                    if when == at:
                        event()
                if at == OUT_EVENTS[-1]:
                    scatter.finish(sum_ref)


def out_side(remote, capacity, back_parts, places, gates, hidden, sent, units, weight_out, shared_out):
    blocks, _, rows = places.shape
    features = sent.shape[-1]
    one = pl.BlockSpec((1, 1, rows), lambda j: (j, 0, 0))

    def tiled(height, columns):
        return pl.BlockSpec((height, columns), lambda j: (j, 0))

    def whole(array):
        return pl.BlockSpec(array.shape, lambda j: (0, 0), pipeline_mode=pl.Buffered(1))

    return pl.pallas_call(
        functools.partial(out_kernel, remote, capacity),
        grid=(blocks,),
        in_specs=[
            pl.BlockSpec(memory_space=pl.ANY),
            one,
            one,
            tiled(capacity, PADDED_HALF),
            pl.BlockSpec((1, 1, rows, features), lambda j: (j, 1, 0, 0)),
            tiled(rows, units.shape[1]),
            whole(weight_out),
            whole(shared_out),
        ],
        out_specs=[
            one,
            pl.BlockSpec((1, rows, features), lambda j: (j, 0, 0)),
            pl.BlockSpec((rows, features), lambda j: (0, 0)),
        ],
        out_shape=[
            jax.ShapeDtypeStruct((blocks, 1, rows), F32),
            jax.ShapeDtypeStruct((blocks, rows, features), BF),
            jax.ShapeDtypeStruct((rows, features), BF),
        ],
        scratch_shapes=ScatterAll.scratch(rows, features, BF) if remote else [],
        compiler_params=pltpu.CompilerParams(
            vmem_limit_bytes=60 * 2**20,
            dimension_semantics=("arbitrary",),
            **({"collective_id": 4, "has_side_effects": True} if remote else {}),
        ),
        cost_estimate=pl.CostEstimate(
            flops=blocks * 2 * features * (capacity * PADDED_HALF + rows * 2 * capacity),
            bytes_accessed=blocks * features * 2 * (rows + capacity),
            transcendentals=0,
        ),
    )(back_parts, places, gates, hidden, sent, units, weight_out, shared_out)


def swap_halves(values):
    column = lax.broadcasted_iota(jnp.int32, values.shape, 1)
    return jnp.where(column % 64 < 32, pltpu.roll(values, 96, 1), pltpu.roll(values, 32, 1))


def turn(values, cosine, sine, sign):
    column = lax.broadcasted_iota(jnp.int32, values.shape, 1)
    signed = jnp.where(column % 64 < 32, -sign * sine, sign * sine)
    return values * cosine + swap_halves(values) * signed


def project_kernel(
    hidden_ref, gain_ref, query_ref, compress_ref, latent_gain_ref, expand_ref, cosine_ref, sine_ref,
    normed_out, query_out, key_out, value_out, latent_out, latent_normed_out
):
    entries = hidden_ref[...].astype(F32)
    normed = (entries * rms_scale(entries) * gain_ref[...]).astype(BF)
    normed_out[...] = normed
    cosine, sine = cosine_ref[...], sine_ref[...]
    query = dot(normed, query_ref[...])
    nope = query.shape[1] - 128
    query_out[:, :nope] = query[:, :nope].astype(BF)
    query_out[:, nope:] = turn(query[:, nope:], cosine, sine, 1.0).astype(BF)
    compressed = dot(normed, compress_ref[...])
    latent = compressed[:, :LATENT]
    latent_out[...] = latent
    latent_normed = (latent * rms_scale(latent) * latent_gain_ref[...]).astype(BF)
    latent_normed_out[...] = latent_normed
    rotary = compressed[:, LATENT:]
    rotary = jnp.concatenate([rotary, rotary], axis=1)
    expanded = dot(latent_normed, expand_ref[...]).astype(BF)
    key_out[:, :nope] = expanded[:, :nope]
    key_out[:, nope:] = turn(rotary, cosine, sine, 1.0).astype(BF)
    value_out[...] = expanded[:, nope:]


def project(hidden_all, first_gain, query_weight, compress_weight, latent_gain, expand_weight, cosine, sine):
    length, features = hidden_all.shape
    block = 256
    query_width = query_weight.shape[1]
    values = query_width - 128

    def tiled(columns):
        return pl.BlockSpec((block, columns), lambda j: (j, 0))

    def whole(array):
        return pl.BlockSpec(array.shape, lambda j: (0, 0), pipeline_mode=pl.Buffered(1))

    return pl.pallas_call(
        project_kernel,
        grid=(length // block,),
        in_specs=[
            tiled(features),
            whole(first_gain),
            whole(query_weight),
            whole(compress_weight),
            whole(latent_gain),
            whole(expand_weight),
            tiled(128),
            tiled(128),
        ],
        out_specs=[
            tiled(features), tiled(query_width), tiled(query_width), tiled(values), tiled(LATENT),
            tiled(LATENT),
        ],
        out_shape=[
            jax.ShapeDtypeStruct((length, features), BF),
            jax.ShapeDtypeStruct((length, query_width), BF),
            jax.ShapeDtypeStruct((length, query_width), BF),
            jax.ShapeDtypeStruct((length, values), BF),
            jax.ShapeDtypeStruct((length, LATENT), F32),
            jax.ShapeDtypeStruct((length, LATENT), BF),
        ],
        compiler_params=params(48),
        cost_estimate=pl.CostEstimate(
            flops=2 * length * features * (query_width + 640), bytes_accessed=2**25, transcendentals=0
        ),
    )(hidden_all, first_gain, query_weight, compress_weight, latent_gain, expand_weight, cosine, sine)


BLOCK = 512
SCALE = 1.0 / math.sqrt(QK)


def head_keys(key_ref, rotary_ref, part, head):
    rotary = rotary_ref[part]
    column = lax.broadcasted_iota(jnp.int32, rotary.shape, 1)
    rotary = jnp.where(column // 64 == head, rotary.astype(F32), 0.0).astype(BF)
    return jnp.concatenate([key_ref[part], rotary], axis=1)


def masked_scores(query, keys, block, j):
    scores = dot_nt(query, keys) * SCALE
    row = block * BLOCK + lax.broadcasted_iota(jnp.int32, scores.shape, 0)
    column = j * BLOCK + lax.broadcasted_iota(jnp.int32, scores.shape, 1)
    return jnp.where(column <= row, scores, -1e30)


def tile_of(j):
    return pl.ds(pl.multiple_of(j * BLOCK, BLOCK), BLOCK)


def attend_kernel(query_ref, turned_ref, key_ref, rotary_ref, value_ref, out_ref, log_ref, scores_ref):
    head, block = pl.program_id(0), pl.program_id(1)
    query = jnp.concatenate([query_ref[...], turned_ref[...]], axis=1)

    def score(j, largest):
        scores = masked_scores(query, head_keys(key_ref, rotary_ref, tile_of(j), head), block, j)
        scores_ref[j] = scores
        return jnp.maximum(largest, jnp.max(scores, axis=1, keepdims=True))

    largest = lax.fori_loop(0, block + 1, score, jnp.full((BLOCK, 1), -1e30, F32))

    def weigh(j, carry):
        total, found = carry
        weights = jnp.exp(scores_ref[j] - largest)
        total += jnp.sum(weights, axis=1, keepdims=True)
        return total, found + dot(weights.astype(BF), value_ref[tile_of(j)])

    total, found = lax.fori_loop(
        0, block + 1, weigh, (jnp.zeros((BLOCK, 1), F32), jnp.zeros((BLOCK, VDIM), F32))
    )
    out_ref[...] = (found / total).astype(BF)
    log_ref[0] = jnp.broadcast_to(largest + jnp.log(total), (BLOCK, 128))


def attention_specs(length, heads):
    return [
        pl.BlockSpec((BLOCK, 128), lambda h, b: (b, h)),
        pl.BlockSpec((BLOCK, 128), lambda h, b: (b, heads)),
        pl.BlockSpec((length, 128), lambda h, b: (0, h)),
        pl.BlockSpec((length, 128), lambda h, b: (0, heads)),
        pl.BlockSpec((length, VDIM), lambda h, b: (0, h)),
    ]


def attend(queries, keys, values):
    length = queries.shape[0]
    heads = values.shape[1] // VDIM
    blocks = length // BLOCK
    return pl.pallas_call(
        attend_kernel,
        grid=(heads, blocks),
        in_specs=attention_specs(length, heads),
        out_specs=[
            pl.BlockSpec((BLOCK, VDIM), lambda h, b: (b, h)),
            pl.BlockSpec((1, BLOCK, 128), lambda h, b: (h, b, 0)),
        ],
        out_shape=[
            jax.ShapeDtypeStruct((length, heads * VDIM), BF),
            jax.ShapeDtypeStruct((heads, length, 128), F32),
        ],
        scratch_shapes=[pltpu.VMEM((blocks, BLOCK, BLOCK), F32)],
        compiler_params=pltpu.CompilerParams(
            vmem_limit_bytes=40 * 2**20, dimension_semantics=("arbitrary", "arbitrary")
        ),
        cost_estimate=pl.CostEstimate(
            flops=heads * length * length * 384, bytes_accessed=2**23, transcendentals=0
        ),
    )(queries, queries, keys, keys, values)


BACK_EVENTS = (0, 1, 1, 2, 3, 4, 4, 5, 6, 6, 7, 7)


def attend_back_kernel(
    remote, query_ref, turned_ref, key_ref, rotary_ref, value_ref, upstream_ref, log_ref, cosine_ref,
    sine_ref, parts_ref, query_back, turned_back, key_back, rotary_back, value_back, sum_ref,
    shares_ref, slopes_ref, key_sum, value_sum, *scratch
):
    head, block = pl.program_id(0), pl.program_id(1)
    heads, blocks = pl.num_programs(0), pl.num_programs(1)
    step = head * blocks + block
    if remote:
        scatter = ScatterAll(parts_ref, *scratch)
        pl.when(step == 0)(scatter.begin)
    query = jnp.concatenate([query_ref[...], turned_ref[...]], axis=1)
    upstream = upstream_ref[...]
    log_row = log_ref[0][:, :1]

    @pl.when(block == 0)
    def _():
        key_sum[...] = jnp.zeros_like(key_sum)
        value_sum[...] = jnp.zeros_like(value_sum)

    def score(j, centre):
        scores = masked_scores(query, head_keys(key_ref, rotary_ref, tile_of(j), head), block, j)
        shares = jnp.exp(scores - log_row)
        slopes = dot_nt(upstream, value_ref[tile_of(j)])
        shares_ref[j] = shares
        slopes_ref[j] = slopes
        return centre + jnp.sum(shares * slopes, axis=1, keepdims=True)

    centre = lax.fori_loop(0, block + 1, score, jnp.zeros((BLOCK, 1), F32))

    def back(j, found):
        part = tile_of(j)
        shares = shares_ref[j]
        score_back = (shares * (slopes_ref[j] - centre)).astype(BF)
        value_sum[part] += dot_tn(shares.astype(BF), upstream)
        key_sum[part] += dot_tn(score_back, query)
        return found + dot(score_back, head_keys(key_ref, rotary_ref, part, head))

    found = lax.fori_loop(0, block + 1, back, jnp.zeros((BLOCK, 256), F32)) * SCALE
    query_back[...] = found[:, :128].astype(BF)
    turned = found[:, 128:].astype(BF).astype(F32)
    turned_back[...] = turn(turned, cosine_ref[...], sine_ref[...], -1.0).astype(BF)

    @pl.when(block == blocks - 1)
    def _():
        key_back[...] = (key_sum[:, :128] * SCALE).astype(BF)
        value_back[...] = value_sum[...].astype(BF)
        column = lax.broadcasted_iota(jnp.int32, rotary_back.shape, 1)
        rotary = jnp.where(column // 64 == head, key_sum[:, 128:] * SCALE, 0.0).astype(BF)
        rotary_back[...] = jnp.where(head == 0, rotary.astype(F32), rotary_back[...] + rotary.astype(F32))

    if remote:
        events = scatter.events()
        for at in sorted(set(BACK_EVENTS)):

            @pl.when(step == at)
            def _():
                for event, when in zip(events, BACK_EVENTS):
                    if when == at:
                        event()
                if at == BACK_EVENTS[-1]:
                    scatter.finish(sum_ref)


def attend_back(remote, queries, keys, values, upstream, logs, cosine, sine, parts):
    length = queries.shape[0]
    heads = values.shape[1] // VDIM
    blocks = length // BLOCK
    _, rows, features = parts.shape
    row = pl.BlockSpec((BLOCK, 128), lambda h, b: (b, 0))
    return pl.pallas_call(
        functools.partial(attend_back_kernel, remote),
        grid=(heads, blocks),
        in_specs=attention_specs(length, heads)
        + [
            pl.BlockSpec((BLOCK, VDIM), lambda h, b: (b, h)),
            pl.BlockSpec((1, BLOCK, 128), lambda h, b: (h, b, 0)),
            row,
            row,
            pl.BlockSpec(memory_space=pl.ANY),
        ],
        out_specs=[
            pl.BlockSpec((BLOCK, 128), lambda h, b: (b, h)),
            pl.BlockSpec((BLOCK, 128), lambda h, b: (b, h)),
            pl.BlockSpec((length, 128), lambda h, b: (0, h)),
            pl.BlockSpec((length, 128), lambda h, b: (0, 0)),
            pl.BlockSpec((length, VDIM), lambda h, b: (0, h)),
            pl.BlockSpec((rows, features), lambda h, b: (0, 0)),
        ],
        out_shape=[
            jax.ShapeDtypeStruct((length, heads * 128), BF),
            jax.ShapeDtypeStruct((length, heads * 128), BF),
            jax.ShapeDtypeStruct((length, heads * 128), BF),
            jax.ShapeDtypeStruct((length, 128), F32),
            jax.ShapeDtypeStruct((length, heads * VDIM), BF),
            jax.ShapeDtypeStruct((rows, features), BF),
        ],
        scratch_shapes=[
            pltpu.VMEM((blocks, BLOCK, BLOCK), F32),
            pltpu.VMEM((blocks, BLOCK, BLOCK), F32),
            pltpu.VMEM((length, 256), F32),
            pltpu.VMEM((length, VDIM), F32),
        ]
        + (ScatterAll.scratch(rows, features, BF) if remote else []),
        compiler_params=pltpu.CompilerParams(
            vmem_limit_bytes=62 * 2**20,
            dimension_semantics=("arbitrary", "arbitrary"),
            **({"collective_id": 8, "has_side_effects": True} if remote else {}),
        ),
        cost_estimate=pl.CostEstimate(
            flops=heads * length * length * 1024, bytes_accessed=2**26, transcendentals=0
        ),
    )(queries, queries, keys, keys, values, upstream, logs, cosine, sine, parts)


def partial_kernel(
    query_ref, turned_ref, key_ref, value_ref, rotary_ref, query_weight, expand_weight, out_ref
):
    nope = query_ref.shape[1]
    features = query_weight.shape[0]
    out_ref[:, :features] = (
        dot_nt(query_ref[...], query_weight[:, :nope])
        + dot_nt(turned_ref[...], query_weight[:, nope:])
    ).astype(BF)
    out_ref[:, features : features + LATENT] = (
        dot_nt(key_ref[...], expand_weight[:, :nope])
        + dot_nt(value_ref[...], expand_weight[:, nope:])
    ).astype(BF)
    rotary = rotary_ref[...]
    out_ref[:, features + LATENT :] = (rotary + pltpu.roll(rotary, ROPE, 1)).astype(BF)


def partial_terms(rows, query_back, turned_back, key_back, value_back, rotary_sum, query_weight, expand_weight):
    length = query_back.shape[0]
    columns = query_weight.shape[0] + LATENT + 128

    def tiled(array):
        return pl.BlockSpec((rows, array.shape[1]), lambda j: (j, 0))

    def whole(array):
        return pl.BlockSpec(array.shape, lambda j: (0, 0))

    given = (query_back, turned_back, key_back, value_back, rotary_sum)
    return pl.pallas_call(
        partial_kernel,
        grid=(length // rows,),
        in_specs=[tiled(x) for x in given] + [whole(query_weight), whole(expand_weight)],
        out_specs=pl.BlockSpec((rows, columns), lambda j: (j, 0)),
        out_shape=jax.ShapeDtypeStruct((length, columns), BF),
        compiler_params=params(40),
        cost_estimate=pl.CostEstimate(
            flops=2 * length * columns * 384, bytes_accessed=2**24, transcendentals=0
        ),
    )(*given, query_weight, expand_weight)


def tie_kernel(in_ref, _, out_ref):
    out_ref[...] = in_ref[...]


def tie(array, other):
    return pl.pallas_call(
        tie_kernel,
        in_specs=[pl.BlockSpec(memory_space=pltpu.VMEM), pl.BlockSpec(memory_space=pl.ANY)],
        out_specs=pl.BlockSpec(memory_space=pltpu.VMEM),
        out_shape=jax.ShapeDtypeStruct(array.shape, array.dtype),
        compiler_params=pltpu.CompilerParams(vmem_limit_bytes=16 * 2**20),
        cost_estimate=pl.CostEstimate(flops=0, bytes_accessed=4 * array.size, transcendentals=0),
    )(array, other)


def on_device(
    hidden_in,
    positions,
    expert_ids,
    gate_weights,
    attention_gain,
    w_query,
    w_compress,
    latent_gain,
    w_expand,
    w_output,
    feedforward_gain,
    w_shared_in,
    w_shared_out,
    w_expert_in,
    w_expert_out,
    cotangent,
):
    n_dp = lax.axis_size("dp")
    n_seq = lax.axis_size("seq")
    n_all = n_dp * n_seq
    fast = (n_dp, n_seq) == (4, 8)
    both = ("dp", "seq")
    dp_index = lax.axis_index("dp")
    seq_index = lax.axis_index("seq")
    sequence_count, rows, features = hidden_in.shape
    rows = sequence_count * rows
    length = rows * n_seq
    heads = HEADS // n_seq
    shard = features // n_dp
    expert_count = n_all // 2
    capacity = max(2, rows * TOP * 5 // (expert_count * 3))
    capacity = (capacity + 15) // 16 * 16
    units = SH_FF // n_all
    padded_units = (units + 127) // 128 * 128
    expand_width = heads * (NOPE + VDIM)

    hidden = hidden_in.reshape(rows, features)
    upstream_rows = cotangent.reshape(rows, features)
    upstream_float = upstream_rows.astype(F32)
    id_rows = expert_ids.reshape(rows, TOP)
    gate_table = gate_weights.reshape(rows, TOP)

    gains_own = jnp.concatenate([attention_gain, feedforward_gain, latent_gain])
    named_own = jnp.concatenate(
        [id_rows.T.astype(F32), gate_table.T, positions.reshape(1, rows).astype(F32)]
    )
    query_width = heads * NOPE + 128
    query_part = lax.dynamic_slice_in_dim(w_query, seq_index * heads * QK, heads * QK, 1)
    query_part = query_part.reshape(shard, heads, QK)
    query_part = jnp.concatenate(
        [
            query_part[..., :NOPE].reshape(shard, -1),
            query_part[..., NOPE:].reshape(shard, -1),
            jnp.zeros((shard, 128 - heads * ROPE), BF),
        ],
        axis=1,
    )
    expand_part = lax.dynamic_slice_in_dim(w_expand, seq_index * expand_width, expand_width, 1)
    expand_part = expand_part.reshape(-1, heads, NOPE + VDIM)
    expand_part = jnp.concatenate(
        [part.reshape(-1, heads * NOPE) for part in jnp.split(expand_part, 2, axis=-1)], axis=1
    )
    if fast:
        named_own = jnp.pad(named_own, ((0, 16 - named_own.shape[0]), (0, 0)))
        gains_size = gains_own.shape[0]
        gains_own = jnp.pad(gains_own, (0, 2048 - gains_size)).reshape(16, 128)
        (
            hidden_all, named_all, gains, query_weight, expand_weight, compress_weight,
            output_weight,
        ) = gather_start(
            hidden, named_own, gains_own, query_part, expand_part, w_compress, w_output, 1
        )
        gains = gains.reshape(n_dp, 2048)[:, :gains_size]
        dp_places = (dp_index - jnp.arange(n_dp)) % n_dp
        slot_of_seq = small_take([0, 1, 2, 4, 3, 5, 6, 7], seq_index ^ jnp.arange(n_seq))
        named_all = jnp.stack([named_all[k] for k in (0, 4, 1, 2, 5, 6, 3, 7)])
        positions_all = reorder(named_all[:, 0, 2 * TOP], slot_of_seq)
        named_all = named_all.swapaxes(0, 1).reshape(n_all, 16, rows)
    else:
        hidden_all = lax.all_gather(hidden, "seq", axis=0)
        named_all = lax.all_gather(named_own, both, axis=0)
        positions_all = lax.dynamic_slice_in_dim(named_all, dp_index * n_seq, n_seq, 0)[:, 2 * TOP]
        gains = lax.all_gather(gains_own, "dp", axis=0)
        query_weight = lax.all_gather(query_part, "dp", axis=0)
        expand_weight = lax.all_gather(expand_part, "dp", axis=0)
        compress_weight = lax.all_gather(w_compress, "dp", axis=0)
        output_weight = lax.all_gather(w_output, "dp", axis=0)
    hidden_all = hidden_all.reshape(length, features)
    query_weight = query_weight.reshape(features, query_width)
    expand_weight = expand_weight.reshape(LATENT, expand_width)
    compress_weight = compress_weight.reshape(features, LATENT + ROPE)
    gains = gains.astype(F32)
    first_gain = gains[:, :shard].reshape(features)
    second_gain = gains[:, shard : 2 * shard].reshape(features)
    latent_gain_row = gains[:, 2 * shard :].reshape(LATENT)
    output_weight = output_weight.reshape(HEADS * VDIM, features)
    shared_part = jnp.stack(
        [
            jnp.stack(
                [
                    lax.dynamic_slice_in_dim(
                        w_shared_in, half * SH_FF + (z * n_seq + seq_index) * units, units, 1
                    )
                    for half in range(2)
                ],
                axis=1,
            )
            for z in range(n_dp)
        ]
    )
    shared_in = lax.all_to_all(
        shared_part, "dp", split_axis=0, concat_axis=0, tiled=True
    ).reshape(features, 2, units)
    pad = padded_units - units
    shared_in = jnp.pad(shared_in, ((0, 0), (0, 0), (0, pad))).reshape(features, 2 * padded_units)
    shared_out = lax.dynamic_slice_in_dim(w_shared_out, seq_index * units, units, 0)
    shared_out = jnp.pad(shared_out, ((0, pad), (0, 0)))
    weight_in, weight_out = w_expert_in[0], w_expert_out[0]
    expert = (dp_index * n_seq + seq_index) // 2
    named = named_all[:, :TOP] == expert.astype(F32)
    chosen = jnp.any(named, axis=1)
    gate_rows = jnp.sum(jnp.where(named, named_all[:, TOP : 2 * TOP], 0.0), axis=1)[:, None]
    before = (jnp.arange(rows)[:, None] < jnp.arange(rows)[None, :]).astype(BF)
    place = dot(chosen.astype(BF), before).astype(jnp.int32)
    place = jnp.where(chosen, place, -1)[:, None]

    angles = rotary_angles(positions_all.reshape(length))
    angles = jnp.concatenate([angles] * 4, axis=1)
    cosine_all, sine_all = jnp.cos(angles), jnp.sin(angles)
    normed_all, queries, keys_all, values_all, latent, latent_normed = project(
        hidden_all, first_gain[None], query_weight, compress_weight, latent_gain_row[None],
        expand_weight, cosine_all, sine_all,
    )
    attended_heads, logs = attend(queries, keys_all, values_all)
    attended = lax.all_to_all(
        attended_heads, "seq", split_axis=0, concat_axis=1, tiled=True
    )
    hidden_float = hidden.astype(F32)
    middle = hidden_float + dot(attended, output_weight)
    second_scale = rms_scale(middle)
    moe_rows = (middle * second_scale * second_gain).astype(BF)

    sent = jnp.stack([moe_rows, upstream_rows])
    if not fast:
        sent = lax.all_gather(sent, both, axis=0)
    (
        sent_all, expert_in_grad, expert_out_grad, hidden_units, shared_units, back_parts,
        shared_in_grad, shared_out_grad,
    ) = experts(
        fast, capacity, sent, place, gate_rows, weight_in, weight_out, shared_in, shared_out
    )
    gate_grads, out_parts, moe_back = out_side(
        fast, capacity, back_parts, place, gate_rows, hidden_units, sent_all if fast else sent, shared_units,
        weight_out, shared_out,
    )
    if fast:
        gate_grads = reorder(gate_grads.reshape(n_dp, n_seq, rows), dp_places)
        gate_grads = reorder(gate_grads.swapaxes(0, 1), slot_of_seq).swapaxes(0, 1)
        gate_grads = gate_grads.reshape(n_all, 1, rows)
    else:
        moe_back = lax.psum_scatter(
            back_parts.reshape(n_all * rows, features), both, scatter_dimension=0, tiled=True
        )
    moe_back = moe_back.astype(F32)
    gate_grads = lax.all_to_all(gate_grads, both, split_axis=0, concat_axis=0, tiled=True)
    gate_grads = jnp.sum(gate_grads.reshape(expert_count, 2, rows), axis=1)
    gate_gradient = jnp.sum(
        jnp.where(
            id_rows[:, :, None] == jnp.arange(expert_count, dtype=jnp.int32),
            gate_grads.T[:, None, :],
            0.0,
        ),
        axis=-1,
    )
    second_gain_grad = jnp.sum(moe_back * middle * second_scale, axis=0)
    middle_back = upstream_float + norm_backward(moe_back, middle, second_scale, second_gain)
    middle_low = middle_back.astype(BF)
    attended_back = dot_nt(middle_low, output_weight).astype(BF)
    upstream_heads = lax.all_to_all(
        attended_back, "seq", split_axis=1, concat_axis=0, tiled=True
    )
    attended_all = lax.all_gather(tie(attended, middle_low), "seq", axis=0, tiled=True)
    middle_columns = lax.all_to_all(middle_low, "seq", split_axis=1, concat_axis=0, tiled=True)
    output_grad = dot_tn(attended_all, middle_columns)

    query_back, turned_back, key_back, rotary_sum, value_back, out_sum = attend_back(
        fast, queries, keys_all, values_all, upstream_heads, logs, cosine_all, sine_all, out_parts
    )
    if not fast:
        out_sum = lax.psum_scatter(
            out_parts.reshape(n_all * rows, features), both, scatter_dimension=0, tiled=True
        )
    block_out = (middle + out_sum.astype(F32)).astype(BF)
    turned_back = sum(turned_back[:, 128 * h : 128 * h + 128] for h in range(heads))
    query_raw_back = jnp.concatenate([query_back, turned_back], axis=1)
    expanded_back = jnp.concatenate([key_back, value_back], axis=1)
    partial_back = partial_terms(
        rows, query_back, turned_back, key_back, value_back, rotary_sum, query_weight, expand_weight
    )
    if fast:
        summed_back = plane_scatter(partial_back.reshape(n_seq, rows, -1), 5)
    else:
        summed_back = lax.psum_scatter(partial_back, "seq", scatter_dimension=0, tiled=True)
    summed_back = summed_back[:, : features + LATENT + ROPE].astype(F32)
    query_grad = dot_tn(normed_all, query_raw_back)
    expand_grad = dot_tn(latent_normed, expanded_back)
    latent_normed_back = summed_back[:, features : features + LATENT]
    own = seq_index * rows

    def mine(array):
        return lax.dynamic_slice_in_dim(array, own, rows, 0)

    latent_own = mine(latent)
    latent_scale_own = rms_scale(latent_own)
    latent_gain_grad = jnp.sum(latent_normed_back * latent_own * latent_scale_own, axis=0)
    latent_back = norm_backward(latent_normed_back, latent_own, latent_scale_own, latent_gain_row)
    half_turn = ROPE // 2
    rotary_back = rotate(
        summed_back[:, features + LATENT :],
        mine(cosine_all)[:, :half_turn],
        -mine(sine_all)[:, :half_turn],
    )
    compressed_back = jnp.concatenate([latent_back, rotary_back], axis=-1).astype(BF)
    width = (LATENT + ROPE) // n_seq
    if fast:
        compressed_back_all = plane_gather(jnp.pad(compressed_back, ((0, 0), (0, 64))), 6)
        compressed_back_all = compressed_back_all[:, :, : LATENT + ROPE]
    else:
        compressed_back_all = lax.all_gather(compressed_back, "seq", axis=0)
    compressed_back_all = compressed_back_all.reshape(length, LATENT + ROPE)
    compress_grad = dot_tn(
        normed_all, lax.dynamic_slice_in_dim(compressed_back_all, seq_index * width, width, 1)
    )
    normed_back = summed_back[:, :features] + dot_nt(compressed_back, compress_weight)
    first_scale = rms_scale(hidden_float)
    first_gain_grad = jnp.sum(normed_back * hidden_float * first_scale, axis=0)
    hidden_gradient = (
        middle_back + norm_backward(normed_back, hidden_float, first_scale, first_gain)
    ).astype(BF)

    gain_grads = jnp.concatenate([first_gain_grad, second_gain_grad, latent_gain_grad])
    bit = 1
    while bit < n_seq:
        gain_grads = gain_grads + lax.ppermute(
            gain_grads, "seq", [(i, i ^ bit) for i in range(n_seq)]
        )
        bit *= 2
    bit = 1
    while bit < n_dp:
        gain_grads = gain_grads + lax.ppermute(
            gain_grads, "dp", [(i, i ^ bit) for i in range(n_dp)]
        )
        bit *= 2
    latent_shard = LATENT // n_dp

    def gain_part(start, size):
        return lax.dynamic_slice_in_dim(gain_grads, start + dp_index * size, size, 0)

    widths = [query_width, expand_width * latent_shard // shard, features // n_seq, width]
    parts = jnp.concatenate(
        [
            query_grad.reshape(n_dp, shard, -1),
            expand_grad.reshape(n_dp, shard, -1),
            output_grad.reshape(n_dp, shard, -1),
            compress_grad.reshape(n_dp, shard, -1),
        ],
        axis=-1,
    )
    if fast:
        extra = -parts.shape[-1] % 128
        summed = sum_grads(jnp.pad(parts, ((0, 0), (0, 0), (0, extra))).astype(BF), 7)
    else:
        summed = lax.psum_scatter(parts, "dp", scatter_dimension=0)
        summed = lax.all_gather(summed.astype(BF), "seq", axis=0)

    def columns(start, size, height):
        found = summed[:, :, start : start + size].reshape(n_seq, height, -1)
        return found.transpose(1, 0, 2).reshape(height, -1).astype(F32)

    def in_heads(start, size, height, first, second):
        found = summed[:, :, start : start + size].reshape(n_seq, height, -1)
        cut = heads * first
        found = jnp.concatenate(
            [
                found[:, :, :cut].reshape(n_seq, height, heads, first),
                found[:, :, cut : cut + heads * second].reshape(n_seq, height, heads, second),
            ],
            axis=-1,
        )
        return found.transpose(1, 0, 2, 3).reshape(height, -1).astype(F32)

    starts = [sum(widths[:n]) for n in range(4)]
    shared_in_grad = shared_in_grad.reshape(2, padded_units, n_dp, shard)[:, :units].astype(BF)
    shared_in_out = lax.all_to_all(
        shared_in_grad.transpose(2, 3, 0, 1), "dp", split_axis=0, concat_axis=0, tiled=True
    )
    shared_in_out = lax.all_gather(shared_in_out, "seq", axis=0)
    shared_in_out = shared_in_out.transpose(2, 3, 1, 0, 4).reshape(shard, 2 * SH_FF).astype(F32)
    shared_out_out = lax.all_gather(
        shared_out_grad[:units].astype(BF), "seq", axis=0, tiled=True
    ).astype(F32)
    return (
        block_out.reshape(hidden_in.shape),
        hidden_gradient.reshape(hidden_in.shape),
        gate_gradient.reshape(gate_weights.shape),
        gain_part(0, shard),
        in_heads(starts[0], widths[0], shard, NOPE, ROPE),
        columns(starts[3], widths[3], shard),
        gain_part(2 * features, latent_shard),
        in_heads(starts[1], widths[1], latent_shard, NOPE, VDIM),
        columns(starts[2], widths[2], shard),
        gain_part(features, shard),
        shared_in_out,
        shared_out_out,
        expert_in_grad[None],
        expert_out_grad[None],
    )


def solution(mesh):
    token = P("dp", "seq", None)
    row = P("dp", None)
    half = P(("dp", "seq"), None, None)
    return jax.shard_map(
        on_device,
        mesh=mesh,
        in_specs=(
            token, P("dp", "seq"), token, token, P("dp"), row, row, P("dp"), row, row,
            P("dp"), row, row, half, half, token,
        ),
        out_specs=(
            token, token, token, P("dp"), row, row, P("dp"), row, row, P("dp"), row, row,
            half, half,
        ),
        check_vma=False,
    )
```

time: 1670 us -> 1360 us (0.81)
  matrix products: 168 us -> 28.3 us
  other arithmetic: 131 us -> 47.3 us
  local copies, waits for them, and re-layouts: 211 us -> 133 us
  waiting for transfers between devices: 7.06 us -> 44.6 us
  Pallas kernels: 1040 us -> 1020 us
    pallas_call x1, Pallas kernels: 171 us -> 99.3 us  [gather_start(): pl.pallas_call(gather_start_kernel, out_shape=[jax.ShapeDtypeStruct((8, *...]
    dot_general x6 -> x4, matrix products: 79.9 us -> 14.7 us  [dot_tn(): return jnp.einsum('ki,kj->ij', a, b, preferred_element_type=F32)]
    dot_general x24 -> x0, matrix products: 47.9 us -> none  [the longest x4 15.9 us: attention_forward(): jnp.einsum('hqk,khd->qhd', shares, values_all[:end], preferred_element_ty...]
    unnamed x270 -> x128, local copies, waits for them, and re-layouts: 102 us -> 68.3 us
    pallas_call x1, Pallas kernels: 340 us -> 367 us  [experts(): pl.pallas_call(functools.partial(experts_kernel, remote, capacity), grid=...]
    pallas_call x2 -> x6, Pallas kernels: 367 us -> 390 us  [the longest x1 180 us: out_side(): pl.pallas_call(functools.partial(out_kernel, remote, capacity), grid=(blo...]
    all_to_all x1, waiting for transfers between devices: 0.01 us -> 22.3 us  [on_device(): lax.all_to_all(attended_back, 'seq', split_axis=1, concat_axis=0, tiled=T...]
    dot_general x5 -> x2, matrix products: 25.7 us -> 6.43 us  [dot(): return jnp.dot(a, b, preferred_element_type=F32)]
  transfers between devices with their start and end apart: 14 -> 13, of which waited for: 3 -> 7; matrix products, arithmetic and copies ran while one was open for 29% -> 7% of each run, Pallas kernels for 63% -> 31%
where the time goes in v3:
time: 1360 us
  Pallas kernels  1020 us (75%)
  local copies, waits for them, and re-layouts  133 us (10%)
  other arithmetic  47.3 us (3%)
  waiting for transfers between devices  44.6 us (3%)
  between operations  38.6 us (3%)
  matrix products  28.3 us (2%)
  blocking collectives  25.1 us (2%)
  starting transfers between devices  20.4 us (1%)
    pallas_call x1, Pallas kernels, experts(): pl.pallas_call(functools.partial(experts_kernel, remote, capacity), grid=...  367 us
    pallas_call x1, Pallas kernels, out_side(): pl.pallas_call(functools.partial(out_kernel, remote, capacity), grid=(blo...  180 us
    pallas_call x1, Pallas kernels, attend_back(): pl.pallas_call(functools.partial(attend_back_kernel, remote), grid=(heads...  160 us
    pallas_call x1, Pallas kernels, gather_start(): pl.pallas_call(gather_start_kernel, out_shape=[jax.ShapeDtypeStruct((8, *...  99.3 us
    pallas_call x1, Pallas kernels, sum_grads(): pl.pallas_call(grads_kernel, out_shape=jax.ShapeDtypeStruct((8, rows, col...  95.5 us
    unnamed x128, local copies, waits for them, and re-layouts  68.3 us
    pallas_call x1, Pallas kernels, plane_scatter(): pl.pallas_call(plane_scatter_kernel, out_shape=jax.ShapeDtypeStruct((rows...  51.6 us
  transfers between devices with their start and end apart: 13, of which 7 were waited for; matrix products, arithmetic and copies ran while one was open for 7% of the time, Pallas kernels for 31%

profile of v3, /device:TPU:0, one launch (start us, length us, event | category | flops | bytes accessed | tf_op | source)
XLA Modules:
  0.0 1355.8 jit_solution(12609451891408324242)
XLA Ops:
  22.3 1.6 copy-done.12
  23.9 99.3 %shard_map.272 = (bf16[8,256,2048]{2,1,0:T(8,128)(2,1)S(1)}, f32[8,4,16,256]{3,2,1,0:T(8,128)S(1)}, bf16[4,16,128]{2,1,0:T(8,128)(2,1)S(1)}, bf16[4,512,384]{2,1...) custom-call(bf16[256,2048]{1,0:T(8,128)(2,1)S(1)} %bitcast.202, ...), custom_call_target="tpu_custom_call" | custom-call | bytes 67108864 | tf_op jit(solution)/shard_map/pallas_call | solution.py:457
  123.2 1.5 copy-done.9
  125.9 3.2 copy-done.24
  129.1 3.4 copy-done.25
  139.4 4.6 fusion.36
  144.1 20.2 %shard_map.273 = (bf16[2048,2048]{1,0:T(8,128)(2,1)}, bf16[2048,384]{1,0:T(8,128)(2,1)S(1)}, bf16[2048,384]{1,0:T(8,128)(2,1)}, bf16[2048,256]{1,0:T(8,128)(2,1)...) custom-call(bf16[2048,2048]{1,0:T(8,128)(2,1)} %bitcast.218, f32[1,2048]{1,0:T(1,128)S(1)} %bitcast.214, ...), custom_call_target="tpu_custom_call" | custom-call | flops 8589934592 | bytes 33554432 | tf_op jit(solution)/shard_map/pallas_call | solution.py:1173
  164.3 2.3 copy-done.4
  166.7 19.5 %shard_map.274 = (bf16[2048,256]{1,0:T(8,128)(2,1)}, f32[2,2048,128]{2,1,0:T(8,128)S(1)}) custom-call(bf16[2048,384]{1,0:T(8,128)(2,1)S(1)} %get-tuple-element.52.query_ref.turned_ref, bf16[2048,384]{1,0:T(8,128)(2,1)S(1)} %get-tuple-element.52.query_ref.turned_ref, bf16[2048,384]{1,0:T(8,128)(2,1)S(1)} %copy-done.4, bf16[2048,384]{1,0:T(8,128)(2,1)S(1)} %copy-done.4, ...), custom_call_target="tpu_custom_call" | custom-call | flops 3221225472 | bytes 8388608 | tf_op jit(solution)/shard_map/pallas_call | solution.py:1265
  186.2 1.3 copy-done.11
  187.5 3.6 all-to-all-start
  192.8 1.9 constant_dynamic-slice_fusion.20
  198.6 7.9 all-to-all-done
  206.4 3.8 all-to-all-start.1
  210.5 6.3 multiply_reduce_fusion
  218.8 1.5 pad_maximum_fusion.rows_in
  220.3 5.7 all-to-all-done.1
  227.5 367.1 %shard_map.275 = (bf16[32,2,256,2048]{3,2,1,0:T(8,128)(2,1)}, f32[2048,1408]{1,0:T(8,128)}, f32[704,2048]{1,0:T(8,128)}, bf16[5120,768]{1,0:T(8,128)(2,1)}, bf16...) custom-call(bf16[2,256,2048]{2,1,0:T(8,128)(2,1)} %pad_maximum_fusion.rows_in, ...), custom_call_target="tpu_custom_call" | custom-call | flops 96636764160 | bytes 134217728 | tf_op jit(solution)/shard_map/pallas_call | solution.py:839
  594.7 1.9 slice.253
  596.7 1.7 convert.51
  599.6 25.1 %all_to_all.72 = bf16[4,512,2,88]{1,3,2,0:T(8,128)(2,1)} all-to-all(bf16[4,512,2,88]{1,3,2,0:T(8,128)(2,1)S(1)} %bitcast.239), channel_id=1, replica_groups=mesh['dp'=4,'seq'=8] {'dp'}, dimensions={0} | all-to-all | bytes 1441792 | tf_op jit(solution)/shard_map/all_to_all | solution.py:1755
  625.0 180.5 %shard_map.276 = (f32[32,1,256]{2,1,0:T(1,128)}, bf16[32,256,2048]{2,1,0:T(8,128)(2,1)}, bf16[256,2048]{1,0:T(8,128)(2,1)}) custom-call(bf16[32,256,2048]{2,1,0:T(8,128)(2,1)} %get-tuple-element.57.back_ref, s32[32,1,256]{2,1,0:T(1,128)} %broadcast_in_dim.61.place_ref.refs_0_, f32[32,1,256]{2,1,0:T(1,128)} %broadcast_in_dim.63.gate_ref.refs_1_, ...), custom_call_target="tpu_custom_call" | custom-call | flops 26843545600 | bytes 54525952 | tf_op jit(solution)/shard_map/pallas_call | solution.py:1088
  805.6 2.0 fusion.13
  819.1 2.5 all-to-all-start.3
  821.6 5.7 convolution_convert_fusion.1
  828.9 4.3 all-to-all-start.2
  836.6 22.3 %all-to-all-done.2 = bf16[256,8,256]{2,0,1:T(8,128)(2,1)} async-done(((bf16[256,8,256]{2,0,1:T(8,128)(2,1)}), bf16[256,8,256]{2,0,1:T(8,128)(2,1)}, u32[]{:S(2)}, u32[]{:S(2)}) %all-to-all-start.2) | async-done | bytes 1048608 | tf_op jit(solution)/shard_map/all_to_all | solution.py:1640
  858.9 4.7 all-to-all-start.4
  863.6 160.2 %shard_map.277 = (bf16[2048,256]{1,0:T(8,128)(2,1)}, bf16[2048,256]{1,0:T(8,128)(2,1)}, bf16[2048,256]{1,0:T(8,128)(2,1)}, f32[2048,128]{1,0:T(8,128)}, bf16[204...) custom-call(bf16[2048,384]{1,0:T(8,128)(2,1)} %copy-done.3, bf16[2048,384]{1,0:T(8,128)(2,1)} %copy-done.3, ...), custom_call_target="tpu_custom_call" | custom-call | flops 8589934592 | bytes 67108864 | tf_op jit(solution)/shard_map/pallas_call | solution.py:1360
  1023.8 1.4 slice_add_fusion.turned_ref
  1030.5 8.5 shard_map.278
  1039.0 4.1 copy-done
  1043.1 51.6 %shard_map.279 = bf16[256,2688]{1,0:T(8,128)(2,1)S(1)} custom-call(bf16[8,256,2688]{2,1,0:T(8,128)(2,1)S(1)} %bitcast.201), custom_call_target="tpu_custom_call" | custom-call | flops 5505024 | bytes 11010048 | tf_op jit(solution)/shard_map/pallas_call | solution.py:928
  1095.4 1.5 multiply_reduce_fusion.1
  1099.3 1.4 fusion.21
  1100.9 5.6 convolution_convert_fusion
  1107.1 3.3 collective-permute-done.1
  1110.9 2.4 fusion.35
  1113.3 15.4 %shard_map.281 = bf16[8,256,640]{2,1,0:T(8,128)(2,1)S(1)} custom-call(bf16[256,640]{1,0:T(8,128)(2,1)S(1)} %pad.29.in_ref), custom_call_target="tpu_custom_call" | custom-call | bytes 5242880 | tf_op jit(solution)/shard_map/pallas_call | solution.py:965
  1128.9 1.7 convolution_convert_fusion.2
  1130.6 2.1 collective-permute-done.3
  1134.5 2.8 collective-permute-done.4
  1138.6 5.1 convert_element_type.149
  1143.7 8.7 convert_bitcast_fusion
  1152.3 10.5 copy.206
  1162.8 11.9 copy.210
  1174.8 12.2 copy.214
  1187.0 6.1 convolution_convert_fusion.3
  1193.6 95.5 %shard_map.282 = bf16[8,512,896]{2,1,0:T(8,128)(2,1)S(1)} custom-call(bf16[4,512,896]{2,1,0:T(8,128)(2,1)S(1)} %fusion.6.in_ref), custom_call_target="tpu_custom_call" | custom-call | bytes 14680064 | tf_op jit(solution)/shard_map/pallas_call | solution.py:1013
  1289.1 1.9 fusion.68
  1290.9 2.5 convert_bitcast_fusion.1
  1293.4 1.5 convert_bitcast_fusion.3
  1294.9 1.7 reshape.287
  1300.0 2.8 convert_bitcast_fusion.2
  1302.8 4.1 reshape.294
  1306.9 2.4 copy.216
  1309.2 1.6 copy.199
  1311.1 3.6 maximum_convert_fusion
  1314.7 6.6 copy.208
  1321.3 5.3 copy.204
  1326.6 5.5 copy.209
  1332.1 1.6 copy.201
  1333.7 9.4 copy.260
  1343.2 5.9 copy.261
  (230 shorter events, 43.5 us)
Async XLA Ops:
  7.2 1.4 copy-start.49
  7.2 14.1 %copy-start.44 = (s32[1,256,6]{1,0,2:T(1,128)S(1)}, s32[1,256,6]{1,0,2:T(1,128)}, u32[]{:S(2)}) copy-start(s32[1,256,6]{1,0,2:T(1,128)} %param.19) | copy-start | bytes 18436
  7.2 14.6 %copy-start.43 = (f32[1,256,6]{1,0,2:T(1,128)S(1)}, f32[1,256,6]{1,0,2:T(1,128)}, u32[]{:S(2)}) copy-start(f32[1,256,6]{1,0,2:T(1,128)} %param.20) | copy-start | bytes 18436
  7.2 14.6 %copy-start.45 = (s32[1,256]{1,0:T(1,128)S(1)}, s32[1,256]{1,0:T(1,128)}, u32[]{:S(2)}) copy-start(s32[1,256]{1,0:T(1,128)} %param.18) | copy-start | bytes 3076
  7.2 14.6 %copy-start.38 = (bf16[512,576]{0,1:T(8,128)(2,1)S(1)}, bf16[512,576]{0,1:T(8,128)(2,1)}, u32[]{:S(2)}) copy-start(bf16[512,576]{0,1:T(8,128)(2,1)} %param.23) | copy-start | bytes 1769476
  19.8 2.5 copy-start.46
  19.8 2.5 copy-start.47
  19.8 2.5 copy-start.48
  19.8 2.5 copy-start.1
  22.3 1.6 copy-start.12
  123.2 1.5 copy-start.9
  125.9 3.2 copy-start.24
  129.1 3.4 copy-start.25
  132.5 11.6 copy-start.22
  144.0 20.3 %copy-start.5 = (f32[2048,128]{1,0:T(8,128)}, f32[2048,128]{1,0:T(8,128)S(1)}, u32[]{:S(2)}) copy-start(f32[2048,128]{1,0:T(8,128)S(1)} %get-tuple-element.174.sine_ref) | copy-start | bytes 3145732
  144.0 20.3 %copy-start.6 = (f32[2048,128]{1,0:T(8,128)}, f32[2048,128]{1,0:T(8,128)S(1)}, u32[]{:S(2)}) copy-start(f32[2048,128]{1,0:T(8,128)S(1)} %get-tuple-element.175.cosine_ref) | copy-start | bytes 3145732
  164.3 21.9 %copy-start.3 = (bf16[2048,384]{1,0:T(8,128)(2,1)}, bf16[2048,384]{1,0:T(8,128)(2,1)S(1)}, u32[]{:S(2)}) copy-start(bf16[2048,384]{1,0:T(8,128)(2,1)S(1)} %get-tuple-element.52.query_ref.turned_ref) | copy-start | bytes 4718596
  164.3 21.9 %copy-start.15 = (bf16[2048,256]{1,0:T(8,128)(2,1)}, bf16[2048,256]{1,0:T(8,128)(2,1)S(1)}, u32[]{:S(2)}) copy-start(bf16[2048,256]{1,0:T(8,128)(2,1)S(1)} %get-tuple-element.54.value_ref) | copy-start | bytes 3145732
  164.3 2.4 copy-start.4
  186.2 1.3 copy-start.11
  187.5 18.9 %all-to-all-start = ((bf16[8,256,256]{2,1,0:T(8,128)(2,1)}), bf16[8,256,256]{2,1,0:T(8,128)(2,1)S(1)}, u32[]{:S(2)}, u32[]{:S(2)}) async-start(bf16[8,256,256]{2,1,0:T(8,128)(2,1)} %bitcast.28), calls=%async_computation | async-start | bytes 2097152 | tf_op jit(solution)/shard_map/all_to_all | solution.py:1596
  206.4 19.6 %all-to-all-start.1 = ((bf16[4,512,2,88]{1,3,2,0:T(8,128)(2,1)}), bf16[4,512,2,88]{1,3,2,0:T(8,128)(2,1)S(1)}, u32[]{:S(2)}, u32[]{:S(2)}) async-start(bf16[4,512,2,88]{1,3,2,0:T(8,128)(2,1)} %pad_maximum_fusion.3), calls=%async_computation.1 | async-start | bytes 1441792 | tf_op jit(solution)/shard_map/all_to_all | solution.py:1572
  210.2 928.4 %all-gather.7.cloned.1.call-start = ((), (), s32[]{:S(2)}) async-start(), calls=%async_computation.7 | async-start | bytes 3244032 | tf_op jit(solution)/shard_map/all_gather | solution.py:1760
  210.5 6.3 copy-start.7
  216.8 1.3 copy-start.26
  216.8 2.0 copy-start.29
  596.6 547.1 %all-gather.9.cloned.1.call-start = ((), (), s32[]{:S(2)}) async-start(), calls=%async_computation.8 | async-start | bytes 6488064 | tf_op jit(solution)/shard_map/all_gather | solution.py:1758
  624.8 550.0 %all-gather.5.cloned.1.call-start = ((), (), s32[]{:S(2)}) async-start(), calls=%async_computation.6 | async-start | bytes 9437184 | tf_op jit(solution)/shard_map/all_gather | solution.py:1643
  625.0 180.5 %copy-start.27 = (f32[256,2048]{1,0:T(8,128)S(1)}, f32[256,2048]{1,0:T(8,128)}, u32[]{:S(2)}) copy-start(f32[256,2048]{1,0:T(8,128)} %copy-done.26) | copy-start | bytes 6291460
  805.5 2.1 copy-start.30
  805.5 2.1 copy-start.32
  807.6 1.2 copy-start.8
  808.8 9.5 copy-start.40
  819.1 9.8 all-to-all-start.3
  827.4 5.8 copy-start.39
  827.4 6.9 copy-start.2
  828.9 30.0 %all-to-all-start.2 = ((bf16[256,8,256]{2,0,1:T(8,128)(2,1)}), bf16[256,8,256]{2,0,1:T(8,128)(2,1)}, u32[]{:S(2)}, u32[]{:S(2)}) async-start(bf16[256,8,256]{2,0,1:T(8,128)(2,1)} %bitcast.233), calls=%async_computation.2 | async-start | bytes 2097152 | tf_op jit(solution)/shard_map/all_to_all | solution.py:1640
  833.1 2.8 copy-start.41
  858.9 328.1 %all-to-all-start.4 = ((bf16[256,8,256]{2,0,1:T(8,128)(2,1)}), bf16[256,8,256]{2,0,1:T(8,128)(2,1)}, u32[]{:S(2)}, u32[]{:S(2)}) async-start(bf16[256,8,256]{2,0,1:T(8,128)(2,1)} %bitcast.232), calls=%async_computation.4 | async-start | bytes 2097152 | tf_op jit(solution)/shard_map/all_to_all | solution.py:1644
  863.6 161.6 %copy-start.23 = (bf16[4,128,512]{2,1,0:T(8,128)(2,1)S(1)}, bf16[4,128,512]{2,1,0:T(8,128)(2,1)}, u32[]{:S(2)}) copy-start(bf16[4,128,512]{2,1,0:T(8,128)(2,1)} %copy-done.22) | copy-start | bytes 1572868
  1023.8 1.7 copy-start.14
  1025.5 1.2 copy-start.16
  1026.8 1.2 copy-start.18
  1028.0 1.2 copy-start.19
  1029.2 1.2 copy-start.21
  1030.5 70.4 %slice-start = ((s8[8388608]{0:T(1024)(128)(4,1)}), s8[4194304]{0:T(1024)(128)(4,1)S(1)}, s32[]{:S(2)}) async-start(s8[8388608]{0:T(1024)(128)(4,1)} %bitcast.222), calls=%async_computation.9 | async-start | bytes 8388608
  1039.0 4.1 copy-start
  1043.1 57.7 %slice-start.1 = ((s8[8388608]{0:T(1024)(128)(4,1)}), s8[4194304]{0:T(1024)(128)(4,1)S(1)}, s32[]{:S(2)}) async-start(s8[8388608]{0:T(1024)(128)(4,1)} %bitcast.222), calls=%async_computation.10 | async-start | bytes 8388608
  1094.9 4.4 copy-start.10
  1099.3 1.5 copy-start.20
  1100.7 5.8 collective-permute-start
  1100.9 10.0 copy-start.28
  1100.9 10.0 copy-start.31
  1100.9 10.0 copy-start.33
  1100.9 10.0 copy-start.37
  1106.5 3.8 collective-permute-start.1
  1110.4 18.3 %collective-permute-start.2 = (f32[4608]{0:T(1024)S(1)}, f32[4608]{0:T(1024)S(1)}, u32[]{:S(2)}, u32[]{:S(2)}) collective-permute-start(f32[4608]{0:T(1024)S(1)} %add.274), channel_id=1, source_target_pairs={{0,4},{1,5},{2,6},{3,7},{4,0},{5,1},{6,2},{7,3},{8,12},{9,13},{10,... | collective-permute-start | bytes 55304 | tf_op jit(solution)/shard_map/ppermute | solution.py:1705
  1128.8 3.9 collective-permute-start.3
  1128.8 3.8 copy-start.17
  1128.9 3.8 copy-start.50
  1132.6 4.7 collective-permute-start.4
  1187.0 6.1 copy-start.36
  1309.2 1.9 copy-start.35
  1326.6 5.5 copy-start.34
  (2 other events, 1.9 us)
Sparse Core Ops, SparseCore 0:
  596.7 33.6 all-gather.6
  632.3 68.0 all-gather.8
  810.0 66.6 all-gather.4

commit v4 on v3

--- a/solution.py
+++ b/solution.py
@@ -234,8 +234,8 @@
             for k in range(4)
         ]
 
-    def begin(self):
-        greet((self.core, self.across_x, self.across_y, self.following, self.previous))
+    def begin(self, *others):
+        greet((self.core, self.across_x, self.across_y, self.following, self.previous, *others))
         for i in SCATTER_ORDER:
             for k in (3, 1, 2, 0):
                 self.to_core(i, k).start()
@@ -1054,12 +1054,34 @@
     gate_grad_ref[0] = jnp.sum(jnp.where(chosen, slot_grad, 0.0), axis=0, keepdims=True)
 
 
-def out_kernel(remote, capacity, back_ref, *refs):
+def out_kernel(remote, capacity, back_ref, shared_ref, *refs):
     step = pl.program_id(0)
-    terms, sum_ref, scratch = refs[:9], refs[9], refs[10:]
+    terms, sum_ref, dealt_ref, scratch = refs[:9], refs[9], refs[10], refs[11:]
     if remote:
+        *scratch, send_sems, recv_sems, own_sem = scratch
         scatter = ScatterAll(back_ref, *scratch)
-        pl.when(step == 0)(scatter.begin)
+        dp = lax.axis_index("dp")
+        seq = lax.axis_index("seq")
+        own = pltpu.make_async_copy(shared_ref.at[dp], dealt_ref.at[dp], own_sem)
+
+        def deal(r):
+            at = (dp + r) % 4
+            return pltpu.make_async_remote_copy(
+                src_ref=shared_ref.at[at],
+                dst_ref=dealt_ref.at[dp],
+                send_sem=send_sems.at[r - 1],
+                recv_sem=recv_sems.at[r - 1],
+                device_id={"dp": at, "seq": seq},
+                device_id_type=MESH_ID,
+            )
+
+        @pl.when(step == 0)
+        def _():
+            scatter.begin({"dp": (dp + 2) % 4, "seq": seq})
+            own.start()
+            for r in range(1, 4):
+                deal(r).start()
+
     out_terms(capacity, *terms)
     if remote:
         events = scatter.events()
@@ -1072,9 +1094,12 @@
                         event()
                 if at == OUT_EVENTS[-1]:
                     scatter.finish(sum_ref)
-
-
-def out_side(remote, capacity, back_parts, places, gates, hidden, sent, units, weight_out, shared_out):
+                    own.wait()
+                    for r in range(1, 4):
+                        deal(r).wait()
+
+
+def out_side(remote, capacity, back_parts, shared_grad, places, gates, hidden, sent, units, weight_out, shared_out):
     blocks, _, rows = places.shape
     features = sent.shape[-1]
     one = pl.BlockSpec((1, 1, rows), lambda j: (j, 0, 0))
@@ -1089,6 +1114,7 @@
         functools.partial(out_kernel, remote, capacity),
         grid=(blocks,),
         in_specs=[
+            pl.BlockSpec(memory_space=pl.ANY),
             pl.BlockSpec(memory_space=pl.ANY),
             one,
             one,
@@ -1102,13 +1128,22 @@
             one,
             pl.BlockSpec((1, rows, features), lambda j: (j, 0, 0)),
             pl.BlockSpec((rows, features), lambda j: (0, 0)),
+            pl.BlockSpec(memory_space=pl.ANY),
         ],
         out_shape=[
             jax.ShapeDtypeStruct((blocks, 1, rows), F32),
             jax.ShapeDtypeStruct((blocks, rows, features), BF),
             jax.ShapeDtypeStruct((rows, features), BF),
-        ],
-        scratch_shapes=ScatterAll.scratch(rows, features, BF) if remote else [],
+            jax.ShapeDtypeStruct(shared_grad.shape, BF),
+        ],
+        scratch_shapes=ScatterAll.scratch(rows, features, BF)
+        + [
+            pltpu.SemaphoreType.DMA((3,)),
+            pltpu.SemaphoreType.DMA((3,)),
+            pltpu.SemaphoreType.DMA,
+        ]
+        if remote
+        else [],
         compiler_params=pltpu.CompilerParams(
             vmem_limit_bytes=60 * 2**20,
             dimension_semantics=("arbitrary",),
@@ -1119,7 +1154,7 @@
             bytes_accessed=blocks * features * 2 * (rows + capacity),
             transcendentals=0,
         ),
-    )(back_parts, places, gates, hidden, sent, units, weight_out, shared_out)
+    )(back_parts, shared_grad, places, gates, hidden, sent, units, weight_out, shared_out)
 
 
 def swap_halves(values):
@@ -1456,6 +1491,313 @@
         compiler_params=pltpu.CompilerParams(vmem_limit_bytes=16 * 2**20),
         cost_estimate=pl.CostEstimate(flops=0, bytes_accessed=4 * array.size, transcendentals=0),
     )(array, other)
+
+
+def tail_scatter_kernel(
+    in_ref, columns_ref, latents_ref, out_ref, columns_out, latents_out, held, far, near, stage,
+    columns_total, columns_ring, latents_total, latents_ring, send_sems, recv_sems, local_sems
+):
+    core, across_x, across_y, following, previous = neighbours()
+    greet((core, across_x, across_y, following, previous))
+    dp = lax.axis_index("dp")
+    seq = lax.axis_index("seq")
+    rows = out_ref.shape[0]
+    top, bottom = pl.ds(0, rows // 2), pl.ds(rows // 2, rows // 2)
+    post = Courier(send_sems, recv_sems)
+    x_seq = seq + 2 - 4 * ((seq // 2) % 2)
+    y_seq = seq + 4 - 8 * (seq // 4)
+    xy_seq = x_seq + 4 - 8 * (seq // 4)
+    core_step = 1 - 2 * (seq % 2)
+    sums = (
+        (columns_ref, columns_total, columns_ring, columns_out),
+        (latents_ref, latents_total, latents_ring, latents_out),
+    )
+    ring_loads = {}
+    for n, i in enumerate(SCATTER_ORDER):
+        for m, (source, total, _, _) in enumerate(sums):
+            load = pltpu.make_async_copy(
+                source.at[(dp + 4 - i) % 4], total.at[n], local_sems.at[4 + 2 * n + m]
+            )
+            load.start()
+            ring_loads[n, m] = load
+    loads, arriving, hops = {}, {}, {}
+    for k, place in ((3, xy_seq), (1, x_seq), (2, y_seq), (0, seq)):
+        arriving[k] = post.send(in_ref.at[place + core_step], held.at[k], core)
+        loads[k] = pltpu.make_async_copy(in_ref.at[place], stage.at[k], local_sems.at[k])
+        loads[k].start()
+
+    def ring_step(n):
+        for m, (_, total, ring, out) in enumerate(sums):
+            ring_loads[n, m].wait()
+            if n > 0:
+                post.take(hops[n - 1, m])
+                accumulate(total.at[n], ring.at[n - 1])
+            if n < 3:
+                hops[n, m] = post.send(total.at[n], ring.at[n], following)
+            else:
+                out[...] = total[3]
+
+    def join(k):
+        loads[k].wait()
+        post.take(arriving[k])
+        accumulate(held.at[k], stage.at[k])
+
+    ring_step(0)
+    join(3)
+    far_top = post.send(held.at[3, top], far.at[0], across_y)
+    far_bottom = post.send(held.at[3, bottom], far.at[1], across_x)
+    join(1)
+    x_bottom = post.send(held.at[1, bottom], near.at[0, bottom], across_x)
+    join(2)
+    y_top = post.send(held.at[2, top], near.at[1, top], across_y)
+    join(0)
+    post.take(far_top)
+    accumulate(held.at[1, top], far.at[0])
+    x_top = post.send(held.at[1, top], near.at[0, top], across_x)
+    post.take(far_bottom)
+    accumulate(held.at[2, bottom], far.at[1])
+    y_bottom = post.send(held.at[2, bottom], near.at[1, bottom], across_y)
+    ring_step(1)
+    ring_step(2)
+    for copy in (x_bottom, y_top, x_top, y_bottom):
+        post.take(copy)
+    accumulate(held.at[0], near.at[0], near.at[1])
+    out_ref[...] = held[0]
+    ring_step(3)
+    post.finish()
+
+
+def tail_scatter(parts, columns, latents, collective_id):
+    _, rows, width = parts.shape
+    anywhere = pl.BlockSpec(memory_space=pl.ANY)
+    here = pl.BlockSpec(memory_space=pltpu.VMEM)
+    return pl.pallas_call(
+        tail_scatter_kernel,
+        out_shape=[
+            jax.ShapeDtypeStruct((rows, width), BF),
+            jax.ShapeDtypeStruct(columns.shape[1:], BF),
+            jax.ShapeDtypeStruct(latents.shape[1:], BF),
+        ],
+        in_specs=[anywhere] * 3,
+        out_specs=[here] * 3,
+        scratch_shapes=[
+            pltpu.VMEM((4, rows, width), BF),
+            pltpu.VMEM((2, rows // 2, width), BF),
+            pltpu.VMEM((2, rows, width), BF),
+            pltpu.VMEM((4, rows, width), BF),
+            pltpu.VMEM(columns.shape, BF),
+            pltpu.VMEM((3, *columns.shape[1:]), BF),
+            pltpu.VMEM(latents.shape, BF),
+            pltpu.VMEM((3, *latents.shape[1:]), BF),
+            pltpu.SemaphoreType.DMA((16,)),
+            pltpu.SemaphoreType.DMA((16,)),
+            pltpu.SemaphoreType.DMA((12,)),
+        ],
+        compiler_params=pltpu.CompilerParams(
+            collective_id=collective_id, has_side_effects=True, vmem_limit_bytes=48 * 2**20
+        ),
+        cost_estimate=pl.CostEstimate(flops=0, bytes_accessed=2**25, transcendentals=0),
+    )(parts, columns, latents)
+
+
+def tail_gather_kernel(*refs):
+    sources, found = refs[:3], refs[3:6]
+    send_sems, recv_sems, local_sems = refs[6:]
+    core, across_x, across_y, _, _ = neighbours()
+    greet((core, across_x, across_y))
+    seq = lax.axis_index("seq")
+    post = Courier(send_sems, recv_sems)
+    owns = []
+    for n in range(3):
+        own = pltpu.make_async_copy(sources[n], found[n].at[seq], local_sems.at[n])
+        own.start()
+        owns.append(own)
+    spreads = [
+        spread(post, sources[n], blocks_of(found[n]), core, across_x, across_y) for n in range(3)
+    ]
+    for _ in range(3):
+        advance(*spreads)
+    for own in owns:
+        own.wait()
+    post.finish()
+
+
+def tail_gather(blocks, collective_id):
+    anywhere = pl.BlockSpec(memory_space=pl.ANY)
+    return pl.pallas_call(
+        tail_gather_kernel,
+        out_shape=[jax.ShapeDtypeStruct((8, *b.shape), b.dtype) for b in blocks],
+        in_specs=[anywhere] * 3,
+        out_specs=[anywhere] * 3,
+        scratch_shapes=[
+            pltpu.SemaphoreType.DMA((24,)),
+            pltpu.SemaphoreType.DMA((24,)),
+            pltpu.SemaphoreType.DMA((3,)),
+        ],
+        compiler_params=pltpu.CompilerParams(
+            collective_id=collective_id, has_side_effects=True, vmem_limit_bytes=16 * 2**20
+        ),
+        cost_estimate=pl.CostEstimate(flops=0, bytes_accessed=2**24, transcendentals=0),
+    )(*blocks)
+
+
+def chosen_columns(source, target):
+    return jnp.where(source == target, 1.0, 0.0).astype(BF)
+
+
+def layout_kernel(width, columns_ref, latents_ref, small_ref, query_out, expand_out, output_out, small_out):
+    step = pl.program_id(0)
+    query = columns_ref[0, :, : 3 * 128]
+    row = lax.broadcasted_iota(jnp.int32, (3 * 128, 3 * 128), 0)
+    column = lax.broadcasted_iota(jnp.int32, (3 * 128, 3 * 128), 1)
+    head = jnp.where(column < QK, 0, 1)
+    entry = column - QK * head
+    source = jnp.where(entry < NOPE, NOPE * head + entry, 2 * NOPE + ROPE * head + entry - NOPE)
+    query_out[...] = dot(query, chosen_columns(row, source))
+    for part, place in enumerate((0, 2, 1, 3)):
+        expand_out[:, 128 * place : 128 * place + 128] = latents_ref[
+            0, :, 128 * part : 128 * part + 128
+        ].astype(F32)
+    output_out[...] = columns_ref[0, :, 3 * 128 :].astype(F32)
+    row = lax.broadcasted_iota(jnp.int32, (128, small_out.shape[1]), 0)
+    column = lax.broadcasted_iota(jnp.int32, (128, small_out.shape[1]), 1)
+    place = jnp.where(row < width, row + width * step, -1)
+    small = dot(small_ref[0], chosen_columns(place, column))
+
+    @pl.when(step == 0)
+    def _():
+        small_out[...] = small
+
+    @pl.when(step > 0)
+    def _():
+        small_out[...] += small
+
+
+def layout_grads(columns, latents, small, width):
+    count, shard, _ = columns.shape
+    latent_shard = latents.shape[1]
+
+    def given(array):
+        return pl.BlockSpec((1, *array.shape[1:]), lambda j: (j, 0, 0))
+
+    def made(rows, size):
+        return pl.BlockSpec((rows, size), lambda j: (0, j))
+
+    return pl.pallas_call(
+        functools.partial(layout_kernel, width),
+        grid=(count,),
+        in_specs=[given(columns), given(latents), given(small)],
+        out_specs=[
+            made(shard, 384), made(latent_shard, 512), made(shard, 256),
+            pl.BlockSpec((shard, count * width), lambda j: (0, 0)),
+        ],
+        out_shape=[
+            jax.ShapeDtypeStruct((shard, count * 384), F32),
+            jax.ShapeDtypeStruct((latent_shard, count * 512), F32),
+            jax.ShapeDtypeStruct((shard, count * 256), F32),
+            jax.ShapeDtypeStruct((shard, count * width), F32),
+        ],
+        compiler_params=params(32),
+        cost_estimate=pl.CostEstimate(
+            flops=2 * count * shard * 384 * 384, bytes_accessed=2**25, transcendentals=0
+        ),
+    )(columns, latents, small)
+
+
+def shared_layout_kernel(units, in_ref, out_ref):
+    n_seq, n_dp, both, _ = in_ref.shape
+    row = lax.broadcasted_iota(jnp.int32, (both, 128), 0) - units * pl.program_id(1)
+    column = lax.broadcasted_iota(jnp.int32, (both, 128), 1)
+    inside = (row >= 0) & (row < units)
+    for t in range(out_ref.shape[1] // 128):
+        start = 128 * t
+        total = None
+        for device in range(start // units, min((start + 127) // units, n_seq * n_dp - 1) + 1):
+            place = jnp.where(inside, row + (device * units - start), -1)
+            piece = dot_tn(in_ref[device % n_seq, device // n_seq], chosen_columns(place, column))
+            total = piece if total is None else total + piece
+        out_ref[:, start : start + 128] = total
+
+
+def shared_layout(found, units):
+    n_seq, n_dp, both, shard = found.shape
+    rows = min(256, shard)
+    return pl.pallas_call(
+        functools.partial(shared_layout_kernel, units),
+        grid=(shard // rows, 2),
+        in_specs=[pl.BlockSpec((n_seq, n_dp, both, rows), lambda r, g: (0, 0, 0, r))],
+        out_specs=pl.BlockSpec((rows, SH_FF), lambda r, g: (r, g)),
+        out_shape=jax.ShapeDtypeStruct((shard, 2 * SH_FF), F32),
+        compiler_params=pltpu.CompilerParams(
+            vmem_limit_bytes=60 * 2**20, dimension_semantics=("arbitrary", "arbitrary")
+        ),
+        cost_estimate=pl.CostEstimate(
+            flops=2**32, bytes_accessed=2 * found.size + 8 * shard * SH_FF, transcendentals=0
+        ),
+    )(found)
+
+
+def outer_kernel(left_ref, right_ref, out_ref):
+    out_ref[...] = dot_tn(left_ref[0], right_ref[...]).astype(BF)
+
+
+def outer(left, right, size):
+    parts, tokens, columns = left.shape
+    features = parts * columns
+    last = right.shape[1] // size - 1
+    return pl.pallas_call(
+        outer_kernel,
+        grid=(parts,),
+        in_specs=[
+            pl.BlockSpec((1, tokens, columns), lambda j: (j, 0, 0)),
+            pl.BlockSpec((tokens, size), lambda j: (0, last)),
+        ],
+        out_specs=pl.BlockSpec((columns, size), lambda j: (j, 0)),
+        out_shape=jax.ShapeDtypeStruct((features, size), BF),
+        compiler_params=params(32),
+        cost_estimate=pl.CostEstimate(
+            flops=2 * tokens * features * size, bytes_accessed=2 * tokens * features, transcendentals=0
+        ),
+    )(left, right)
+
+
+def exchange_kernel(in_ref, out_ref, send_sems, recv_sems, local_sem):
+    dp = lax.axis_index("dp")
+    seq = lax.axis_index("seq")
+    width = in_ref.shape[1] // 8
+
+    def columns(j):
+        return in_ref.at[:, pl.ds(pl.multiple_of(j * width, width), width)]
+
+    others = [(seq + r) % 8 for r in range(1, 8)]
+    greet([{"dp": dp, "seq": other} for other in others])
+    own = pltpu.make_async_copy(columns(seq), out_ref.at[seq], local_sem)
+    own.start()
+    post = Courier(send_sems, recv_sems)
+    for other in others:
+        post.send(columns(other), out_ref.at[seq], {"dp": dp, "seq": other})
+    own.wait()
+    post.finish()
+
+
+def exchange(array, collective_id):
+    rows, columns = array.shape
+    anywhere = pl.BlockSpec(memory_space=pl.ANY)
+    return pl.pallas_call(
+        exchange_kernel,
+        out_shape=jax.ShapeDtypeStruct((8, rows, columns // 8), array.dtype),
+        in_specs=[anywhere],
+        out_specs=anywhere,
+        scratch_shapes=[
+            pltpu.SemaphoreType.DMA((7,)),
+            pltpu.SemaphoreType.DMA((7,)),
+            pltpu.SemaphoreType.DMA,
+        ],
+        compiler_params=pltpu.CompilerParams(
+            collective_id=collective_id, has_side_effects=True, vmem_limit_bytes=16 * 2**20
+        ),
+        cost_estimate=pl.CostEstimate(flops=0, bytes_accessed=4 * array.size, transcendentals=0),
+    )(array).reshape(8 * rows, columns // 8)
 
 
 def on_device(
@@ -1593,9 +1935,15 @@
         expand_weight, cosine_all, sine_all,
     )
     attended_heads, logs = attend(queries, keys_all, values_all)
-    attended = lax.all_to_all(
-        attended_heads, "seq", split_axis=0, concat_axis=1, tiled=True
-    )
+    if fast:
+        attended_all = plane_gather(attended_heads, 9)
+        attended = lax.dynamic_slice_in_dim(attended_all, seq_index * rows, rows, 1)
+        attended = attended.swapaxes(0, 1).reshape(rows, HEADS * VDIM)
+    else:
+        attended_all = lax.all_gather(attended_heads, "seq", axis=0)
+        attended = lax.all_to_all(
+            attended_heads, "seq", split_axis=0, concat_axis=1, tiled=True
+        )
     hidden_float = hidden.astype(F32)
     middle = hidden_float + dot(attended, output_weight)
     second_scale = rms_scale(middle)
@@ -1610,8 +1958,10 @@
     ) = experts(
         fast, capacity, sent, place, gate_rows, weight_in, weight_out, shared_in, shared_out
     )
-    gate_grads, out_parts, moe_back = out_side(
-        fast, capacity, back_parts, place, gate_rows, hidden_units, sent_all if fast else sent, shared_units,
+    shared_in_grad = shared_in_grad.reshape(2, padded_units, n_dp, shard)[:, :units].astype(BF)
+    shared_in_grad = shared_in_grad.reshape(2 * units, n_dp, shard).swapaxes(0, 1)
+    gate_grads, out_parts, moe_back, shared_dealt = out_side(
+        fast, capacity, back_parts, shared_in_grad, place, gate_rows, hidden_units, sent_all if fast else sent, shared_units,
         weight_out, shared_out,
     )
     if fast:
@@ -1637,15 +1987,18 @@
     middle_back = upstream_float + norm_backward(moe_back, middle, second_scale, second_gain)
     middle_low = middle_back.astype(BF)
     attended_back = dot_nt(middle_low, output_weight).astype(BF)
-    upstream_heads = lax.all_to_all(
-        attended_back, "seq", split_axis=1, concat_axis=0, tiled=True
-    )
-    attended_all = lax.all_gather(tie(attended, middle_low), "seq", axis=0, tiled=True)
-    middle_columns = lax.all_to_all(middle_low, "seq", split_axis=1, concat_axis=0, tiled=True)
-    output_grad = dot_tn(attended_all, middle_columns)
+    part = features // n_seq
+    packed = jnp.concatenate(
+        [attended_back.reshape(rows, n_seq, -1), middle_low.reshape(rows, n_seq, part)], axis=2
+    ).reshape(rows, -1)
+    if fast:
+        packed = exchange(packed, 10)
+    else:
+        packed = lax.all_to_all(packed, "seq", split_axis=1, concat_axis=0, tiled=True)
+    output_grad = outer(attended_all, packed, part)
 
     query_back, turned_back, key_back, rotary_sum, value_back, out_sum = attend_back(
-        fast, queries, keys_all, values_all, upstream_heads, logs, cosine_all, sine_all, out_parts
+        fast, queries, keys_all, values_all, packed, logs, cosine_all, sine_all, out_parts
     )
     if not fast:
         out_sum = lax.psum_scatter(
@@ -1658,13 +2011,19 @@
     partial_back = partial_terms(
         rows, query_back, turned_back, key_back, value_back, rotary_sum, query_weight, expand_weight
     )
+    query_grad = dot_tn(normed_all, query_raw_back).astype(BF)
+    expand_grad = dot_tn(latent_normed, expanded_back).astype(BF)
     if fast:
-        summed_back = plane_scatter(partial_back.reshape(n_seq, rows, -1), 5)
+        column_grads = jnp.concatenate([query_grad, output_grad], axis=1)
+        summed_back, column_grads, latent_grads = tail_scatter(
+            partial_back.reshape(n_seq, rows, -1),
+            column_grads.reshape(n_dp, shard, -1),
+            expand_grad.reshape(n_dp, LATENT // n_dp, -1),
+            5,
+        )
     else:
         summed_back = lax.psum_scatter(partial_back, "seq", scatter_dimension=0, tiled=True)
     summed_back = summed_back[:, : features + LATENT + ROPE].astype(F32)
-    query_grad = dot_tn(normed_all, query_raw_back)
-    expand_grad = dot_tn(latent_normed, expanded_back)
     latent_normed_back = summed_back[:, features : features + LATENT]
     own = seq_index * rows
 
@@ -1684,7 +2043,9 @@
     compressed_back = jnp.concatenate([latent_back, rotary_back], axis=-1).astype(BF)
     width = (LATENT + ROPE) // n_seq
     if fast:
-        compressed_back_all = plane_gather(jnp.pad(compressed_back, ((0, 0), (0, 64))), 6)
+        compressed_back_all, column_grads, latent_grads = tail_gather(
+            (jnp.pad(compressed_back, ((0, 0), (0, 64))), column_grads, latent_grads), 6
+        )
         compressed_back_all = compressed_back_all[:, :, : LATENT + ROPE]
     else:
         compressed_back_all = lax.all_gather(compressed_back, "seq", axis=0)
@@ -1717,30 +2078,12 @@
     def gain_part(start, size):
         return lax.dynamic_slice_in_dim(gain_grads, start + dp_index * size, size, 0)
 
-    widths = [query_width, expand_width * latent_shard // shard, features // n_seq, width]
-    parts = jnp.concatenate(
-        [
-            query_grad.reshape(n_dp, shard, -1),
-            expand_grad.reshape(n_dp, shard, -1),
-            output_grad.reshape(n_dp, shard, -1),
-            compress_grad.reshape(n_dp, shard, -1),
-        ],
-        axis=-1,
-    )
-    if fast:
-        extra = -parts.shape[-1] % 128
-        summed = sum_grads(jnp.pad(parts, ((0, 0), (0, 0), (0, extra))).astype(BF), 7)
-    else:
-        summed = lax.psum_scatter(parts, "dp", scatter_dimension=0)
-        summed = lax.all_gather(summed.astype(BF), "seq", axis=0)
-
-    def columns(start, size, height):
-        found = summed[:, :, start : start + size].reshape(n_seq, height, -1)
-        return found.transpose(1, 0, 2).reshape(height, -1).astype(F32)
-
-    def in_heads(start, size, height, first, second):
-        found = summed[:, :, start : start + size].reshape(n_seq, height, -1)
-        cut = heads * first
+    def over_dp(grad):
+        total = lax.psum_scatter(grad, "dp", scatter_dimension=0, tiled=True)
+        return lax.all_gather(total.astype(BF), "seq", axis=0)
+
+    def in_heads(found, first, second):
+        height, cut = found.shape[1], heads * first
         found = jnp.concatenate(
             [
                 found[:, :, :cut].reshape(n_seq, height, heads, first),
@@ -1750,13 +2093,26 @@
         )
         return found.transpose(1, 0, 2, 3).reshape(height, -1).astype(F32)
 
-    starts = [sum(widths[:n]) for n in range(4)]
-    shared_in_grad = shared_in_grad.reshape(2, padded_units, n_dp, shard)[:, :units].astype(BF)
-    shared_in_out = lax.all_to_all(
-        shared_in_grad.transpose(2, 3, 0, 1), "dp", split_axis=0, concat_axis=0, tiled=True
-    )
-    shared_in_out = lax.all_gather(shared_in_out, "seq", axis=0)
-    shared_in_out = shared_in_out.transpose(2, 3, 1, 0, 4).reshape(shard, 2 * SH_FF).astype(F32)
+    def columns(found):
+        return found.transpose(1, 0, 2).reshape(found.shape[1], -1).astype(F32)
+
+    if fast:
+        compress_grad = jnp.pad(compress_grad.astype(BF), ((0, 0), (0, 128 - width)))
+        small_grads = sum_grads(compress_grad.reshape(n_dp, shard, 128), 7)
+        query_out, expand_out, output_out, compress_out = layout_grads(
+            column_grads, latent_grads, small_grads, width
+        )
+    else:
+        query_out = in_heads(over_dp(query_grad), NOPE, ROPE)
+        expand_out = in_heads(over_dp(expand_grad), NOPE, VDIM)
+        output_out = columns(over_dp(output_grad))
+        compress_out = columns(over_dp(compress_grad))
+    if not fast:
+        shared_dealt = lax.all_to_all(
+            shared_in_grad, "dp", split_axis=0, concat_axis=0, tiled=True
+        )
+    shared_in_out = lax.all_gather(tie(shared_dealt, query_back), "seq", axis=0)
+    shared_in_out = shared_layout(shared_in_out, units)
     shared_out_out = lax.all_gather(
         shared_out_grad[:units].astype(BF), "seq", axis=0, tiled=True
     ).astype(F32)
@@ -1765,11 +2121,11 @@
         hidden_gradient.reshape(hidden_in.shape),
         gate_gradient.reshape(gate_weights.shape),
         gain_part(0, shard),
-        in_heads(starts[0], widths[0], shard, NOPE, ROPE),
-        columns(starts[3], widths[3], shard),
+        query_out,
+        compress_out,
         gain_part(2 * features, latent_shard),
-        in_heads(starts[1], widths[1], latent_shard, NOPE, VDIM),
-        columns(starts[2], widths[2], shard),
+        expand_out,
+        output_out,
         gain_part(features, shard),
         shared_in_out,
         shared_out_out,

time: 1360 us -> 1260 us (0.926)
  local copies, waits for them, and re-layouts: 133 us -> 85.7 us
  waiting for transfers between devices: 44.6 us -> 3.87 us
  blocking collectives: 25.1 us -> 0 us
  Pallas kernels: 1020 us -> 1040 us
  other arithmetic: 47.3 us -> 29.6 us
    pallas_call x1 -> x6, Pallas kernels: 51.6 us -> 152 us  [the longest x1 59.6 us: tail_scatter(): pl.pallas_call(tail_scatter_kernel, out_shape=[jax.ShapeDtypeStruct((rows...]
    pallas_call x1, Pallas kernels: 95.5 us -> 23.9 us  [sum_grads(): pl.pallas_call(grads_kernel, out_shape=jax.ShapeDtypeStruct((8, rows, col...]
    all_to_all x3 -> x0, waiting for transfers between devices: 30.2 us -> none  [the longest x1 22.3 us: on_device(): lax.all_to_all(attended_back, 'seq', split_axis=1, concat_axis=0, tiled=T...]
    all_to_all x1 -> x0, blocking collectives: 25.1 us -> none  [on_device(): lax.all_to_all(shared_in_grad.transpose(2, 3, 0, 1), 'dp', split_axis=0,...]
    pallas_call x1, Pallas kernels: 15.4 us -> 40 us  [plane_gather(): pl.pallas_call(plane_gather_kernel, out_shape=jax.ShapeDtypeStruct((8, *b...]
    convert_element_type x4 -> x0, local copies, waits for them, and re-layouts: 21.5 us -> none  [the longest x1 10.5 us: on_device(): shared_in_out.transpose(2, 3, 1, 0, 4).reshape(shard, 2 * SH_FF).astype(F32)]
    convert_element_type x5 -> x0, other arithmetic: 19 us -> none  [the longest x1 8.66 us: on_device(): shared_in_out.transpose(2, 3, 1, 0, 4).reshape(shard, 2 * SH_FF).astype(F32)]
    pallas_call x1, Pallas kernels: 180 us -> 163 us  [out_side(): pl.pallas_call(functools.partial(out_kernel, remote, capacity), grid=(blo...]
  transfers between devices with their start and end apart: 13 -> 9, of which waited for: 7 -> 2; matrix products, arithmetic and copies ran while one was open for 7% -> 6% of each run, Pallas kernels for 31% -> 53%
where the time goes in v4:
time: 1260 us; the launch traced here: 1250 us
  Pallas kernels  1040 us (83%)
  local copies, waits for them, and re-layouts  85.7 us (7%)
  between operations  39 us (3%)
  other arithmetic  29.6 us (2%)
  matrix products  27.7 us (2%)
  starting transfers between devices  19.2 us (2%)
    pallas_call x1, Pallas kernels, experts(): pl.pallas_call(functools.partial(experts_kernel, remote, capacity), grid=...  369 us
    pallas_call x1, Pallas kernels, out_side(): pl.pallas_call(functools.partial(out_kernel, remote, capacity), grid=(blo...  163 us
    pallas_call x1, Pallas kernels, attend_back(): pl.pallas_call(functools.partial(attend_back_kernel, remote), grid=(heads...  151 us
    pallas_call x1, Pallas kernels, gather_start(): pl.pallas_call(gather_start_kernel, out_shape=[jax.ShapeDtypeStruct((8, *...  97 us
    pallas_call x1, Pallas kernels, tail_scatter(): pl.pallas_call(tail_scatter_kernel, out_shape=[jax.ShapeDtypeStruct((rows...  59.6 us
    unnamed x140, local copies, waits for them, and re-layouts  57 us
    pallas_call x1, Pallas kernels, tail_gather(): pl.pallas_call(tail_gather_kernel, out_shape=[jax.ShapeDtypeStruct((8, *b...  41.1 us
    pallas_call x1, Pallas kernels, plane_gather(): pl.pallas_call(plane_gather_kernel, out_shape=jax.ShapeDtypeStruct((8, *b...  40 us
  transfers between devices with their start and end apart: 9, of which 2 were waited for; matrix products, arithmetic and copies ran while one was open for 6% of the time, Pallas kernels for 53%

profile of v4, /device:TPU:0, one launch (start us, length us, event | category | flops | bytes accessed | tf_op | source)
XLA Modules:
  0.0 1248.0 jit_solution(3507449813810982781)
XLA Ops:
  7.2 1.9 constant_dynamic-slice_fusion.20
  11.1 6.4 all-to-all-start
  32.7 1.6 copy-done.21
  34.3 97.0 %shard_map.272 = (bf16[8,256,2048]{2,1,0:T(8,128)(2,1)S(1)}, f32[8,4,16,256]{3,2,1,0:T(8,128)S(1)}, bf16[4,16,128]{2,1,0:T(8,128)(2,1)S(1)}, bf16[4,512,384]{2,1...) custom-call(bf16[256,2048]{1,0:T(8,128)(2,1)S(1)} %bitcast.170, ...), custom_call_target="tpu_custom_call" | custom-call | bytes 67108864 | tf_op jit(solution)/shard_map/pallas_call | solution.py:457
  131.4 3.2 copy-done.6
  134.6 1.5 copy-done.18
  137.2 3.4 copy-done.31
  147.6 4.6 fusion.29
  152.2 20.2 %shard_map.273 = (bf16[2048,2048]{1,0:T(8,128)(2,1)}, bf16[2048,384]{1,0:T(8,128)(2,1)S(1)}, bf16[2048,384]{1,0:T(8,128)(2,1)}, bf16[2048,256]{1,0:T(8,128)(2,1)...) custom-call(bf16[2048,2048]{1,0:T(8,128)(2,1)} %bitcast.189, f32[1,2048]{1,0:T(1,128)S(1)} %bitcast.187, ...), custom_call_target="tpu_custom_call" | custom-call | flops 8589934592 | bytes 33554432 | tf_op jit(solution)/shard_map/pallas_call | solution.py:1208
  172.5 2.3 copy-done.9
  174.8 19.0 %shard_map.274 = (bf16[2048,256]{1,0:T(8,128)(2,1)S(1)}, f32[2,2048,128]{2,1,0:T(8,128)S(1)}) custom-call(bf16[2048,384]{1,0:T(8,128)(2,1)S(1)} %get-tuple-element.63.query_ref.turned_ref, bf16[2048,384]{1,0:T(8,128)(2,1)S(1)} %get-tuple-element.63.query_ref.turned_ref, bf16[2048,384]{1,0:T(8,128)(2,1)S(1)} %copy-done.9, bf16[2048,384]{1,0:T(8,128)(2,1)S(1)} %copy-done.9, ...), custom_call_target="tpu_custom_call" | custom-call | flops 3221225472 | bytes 8388608 | tf_op jit(solution)/shard_map/pallas_call | solution.py:1300
  193.8 1.3 copy-done.20
  195.2 40.0 %shard_map.275.left_ref = bf16[8,2048,256]{2,1,0:T(8,128)(2,1)S(1)} custom-call(bf16[2048,256]{1,0:T(8,128)(2,1)S(1)} %get-tuple-element.66.in_ref), custom_call_target="tpu_custom_call" | custom-call | bytes 16777216 | tf_op jit(solution)/shard_map/pallas_call | solution.py:965
  235.1 3.4 copy-done
  238.5 1.3 dynamic-slice_bitcast_fusion
  239.8 1.3 copy.132
  242.0 6.2 multiply_reduce_fusion
  248.4 1.3 constant_dynamic-slice_fusion.12
  252.3 1.5 pad_maximum_fusion.1.rows_in
  255.1 1.3 copy.151.shared_in
  256.4 369.3 %shard_map.276 = (bf16[32,2,256,2048]{3,2,1,0:T(8,128)(2,1)}, f32[2048,1408]{1,0:T(8,128)}, f32[704,2048]{1,0:T(8,128)}, bf16[5120,768]{1,0:T(8,128)(2,1)}, bf16...) custom-call(bf16[2,256,2048]{2,1,0:T(8,128)(2,1)} %pad_maximum_fusion.1.rows_, ...), custom_call_target="tpu_custom_call" | custom-call | flops 96636764160 | bytes 134217728 | tf_op jit(solution)/shard_map/pallas_call | solution.py:839
  625.7 1.7 convert.17
  629.5 1.9 slice.218
  631.5 162.8 %shard_map.277 = (f32[32,1,256]{2,1,0:T(1,128)}, bf16[32,256,2048]{2,1,0:T(8,128)(2,1)}, bf16[256,2048]{1,0:T(8,128)(2,1)}, bf16[4,176,512]{2,1,0:T(8,128)(2,1)}) custom-call(bf16[32,256,2048]{2,1,0:T(8,128)(2,1)} %get-tuple-element.68.back_ref, bf16[4,176,512]{2,1,0:T(8,128)(2,1)} %bitcast.204, s32[32,1,256]{2,1,0:T(1,128)} %broadcast_in_dim.61.place_ref.refs_0_, ...), custom_call_target="tpu_custom_call" | custom-call | flops 26843545600 | bytes 54525952 | tf_op jit(solution)/shard_map/pallas_call | solution.py:1113
  794.3 2.0 fusion.6
  797.1 5.7 convolution_convert_fusion.1
  804.5 26.1 %shard_map.278 = bf16[8,256,512]{2,1,0:T(8,128)(2,1)S(1)} custom-call(bf16[256,4096]{1,0:T(8,128)(2,1)S(1)} %bitcast.176), custom_call_target="tpu_custom_call" | custom-call | bytes 4194304 | tf_op jit(solution)/shard_map/pallas_call | solution.py:1786
  830.6 1.3 copy-done.4
  831.9 150.5 %shard_map.279 = (bf16[2048,256]{1,0:T(8,128)(2,1)}, bf16[2048,256]{1,0:T(8,128)(2,1)}, bf16[2048,256]{1,0:T(8,128)(2,1)}, f32[2048,128]{1,0:T(8,128)}, bf16[204...) custom-call(bf16[2048,384]{1,0:T(8,128)(2,1)} %copy-done.8, bf16[2048,384]{1,0:T(8,128)(2,1)} %copy-done.8, ...), custom_call_target="tpu_custom_call" | custom-call | flops 8589934592 | bytes 67108864 | tf_op jit(solution)/shard_map/pallas_call | solution.py:1395
  982.5 1.3 copy-done.14
  995.8 3.4 copy-done.1
  999.2 4.1 shard_map.281
  1004.2 2.5 copy.145
  1006.8 1.3 slice_add_fusion.turned_ref
  1008.2 7.0 convolution_convert_fusion
  1015.1 1.7 pad_maximum_fusion
  1016.8 4.4 copy.146
  1021.3 1.4 copy-done.23
  1023.9 1.3 copy-done.26
  1026.4 8.5 shard_map.280
  1034.9 1.3 fusion.22
  1036.6 59.6 %shard_map.282 = (bf16[256,2688]{1,0:T(8,128)(2,1)S(1)}, bf16[512,640]{1,0:T(8,128)(2,1)S(1)}, bf16[128,512]{1,0:T(8,128)(2,1)S(1)}) custom-call(bf16[8,256,2688]{2,1,0:T(8,128)(2,1)} %bitcast.190, bf16[4,512,640]{2,1,0:T(8,128)(2,1)S(1)} %bitcast.175, bf16[4,128,512]{2,1,0:T(8,128)(2,1)S(1)} %bitcast.182), custom_call_target="tpu_custom_call" | custom-call | bytes 33554432 | tf_op jit(solution)/shard_map/pallas_call | solution.py:1574
  1097.0 1.4 multiply_reduce_fusion.1
  1100.8 1.4 fusion.14
  1102.7 41.1 %shard_map.283 = (bf16[8,256,640]{2,1,0:T(8,128)(2,1)S(1)}, bf16[8,512,640]{2,1,0:T(8,128)(2,1)S(1)}, bf16[8,128,512]{2,1,0:T(8,128)(2,1)S(1)}) custom-call(bf16[256,640]{1,0:T(8,128)(2,1)S(1)} %pad.28.refs_0_, bf16[512,640]{1,0:T(8,128)(2,1)S(1)} %get-tuple-element.87.refs_1_, bf16[128,512]{1,0:T(8,128)(2,1)S(1)} %get-tuple-element.88.refs_2_), custom_call_target="tpu_custom_call" | custom-call | bytes 16777216 | tf_op jit(solution)/shard_map/pallas_call | solution.py:1627
  1143.8 2.3 copy-done.10
  1146.2 6.0 convolution_convert_fusion.2
  1152.2 2.5 fusion.28
  1154.6 1.7 collective-permute-start.1
  1156.3 2.2 collective-permute-done.1
  1158.5 1.6 collective-permute-start.2
  1160.1 1.2 copy.158
  1161.5 23.9 %shard_map.284.small_ref = bf16[8,512,128]{2,1,0:T(8,128)(2,1)S(1)} custom-call(bf16[4,512,128]{2,1,0:T(8,128)(2,1)S(1)} %bitcast.179), custom_call_target="tpu_custom_call" | custom-call | bytes 2097152 | tf_op jit(solution)/shard_map/pallas_call | solution.py:1013
  1186.0 4.6 all-to-all-start.1
  1190.7 1.9 collective-permute-start.3
  1192.6 2.5 copy-done.11
  1195.1 8.3 shard_map.285
  1203.4 1.4 copy.149
  1205.0 2.5 collective-permute-start.4
  1208.1 1.6 collective-permute-done.4
  1211.0 5.1 convert_element_type.100
  1216.1 12.5 %shard_map.287 = f32[512,5632]{1,0:T(8,128)} custom-call(bf16[8,4,176,512]{3,2,1,0:T(8,128)(2,1)} %bitcast.197), custom_call_target="tpu_custom_call" | custom-call | flops 4294967296 | bytes 17301504 | tf_op jit(solution)/shard_map/pallas_call | solution.py:1725
  1228.6 9.6 copy.188
  1238.2 2.5 copy.189
  (220 shorter events, 33.3 us)
Async XLA Ops:
  11.1 7.9 copy-start.54
  11.1 242.7 %all-to-all-start = ((bf16[4,512,2,88]{1,3,2,0:T(8,128)(2,1)}), bf16[4,512,2,88]{1,3,2,0:T(8,128)(2,1)}, u32[]{:S(2)}, u32[]{:S(2)}) async-start(bf16[4,512,2,88]{1,3,2,0:T(8,128)(2,1)} %pad_maximum_fusion.4), calls=%async_computation | async-start | bytes 1441792 | tf_op jit(solution)/shard_map/all_to_all | solution.py:1914
  17.5 14.1 %copy-start.49 = (s32[1,256,6]{1,0,2:T(1,128)S(1)}, s32[1,256,6]{1,0,2:T(1,128)}, u32[]{:S(2)}) copy-start(s32[1,256,6]{1,0,2:T(1,128)} %param.19) | copy-start | bytes 18436
  17.5 14.7 %copy-start.48 = (f32[1,256,6]{1,0,2:T(1,128)S(1)}, f32[1,256,6]{1,0,2:T(1,128)}, u32[]{:S(2)}) copy-start(f32[1,256,6]{1,0,2:T(1,128)} %param.20) | copy-start | bytes 18436
  17.5 14.7 %copy-start.50 = (s32[1,256]{1,0:T(1,128)S(1)}, s32[1,256]{1,0:T(1,128)}, u32[]{:S(2)}) copy-start(s32[1,256]{1,0:T(1,128)} %param.18) | copy-start | bytes 3076
  17.5 14.7 %copy-start.43 = (bf16[512,576]{0,1:T(8,128)(2,1)S(1)}, bf16[512,576]{0,1:T(8,128)(2,1)}, u32[]{:S(2)}) copy-start(bf16[512,576]{0,1:T(8,128)(2,1)} %param.23) | copy-start | bytes 1769476
  17.6 1193.4 %all-gather.4.cloned.1.call-start = ((), (), s32[]{:S(2)}) async-start(), calls=%async_computation.2 | async-start | bytes 3244032 | tf_op jit(solution)/shard_map/all_gather | solution.py:2116
  30.2 2.5 copy-start.51
  30.2 2.5 copy-start.52
  30.2 2.5 copy-start.53
  30.2 2.5 copy-start.2
  32.7 1.6 copy-start.21
  131.4 3.2 copy-start.6
  134.6 1.5 copy-start.18
  136.0 1.2 copy-start.22
  137.2 3.4 copy-start.31
  140.6 11.5 copy-start.29
  152.1 20.3 %copy-start.12 = (f32[2048,128]{1,0:T(8,128)}, f32[2048,128]{1,0:T(8,128)S(1)}, u32[]{:S(2)}) copy-start(f32[2048,128]{1,0:T(8,128)S(1)} %get-tuple-element.204.sine_ref) | copy-start | bytes 3145732
  152.1 20.3 %copy-start.13 = (f32[2048,128]{1,0:T(8,128)}, f32[2048,128]{1,0:T(8,128)S(1)}, u32[]{:S(2)}) copy-start(f32[2048,128]{1,0:T(8,128)S(1)} %get-tuple-element.205.cosine_ref) | copy-start | bytes 3145732
  172.4 21.4 %copy-start.8 = (bf16[2048,384]{1,0:T(8,128)(2,1)}, bf16[2048,384]{1,0:T(8,128)(2,1)S(1)}, u32[]{:S(2)}) copy-start(bf16[2048,384]{1,0:T(8,128)(2,1)S(1)} %get-tuple-element.63.query_ref.turned_ref) | copy-start | bytes 4718596
  172.4 21.4 %copy-start.24 = (bf16[2048,256]{1,0:T(8,128)(2,1)}, bf16[2048,256]{1,0:T(8,128)(2,1)S(1)}, u32[]{:S(2)}) copy-start(bf16[2048,256]{1,0:T(8,128)(2,1)S(1)} %get-tuple-element.65.value_ref) | copy-start | bytes 3145732
  172.4 2.4 copy-start.9
  193.8 1.3 copy-start.20
  235.1 3.4 copy-start
  242.0 6.2 copy-start.41
  248.2 4.1 copy-start.32
  249.9 2.4 copy-start.35
  631.4 584.7 %all-gather.6.cloned.1.call-start = ((), (), s32[]{:S(2)}) async-start(), calls=%async_computation.3 | async-start | bytes 6488064 | tf_op jit(solution)/shard_map/all_gather | solution.py:2114
  631.5 162.9 %copy-start.33 = (f32[256,2048]{1,0:T(8,128)S(1)}, f32[256,2048]{1,0:T(8,128)}, u32[]{:S(2)}) copy-start(f32[256,2048]{1,0:T(8,128)} %copy-done.32) | copy-start | bytes 6291460
  794.3 2.0 copy-start.36
  794.3 2.0 copy-start.38
  830.6 1.3 copy-start.4
  831.9 159.8 %copy-start.44 = (f32[1,4,4,128]{3,2,1,0:T(4,128)S(1)}, f32[1,4,4,128]{3,2,1,0:T(4,128)}, u32[]{:S(2)}) copy-start(f32[1,4,4,128]{3,2,1,0:T(4,128)} %get-tuple-element.222) | copy-start | bytes 24580
  982.5 13.0 %copy-start.3 = (bf16[1,256,2048]{2,1,0:T(8,128)(2,1)S(1)}, bf16[1,256,2048]{2,1,0:T(8,128)(2,1)}, u32[]{:S(2)}) copy-start(bf16[1,256,2048]{2,1,0:T(8,128)(2,1)} %param.17) | copy-start | bytes 3145732
  982.5 1.3 copy-start.14
  983.8 1.1 copy-start.28
  984.9 10.9 copy-start.5
  995.8 3.4 copy-start.1
  1004.2 3.9 copy-start.15
  1008.1 7.0 copy-start.40
  1016.8 4.4 copy-start.30
  1021.3 1.4 copy-start.23
  1022.7 1.2 copy-start.25
  1023.9 1.3 copy-start.26
  1025.1 1.2 copy-start.27
  1026.4 8.5 copy-start.55
  1034.9 1.7 copy-start.7
  1097.0 3.9 copy-start.19
  1100.8 1.8 copy-start.45
  1102.3 52.3 %collective-permute-start = (f32[4608]{0:T(1024)S(1)}, f32[4608]{0:T(1024)S(1)}, u32[]{:S(2)}, u32[]{:S(2)}) collective-permute-start(f32[4608]{0:T(1024)S(1)} %pad_maximum_fusion.9), channel_id=1, source_target_pairs={{0,1},{1,0},{2,3},{3,2},{4,5},{5,4},{6,7},{7,6},{8,9},{9,8},{10,11... | collective-permute-start | bytes 55304 | tf_op jit(solution)/shard_map/ppermute | solution.py:2066
  1143.8 2.4 copy-start.10
  1146.1 6.0 copy-start.34
  1146.1 6.0 copy-start.37
  1146.1 6.0 copy-start.39
  1146.1 6.0 copy-start.42
  1154.6 3.8 collective-permute-start.1
  1158.5 32.2 %collective-permute-start.2 = (f32[4608]{0:T(1024)S(1)}, f32[4608]{0:T(1024)S(1)}, u32[]{:S(2)}, u32[]{:S(2)}) collective-permute-start(f32[4608]{0:T(1024)S(1)} %add.275), channel_id=1, source_target_pairs={{0,4},{1,5},{2,6},{3,7},{4,0},{5,1},{6,2},{7,3},{8,12},{9,13},{10,... | collective-permute-start | bytes 55304 | tf_op jit(solution)/shard_map/ppermute | solution.py:2066
  1186.0 18.8 %all-to-all-start.1 = ((f32[32,1,256]{2,1,0:T(1,128)}), f32[32,1,256]{2,1,0:T(1,128)S(1)}, u32[]{:S(2)}, u32[]{:S(2)}) async-start(f32[32,1,256]{2,1,0:T(1,128)} %reshape.261), calls=%async_computation.1 | async-start | bytes 65536 | tf_op jit(solution)/shard_map/all_to_all | solution.py:1976
  1190.7 14.3 %collective-permute-start.3 = (f32[4608]{0:T(1024)S(1)}, f32[4608]{0:T(1024)S(1)}, u32[]{:S(2)}, u32[]{:S(2)}) collective-permute-start(f32[4608]{0:T(1024)S(1)} %add.276), channel_id=1, source_target_pairs={{0,8},{8,0},{16,24},{24,16},{1,9},{9,1},{17,25},{25,17},{2,10},{10... | collective-permute-start | bytes 55304 | tf_op jit(solution)/shard_map/ppermute | solution.py:2072
  1192.6 2.5 copy-start.11
  1203.4 4.1 copy-start.46
  1205.0 4.7 collective-permute-start.4
  1216.1 22.1 %slice-start = ((s8[5767168]{0:T(1024)(128)(4,1)}), s8[1572864]{0:T(1024)(128)(4,1)S(1)}, s32[]{:S(2)}) async-start(s8[5767168]{0:T(1024)(128)(4,1)} %bitcast.194), calls=%async_computation.4 | async-start | bytes 3145728
  1228.6 9.6 slice-start.1
  (3 other events, 2.6 us)
Sparse Core Ops, SparseCore 0:
  631.5 39.1 all-gather.3
  986.0 41.1 all-gather.5

commit v5 on v4

--- a/solution.py
+++ b/solution.py
@@ -371,8 +371,6 @@
     post = Courier(send_sems, recv_sems)
     strip = output.shape[0] // 8
     own_strip = pl.ds(pl.multiple_of(seq * strip, strip), strip)
-    core_half = compress.shape[0] // 2
-    mine = pl.ds(pl.multiple_of((seq % 2) * core_half, core_half), core_half)
     hidden_spread = spread(post, hidden, blocks_of(hidden_all), core, across_x, across_y)
     advance(hidden_spread)
 
@@ -382,8 +380,8 @@
         return [
             post.send(query if first else query_all.at[at], query_all.at[at], following),
             post.send(
-                compress.at[mine] if first else compress_all.at[at, mine],
-                compress_all.at[at, mine],
+                compress.at[own_strip] if first else compress_all.at[at, own_strip],
+                compress_all.at[at, own_strip],
                 following,
             ),
             post.send(expand if first else expand_all.at[at], expand_all.at[at], following),
@@ -396,14 +394,14 @@
             ),
         ]
 
-    def strip_spread(at):
+    def strip_spread(whole, at):
         def place(index, part=None):
             if part is None:
                 where = pl.ds(pl.multiple_of(index * strip, strip), strip)
             else:
                 half = strip // 2
                 where = pl.ds(pl.multiple_of(index * strip + part * half, half), half)
-            return output_all.at[at, where]
+            return whole.at[at, where]
 
         return spread(post, place(seq), place, core, across_x, across_y)
 
@@ -431,12 +429,11 @@
         at = (dp + 5 - i) % 4
         if i < 4:
             ring = hop(i)
-        post.send(compress_all.at[at, mine], compress_all.at[at, mine], core)
         advance(*spreads)
         if i < 4:
             advance(hidden_spread)
-        spreads.append(strip_spread(at))
-        advance(spreads[-1])
+        spreads += [strip_spread(compress_all, at), strip_spread(output_all, at)]
+        advance(*spreads[-2:])
     locals_[1].wait()
     names_x = post.send(named_all.at[0], named_all.at[1], across_x)
     advance(*spreads)
@@ -453,7 +450,7 @@
 
 def gather_start(hidden, named, gains, query, expand, compress, output, collective_id):
     anywhere = pl.BlockSpec(memory_space=pl.ANY)
-    total = 8 + 6 * 3 + 3 + 3 + 8 * 3
+    total = 8 + 6 * 3 + 3 + 2 * 3 * 8
     return pl.pallas_call(
         gather_start_kernel,
         out_shape=[
@@ -878,76 +875,6 @@
     return found
 
 
-def plane_scatter_kernel(
-    in_ref, out_ref, held, far, near, stage, send_sems, recv_sems, local_sems
-):
-    core, across_x, across_y, _, _ = neighbours()
-    greet((core, across_x, across_y))
-    seq = lax.axis_index("seq")
-    rows = out_ref.shape[0]
-    top, bottom = pl.ds(0, rows // 2), pl.ds(rows // 2, rows // 2)
-    post = Courier(send_sems, recv_sems)
-    x_seq = seq + 2 - 4 * ((seq // 2) % 2)
-    y_seq = seq + 4 - 8 * (seq // 4)
-    xy_seq = x_seq + 4 - 8 * (seq // 4)
-    core_step = 1 - 2 * (seq % 2)
-    loads, arriving = {}, {}
-    for k, place in ((3, xy_seq), (1, x_seq), (2, y_seq), (0, seq)):
-        arriving[k] = post.send(in_ref.at[place + core_step], held.at[k], core)
-        loads[k] = pltpu.make_async_copy(in_ref.at[place], stage.at[k], local_sems.at[k])
-        loads[k].start()
-
-    def join(k):
-        loads[k].wait()
-        post.take(arriving[k])
-        accumulate(held.at[k], stage.at[k])
-
-    join(3)
-    far_top = post.send(held.at[3, top], far.at[0], across_y)
-    far_bottom = post.send(held.at[3, bottom], far.at[1], across_x)
-    join(1)
-    x_bottom = post.send(held.at[1, bottom], near.at[0, bottom], across_x)
-    join(2)
-    y_top = post.send(held.at[2, top], near.at[1, top], across_y)
-    join(0)
-    post.take(far_top)
-    accumulate(held.at[1, top], far.at[0])
-    x_top = post.send(held.at[1, top], near.at[0, top], across_x)
-    post.take(far_bottom)
-    accumulate(held.at[2, bottom], far.at[1])
-    y_bottom = post.send(held.at[2, bottom], near.at[1, bottom], across_y)
-    for copy in (x_bottom, y_top, x_top, y_bottom):
-        post.take(copy)
-    accumulate(held.at[0], near.at[0], near.at[1])
-    out_ref[...] = held[0]
-    post.finish()
-
-
-def plane_scatter(parts, collective_id):
-    _, rows, columns = parts.shape
-    return pl.pallas_call(
-        plane_scatter_kernel,
-        out_shape=jax.ShapeDtypeStruct((rows, columns), parts.dtype),
-        in_specs=[pl.BlockSpec(memory_space=pl.ANY)],
-        out_specs=pl.BlockSpec(memory_space=pltpu.VMEM),
-        scratch_shapes=[
-            pltpu.VMEM((4, rows, columns), parts.dtype),
-            pltpu.VMEM((2, rows // 2, columns), parts.dtype),
-            pltpu.VMEM((2, rows, columns), parts.dtype),
-            pltpu.VMEM((4, rows, columns), parts.dtype),
-            pltpu.SemaphoreType.DMA((10,)),
-            pltpu.SemaphoreType.DMA((10,)),
-            pltpu.SemaphoreType.DMA((4,)),
-        ],
-        compiler_params=pltpu.CompilerParams(
-            collective_id=collective_id, has_side_effects=True, vmem_limit_bytes=32 * 2**20
-        ),
-        cost_estimate=pl.CostEstimate(
-            flops=8 * rows * columns, bytes_accessed=16 * rows * columns, transcendentals=0
-        ),
-    )(parts)
-
-
 def plane_gather_kernel(in_ref, out_ref, send_sems, recv_sems, local_sem):
     core, across_x, across_y, _, _ = neighbours()
     greet((core, across_x, across_y))
@@ -981,8 +908,12 @@
     )(block)
 
 
-def grads_kernel(in_ref, out_ref, total, ring, send_sems, recv_sems, local_sems):
+def grads_kernel(
+    in_ref, columns_ref, latents_ref, out_ref, columns_out, latents_out, total, ring, send_sems,
+    recv_sems, local_sems
+):
     dp = lax.axis_index("dp")
+    seq = lax.axis_index("seq")
     core, across_x, across_y, following, previous = neighbours()
     greet((core, across_x, across_y, following, previous))
     post = Courier(send_sems, recv_sems)
@@ -993,42 +924,60 @@
         loads.append(load)
     loads[0].wait()
     before = post.send(total.at[0], ring.at[0], following)
+    spreads = [
+        spread(post, source, blocks_of(found), core, across_x, across_y)
+        for source, found in ((columns_ref, columns_out), (latents_ref, latents_out))
+    ]
+    advance(*spreads)
+    owns = [
+        pltpu.make_async_copy(columns_ref, columns_out.at[seq], local_sems.at[4]),
+        pltpu.make_async_copy(latents_ref, latents_out.at[seq], local_sems.at[5]),
+    ]
+    for own in owns:
+        own.start()
     for n in (1, 2, 3):
         loads[n].wait()
         post.take(before)
         accumulate(total.at[n], ring.at[n - 1])
         if n < 3:
             before = post.send(total.at[n], ring.at[n], following)
-    own = pltpu.make_async_copy(total.at[3], out_ref.at[lax.axis_index("seq")], local_sems.at[0])
-    own.start()
-    for _ in spread(post, total.at[3], blocks_of(out_ref), core, across_x, across_y):
-        pass
-    own.wait()
+    owns.append(pltpu.make_async_copy(total.at[3], out_ref.at[seq], local_sems.at[0]))
+    owns[2].start()
+    spreads.append(spread(post, total.at[3], blocks_of(out_ref), core, across_x, across_y))
+    advance(spreads[2])
+    advance(*spreads)
+    advance(*spreads)
+    for own in owns:
+        own.wait()
     post.finish()
 
 
-def sum_grads(parts, collective_id):
-    _, rows, columns = parts.shape
+def sum_grads(parts, columns, latents, collective_id):
+    _, rows, width = parts.shape
     anywhere = pl.BlockSpec(memory_space=pl.ANY)
     return pl.pallas_call(
         grads_kernel,
-        out_shape=jax.ShapeDtypeStruct((8, rows, columns), parts.dtype),
-        in_specs=[anywhere],
-        out_specs=anywhere,
+        out_shape=[
+            jax.ShapeDtypeStruct((8, rows, width), parts.dtype),
+            jax.ShapeDtypeStruct((8, *columns.shape), columns.dtype),
+            jax.ShapeDtypeStruct((8, *latents.shape), latents.dtype),
+        ],
+        in_specs=[anywhere] * 3,
+        out_specs=[anywhere] * 3,
         scratch_shapes=[
-            pltpu.VMEM((4, rows, columns), parts.dtype),
-            pltpu.VMEM((3, rows, columns), parts.dtype),
-            pltpu.SemaphoreType.DMA((11,)),
-            pltpu.SemaphoreType.DMA((11,)),
-            pltpu.SemaphoreType.DMA((4,)),
+            pltpu.VMEM((4, rows, width), parts.dtype),
+            pltpu.VMEM((3, rows, width), parts.dtype),
+            pltpu.SemaphoreType.DMA((27,)),
+            pltpu.SemaphoreType.DMA((27,)),
+            pltpu.SemaphoreType.DMA((6,)),
         ],
         compiler_params=pltpu.CompilerParams(
             collective_id=collective_id, has_side_effects=True, vmem_limit_bytes=32 * 2**20
         ),
         cost_estimate=pl.CostEstimate(
-            flops=0, bytes_accessed=32 * rows * columns, transcendentals=0
-        ),
-    )(parts)
+            flops=0, bytes_accessed=32 * rows * width, transcendentals=0
+        ),
+    )(parts, columns, latents)
 
 
 OUT_EVENTS = (3, 5, 7, 9, 13, 17, 18, 23, 27, 30, 31, 31)
@@ -1598,47 +1547,6 @@
         ),
         cost_estimate=pl.CostEstimate(flops=0, bytes_accessed=2**25, transcendentals=0),
     )(parts, columns, latents)
-
-
-def tail_gather_kernel(*refs):
-    sources, found = refs[:3], refs[3:6]
-    send_sems, recv_sems, local_sems = refs[6:]
-    core, across_x, across_y, _, _ = neighbours()
-    greet((core, across_x, across_y))
-    seq = lax.axis_index("seq")
-    post = Courier(send_sems, recv_sems)
-    owns = []
-    for n in range(3):
-        own = pltpu.make_async_copy(sources[n], found[n].at[seq], local_sems.at[n])
-        own.start()
-        owns.append(own)
-    spreads = [
-        spread(post, sources[n], blocks_of(found[n]), core, across_x, across_y) for n in range(3)
-    ]
-    for _ in range(3):
-        advance(*spreads)
-    for own in owns:
-        own.wait()
-    post.finish()
-
-
-def tail_gather(blocks, collective_id):
-    anywhere = pl.BlockSpec(memory_space=pl.ANY)
-    return pl.pallas_call(
-        tail_gather_kernel,
-        out_shape=[jax.ShapeDtypeStruct((8, *b.shape), b.dtype) for b in blocks],
-        in_specs=[anywhere] * 3,
-        out_specs=[anywhere] * 3,
-        scratch_shapes=[
-            pltpu.SemaphoreType.DMA((24,)),
-            pltpu.SemaphoreType.DMA((24,)),
-            pltpu.SemaphoreType.DMA((3,)),
-        ],
-        compiler_params=pltpu.CompilerParams(
-            collective_id=collective_id, has_side_effects=True, vmem_limit_bytes=16 * 2**20
-        ),
-        cost_estimate=pl.CostEstimate(flops=0, bytes_accessed=2**24, transcendentals=0),
-    )(*blocks)
 
 
 def chosen_columns(source, target):
@@ -2043,9 +1951,7 @@
     compressed_back = jnp.concatenate([latent_back, rotary_back], axis=-1).astype(BF)
     width = (LATENT + ROPE) // n_seq
     if fast:
-        compressed_back_all, column_grads, latent_grads = tail_gather(
-            (jnp.pad(compressed_back, ((0, 0), (0, 64))), column_grads, latent_grads), 6
-        )
+        compressed_back_all = plane_gather(jnp.pad(compressed_back, ((0, 0), (0, 64))), 6)
         compressed_back_all = compressed_back_all[:, :, : LATENT + ROPE]
     else:
         compressed_back_all = lax.all_gather(compressed_back, "seq", axis=0)
@@ -2098,7 +2004,9 @@
 
     if fast:
         compress_grad = jnp.pad(compress_grad.astype(BF), ((0, 0), (0, 128 - width)))
-        small_grads = sum_grads(compress_grad.reshape(n_dp, shard, 128), 7)
+        small_grads, column_grads, latent_grads = sum_grads(
+            compress_grad.reshape(n_dp, shard, 128), column_grads, latent_grads, 7
+        )
         query_out, expand_out, output_out, compress_out = layout_grads(
             column_grads, latent_grads, small_grads, width
         )

time: 1260 us -> 1230 us (0.976)
  Pallas kernels: 1040 us -> 1020 us
    pallas_call x2 -> x1, Pallas kernels: 65 us -> 37 us  [sum_grads(): pl.pallas_call(grads_kernel, out_shape=[jax.ShapeDtypeStruct((8, rows, wi...]
    pallas_call x1 -> x2, Pallas kernels: 40 us -> 56.9 us  [plane_gather(): pl.pallas_call(plane_gather_kernel, out_shape=jax.ShapeDtypeStruct((8, *b...]
    unnamed x140 -> x136, local copies, waits for them, and re-layouts: 57 us -> 52.2 us
  transfers between devices with their start and end apart: 9 -> 9, of which waited for: 2 -> 1; matrix products, arithmetic and copies ran while one was open for 6% -> 7% of each run, Pallas kernels for 53% -> 52%
where the time goes in v5:
time: 1230 us; the launch traced here: 1220 us
  Pallas kernels  1020 us (83%)
  local copies, waits for them, and re-layouts  80.9 us (7%)
  between operations  39.1 us (3%)
  other arithmetic  29.9 us (2%)
  matrix products  27.5 us (2%)
  starting transfers between devices  17.9 us (1%)
    pallas_call x1, Pallas kernels, experts(): pl.pallas_call(functools.partial(experts_kernel, remote, capacity), grid=...  369 us
    pallas_call x1, Pallas kernels, out_side(): pl.pallas_call(functools.partial(out_kernel, remote, capacity), grid=(blo...  163 us
    pallas_call x1, Pallas kernels, attend_back(): pl.pallas_call(functools.partial(attend_back_kernel, remote), grid=(heads...  151 us
    pallas_call x1, Pallas kernels, gather_start(): pl.pallas_call(gather_start_kernel, out_shape=[jax.ShapeDtypeStruct((8, *...  84.7 us
    pallas_call x1, Pallas kernels, tail_scatter(): pl.pallas_call(tail_scatter_kernel, out_shape=[jax.ShapeDtypeStruct((rows...  57.2 us
    pallas_call x2, Pallas kernels, plane_gather(): pl.pallas_call(plane_gather_kernel, out_shape=jax.ShapeDtypeStruct((8, *b...  56.9 us
    unnamed x136, local copies, waits for them, and re-layouts  52.2 us
    pallas_call x1, Pallas kernels, sum_grads(): pl.pallas_call(grads_kernel, out_shape=[jax.ShapeDtypeStruct((8, rows, wi...  37 us
  transfers between devices with their start and end apart: 9, of which 1 were waited for; matrix products, arithmetic and copies ran while one was open for 7% of the time, Pallas kernels for 52%

profile of v5, /device:TPU:0, one launch (start us, length us, event | category | flops | bytes accessed | tf_op | source)
XLA Modules:
  0.0 1215.7 jit_solution(1524050516510245452)
XLA Ops:
  7.2 1.9 constant_dynamic-slice_fusion.20
  11.1 6.4 all-to-all-start
  32.7 1.6 copy-done.19
  34.3 84.7 %shard_map.272 = (bf16[8,256,2048]{2,1,0:T(8,128)(2,1)S(1)}, f32[8,4,16,256]{3,2,1,0:T(8,128)S(1)}, bf16[4,16,128]{2,1,0:T(8,128)(2,1)S(1)}, bf16[4,512,384]{2,1...) custom-call(bf16[256,2048]{1,0:T(8,128)(2,1)S(1)} %bitcast.170, ...), custom_call_target="tpu_custom_call" | custom-call | bytes 67108864 | tf_op jit(solution)/shard_map/pallas_call | solution.py:454
  119.0 3.2 copy-done.6
  122.2 1.5 copy-done.16
  124.9 3.4 copy-done.29
  135.2 4.6 fusion.29
  139.8 20.2 %shard_map.273 = (bf16[2048,2048]{1,0:T(8,128)(2,1)}, bf16[2048,384]{1,0:T(8,128)(2,1)S(1)}, bf16[2048,384]{1,0:T(8,128)(2,1)}, bf16[2048,256]{1,0:T(8,128)(2,1)...) custom-call(bf16[2048,2048]{1,0:T(8,128)(2,1)} %bitcast.189, f32[1,2048]{1,0:T(1,128)S(1)} %bitcast.187, ...), custom_call_target="tpu_custom_call" | custom-call | flops 8589934592 | bytes 33554432 | tf_op jit(solution)/shard_map/pallas_call | solution.py:1157
  160.1 2.3 copy-done.9
  162.5 19.0 %shard_map.274 = (bf16[2048,256]{1,0:T(8,128)(2,1)S(1)}, f32[2,2048,128]{2,1,0:T(8,128)S(1)}) custom-call(bf16[2048,384]{1,0:T(8,128)(2,1)S(1)} %get-tuple-element.63.query_ref.turned_ref, bf16[2048,384]{1,0:T(8,128)(2,1)S(1)} %get-tuple-element.63.query_ref.turned_ref, bf16[2048,384]{1,0:T(8,128)(2,1)S(1)} %copy-done.9, bf16[2048,384]{1,0:T(8,128)(2,1)S(1)} %copy-done.9, ...), custom_call_target="tpu_custom_call" | custom-call | flops 3221225472 | bytes 8388608 | tf_op jit(solution)/shard_map/pallas_call | solution.py:1249
  181.5 1.3 copy-done.18
  182.8 40.4 %shard_map.275.left_ref = bf16[8,2048,256]{2,1,0:T(8,128)(2,1)S(1)} custom-call(bf16[2048,256]{1,0:T(8,128)(2,1)S(1)} %get-tuple-element.66.in_ref), custom_call_target="tpu_custom_call" | custom-call | bytes 16777216 | tf_op jit(solution)/shard_map/pallas_call | solution.py:892
  223.3 3.4 copy-done
  226.7 1.3 dynamic-slice_bitcast_fusion
  228.0 1.3 copy.132
  230.1 6.2 multiply_reduce_fusion
  236.6 1.3 constant_dynamic-slice_fusion.12
  240.4 1.5 pad_maximum_fusion.1.rows_in
  243.2 1.3 copy.151.shared_in
  244.5 368.8 %shard_map.276 = (bf16[32,2,256,2048]{3,2,1,0:T(8,128)(2,1)}, f32[2048,1408]{1,0:T(8,128)}, f32[704,2048]{1,0:T(8,128)}, bf16[5120,768]{1,0:T(8,128)(2,1)}, bf16...) custom-call(bf16[2,256,2048]{2,1,0:T(8,128)(2,1)} %pad_maximum_fusion.1.rows_, ...), custom_call_target="tpu_custom_call" | custom-call | flops 96636764160 | bytes 134217728 | tf_op jit(solution)/shard_map/pallas_call | solution.py:836
  613.4 1.7 convert.17
  617.2 1.9 slice.218
  619.1 163.1 %shard_map.277 = (f32[32,1,256]{2,1,0:T(1,128)}, bf16[32,256,2048]{2,1,0:T(8,128)(2,1)}, bf16[256,2048]{1,0:T(8,128)(2,1)}, bf16[4,176,512]{2,1,0:T(8,128)(2,1)}) custom-call(bf16[32,256,2048]{2,1,0:T(8,128)(2,1)} %get-tuple-element.68.back_ref, bf16[4,176,512]{2,1,0:T(8,128)(2,1)} %bitcast.204, s32[32,1,256]{2,1,0:T(1,128)} %broadcast_in_dim.61.place_ref.refs_0_, ...), custom_call_target="tpu_custom_call" | custom-call | flops 26843545600 | bytes 54525952 | tf_op jit(solution)/shard_map/pallas_call | solution.py:1062
  782.3 2.0 fusion.6
  785.0 5.7 convolution_convert_fusion.1
  792.5 26.0 %shard_map.278 = bf16[8,256,512]{2,1,0:T(8,128)(2,1)S(1)} custom-call(bf16[256,4096]{1,0:T(8,128)(2,1)S(1)} %bitcast.176), custom_call_target="tpu_custom_call" | custom-call | bytes 4194304 | tf_op jit(solution)/shard_map/pallas_call | solution.py:1694
  818.5 1.3 copy-done.4
  819.8 151.4 %shard_map.279 = (bf16[2048,256]{1,0:T(8,128)(2,1)}, bf16[2048,256]{1,0:T(8,128)(2,1)}, bf16[2048,256]{1,0:T(8,128)(2,1)}, f32[2048,128]{1,0:T(8,128)}, bf16[204...) custom-call(bf16[2048,384]{1,0:T(8,128)(2,1)} %copy-done.8, bf16[2048,384]{1,0:T(8,128)(2,1)} %copy-done.8, ...), custom_call_target="tpu_custom_call" | custom-call | flops 8589934592 | bytes 67108864 | tf_op jit(solution)/shard_map/pallas_call | solution.py:1344
  971.2 1.3 copy-done.12
  984.5 3.4 copy-done.1
  987.9 4.1 shard_map.281
  992.9 2.5 copy.145
  995.5 1.6 slice_add_fusion.turned_ref
  997.1 7.0 convolution_convert_fusion
  1004.0 1.7 pad_maximum_fusion
  1005.7 4.4 copy.146
  1010.2 1.5 copy-done.21
  1011.7 1.2 copy-done.23
  1012.9 1.2 copy-done.24
  1014.1 1.2 copy-done.25
  1015.3 8.5 shard_map.280
  1023.9 1.3 fusion.22
  1025.6 57.2 %shard_map.282 = (bf16[256,2688]{1,0:T(8,128)(2,1)S(1)}, bf16[512,640]{1,0:T(8,128)(2,1)S(1)}, bf16[128,512]{1,0:T(8,128)(2,1)S(1)}) custom-call(bf16[8,256,2688]{2,1,0:T(8,128)(2,1)} %bitcast.190, bf16[4,512,640]{2,1,0:T(8,128)(2,1)S(1)} %bitcast.175, bf16[4,128,512]{2,1,0:T(8,128)(2,1)S(1)} %bitcast.183), custom_call_target="tpu_custom_call" | custom-call | bytes 33554432 | tf_op jit(solution)/shard_map/pallas_call | solution.py:1523
  1083.5 1.5 multiply_reduce_fusion.1
  1086.1 1.2 subtract_convert_fusion
  1087.5 1.4 fusion.14
  1088.9 2.1 collective-permute-start
  1091.0 2.4 fusion.28
  1093.5 1.6 collective-permute-start.1
  1095.2 16.5 %shard_map.283 = bf16[8,256,640]{2,1,0:T(8,128)(2,1)S(1)} custom-call(bf16[256,640]{1,0:T(8,128)(2,1)S(1)} %pad.28.in_ref), custom_call_target="tpu_custom_call" | custom-call | bytes 5242880 | tf_op jit(solution)/shard_map/pallas_call | solution.py:892
  1112.4 4.2 all-to-all-start.1
  1116.6 1.9 collective-permute-start.2
  1118.5 5.8 convolution_convert_fusion.2
  1124.3 1.2 copy.158
  1125.7 37.0 %shard_map.284 = (bf16[8,512,128]{2,1,0:T(8,128)(2,1)S(1)}, bf16[8,512,640]{2,1,0:T(8,128)(2,1)S(1)}, bf16[8,128,512]{2,1,0:T(8,128)(2,1)S(1)}) custom-call(bf16[4,512,128]{2,1,0:T(8,128)(2,1)S(1)} %bitcast.180, bf16[512,640]{1,0:T(8,128)(2,1)S(1)} %get-tuple-element.87.columns_ref, bf16[128,512]{1,0:T(8,128)(2,1)S(1)} %get-tuple-element.88.latents_ref), custom_call_target="tpu_custom_call" | custom-call | bytes 2097152 | tf_op jit(solution)/shard_map/pallas_call | solution.py:958
  1162.8 8.3 shard_map.285
  1171.1 1.4 copy.149
  1172.7 1.5 collective-permute-start.4
  1174.8 2.6 collective-permute-done.4
  1178.7 5.1 convert_element_type.100
  1183.8 12.5 %shard_map.287 = f32[512,5632]{1,0:T(8,128)} custom-call(bf16[8,4,176,512]{3,2,1,0:T(8,128)(2,1)} %bitcast.197), custom_call_target="tpu_custom_call" | custom-call | flops 4294967296 | bytes 17301504 | tf_op jit(solution)/shard_map/pallas_call | solution.py:1633
  1196.3 9.6 copy.188
  1205.9 2.5 copy.189
  (216 shorter events, 29.3 us)
Async XLA Ops:
  11.1 7.9 copy-start.52
  11.1 230.9 %all-to-all-start = ((bf16[4,512,2,88]{1,3,2,0:T(8,128)(2,1)}), bf16[4,512,2,88]{1,3,2,0:T(8,128)(2,1)}, u32[]{:S(2)}, u32[]{:S(2)}) async-start(bf16[4,512,2,88]{1,3,2,0:T(8,128)(2,1)} %pad_maximum_fusion.4), calls=%async_computation | async-start | bytes 1441792 | tf_op jit(solution)/shard_map/all_to_all | solution.py:1822
  17.5 14.1 %copy-start.47 = (s32[1,256,6]{1,0,2:T(1,128)S(1)}, s32[1,256,6]{1,0,2:T(1,128)}, u32[]{:S(2)}) copy-start(s32[1,256,6]{1,0,2:T(1,128)} %param.19) | copy-start | bytes 18436
  17.5 14.7 %copy-start.46 = (f32[1,256,6]{1,0,2:T(1,128)S(1)}, f32[1,256,6]{1,0,2:T(1,128)}, u32[]{:S(2)}) copy-start(f32[1,256,6]{1,0,2:T(1,128)} %param.20) | copy-start | bytes 18436
  17.5 14.7 %copy-start.48 = (s32[1,256]{1,0:T(1,128)S(1)}, s32[1,256]{1,0:T(1,128)}, u32[]{:S(2)}) copy-start(s32[1,256]{1,0:T(1,128)} %param.18) | copy-start | bytes 3076
  17.5 14.7 %copy-start.41 = (bf16[512,576]{0,1:T(8,128)(2,1)S(1)}, bf16[512,576]{0,1:T(8,128)(2,1)}, u32[]{:S(2)}) copy-start(bf16[512,576]{0,1:T(8,128)(2,1)} %param.23) | copy-start | bytes 1769476
  17.5 1161.1 %all-gather.4.cloned.1.call-start = ((), (), s32[]{:S(2)}) async-start(), calls=%async_computation.2 | async-start | bytes 3244032 | tf_op jit(solution)/shard_map/all_gather | solution.py:2024
  30.1 2.5 copy-start.49
  30.2 2.5 copy-start.50
  30.2 2.5 copy-start.51
  30.2 2.5 copy-start.2
  32.7 1.6 copy-start.19
  119.0 3.2 copy-start.6
  122.2 1.5 copy-start.16
  123.7 1.2 copy-start.20
  124.9 3.4 copy-start.29
  128.3 11.6 copy-start.27
  139.8 20.3 %copy-start.10 = (f32[2048,128]{1,0:T(8,128)}, f32[2048,128]{1,0:T(8,128)S(1)}, u32[]{:S(2)}) copy-start(f32[2048,128]{1,0:T(8,128)S(1)} %get-tuple-element.204.sine_ref) | copy-start | bytes 3145732
  139.8 20.3 %copy-start.11 = (f32[2048,128]{1,0:T(8,128)}, f32[2048,128]{1,0:T(8,128)S(1)}, u32[]{:S(2)}) copy-start(f32[2048,128]{1,0:T(8,128)S(1)} %get-tuple-element.205.cosine_ref) | copy-start | bytes 3145732
  160.1 21.4 %copy-start.8 = (bf16[2048,384]{1,0:T(8,128)(2,1)}, bf16[2048,384]{1,0:T(8,128)(2,1)S(1)}, u32[]{:S(2)}) copy-start(bf16[2048,384]{1,0:T(8,128)(2,1)S(1)} %get-tuple-element.63.query_ref.turned_ref) | copy-start | bytes 4718596
  160.1 21.4 %copy-start.22 = (bf16[2048,256]{1,0:T(8,128)(2,1)}, bf16[2048,256]{1,0:T(8,128)(2,1)S(1)}, u32[]{:S(2)}) copy-start(bf16[2048,256]{1,0:T(8,128)(2,1)S(1)} %get-tuple-element.65.value_ref) | copy-start | bytes 3145732
  160.1 2.4 copy-start.9
  181.5 1.3 copy-start.18
  223.3 3.4 copy-start
  230.1 6.2 copy-start.39
  236.3 4.1 copy-start.30
  238.0 2.4 copy-start.33
  619.1 564.7 %all-gather.6.cloned.1.call-start = ((), (), s32[]{:S(2)}) async-start(), calls=%async_computation.3 | async-start | bytes 6488064 | tf_op jit(solution)/shard_map/all_gather | solution.py:2022
  619.1 163.1 %copy-start.31 = (f32[256,2048]{1,0:T(8,128)S(1)}, f32[256,2048]{1,0:T(8,128)}, u32[]{:S(2)}) copy-start(f32[256,2048]{1,0:T(8,128)} %copy-done.30) | copy-start | bytes 6291460
  782.2 2.0 copy-start.34
  782.2 2.0 copy-start.36
  818.5 1.3 copy-start.4
  819.8 160.6 %copy-start.42 = (f32[1,4,4,128]{3,2,1,0:T(4,128)S(1)}, f32[1,4,4,128]{3,2,1,0:T(4,128)}, u32[]{:S(2)}) copy-start(f32[1,4,4,128]{3,2,1,0:T(4,128)} %get-tuple-element.222) | copy-start | bytes 24580
  971.2 13.0 %copy-start.3 = (bf16[1,256,2048]{2,1,0:T(8,128)(2,1)S(1)}, bf16[1,256,2048]{2,1,0:T(8,128)(2,1)}, u32[]{:S(2)}) copy-start(bf16[1,256,2048]{2,1,0:T(8,128)(2,1)} %param.17) | copy-start | bytes 3145732
  971.2 1.3 copy-start.12
  972.5 1.1 copy-start.26
  973.6 10.9 copy-start.5
  973.6 0.9 copy-start.15
  984.5 3.4 copy-start.1
  991.9 1.0 copy-start.14
  992.9 4.1 copy-start.13
  997.0 7.0 copy-start.38
  1005.7 4.4 copy-start.28
  1010.2 1.5 copy-start.21
  1011.7 1.2 copy-start.23
  1012.9 1.2 copy-start.24
  1014.1 1.2 copy-start.25
  1015.3 8.5 copy-start.53
  1023.9 1.7 copy-start.7
  1083.0 4.4 copy-start.17
  1087.4 3.6 copy-start.43
  1087.4 3.6 copy-start.32
  1087.4 3.6 copy-start.35
  1087.4 3.6 copy-start.37
  1087.4 3.6 copy-start.40
  1088.9 4.6 collective-permute-start
  1093.5 23.1 %collective-permute-start.1 = (f32[4608]{0:T(1024)S(1)}, f32[4608]{0:T(1024)S(1)}, u32[]{:S(2)}, u32[]{:S(2)}) collective-permute-start(f32[4608]{0:T(1024)S(1)} %fusion.59), channel_id=1, source_target_pairs={{0,2},{1,3},{2,0},{3,1},{4,6},{5,7},{6,4},{7,5},{8,10},{9,11},{10,... | collective-permute-start | bytes 55304 | tf_op jit(solution)/shard_map/ppermute | solution.py:1972
  1112.4 60.1 %all-to-all-start.1 = ((f32[32,1,256]{2,1,0:T(1,128)}), f32[32,1,256]{2,1,0:T(1,128)S(1)}, u32[]{:S(2)}, u32[]{:S(2)}) async-start(f32[32,1,256]{2,1,0:T(1,128)} %reshape.261), calls=%async_computation.1 | async-start | bytes 65536 | tf_op jit(solution)/shard_map/all_to_all | solution.py:1884
  1116.6 46.1 %collective-permute-start.2 = (f32[4608]{0:T(1024)S(1)}, f32[4608]{0:T(1024)S(1)}, u32[]{:S(2)}, u32[]{:S(2)}) collective-permute-start(f32[4608]{0:T(1024)S(1)} %add.275), channel_id=1, source_target_pairs={{0,4},{1,5},{2,6},{3,7},{4,0},{5,1},{6,2},{7,3},{8,12},{9,13},{10,... | collective-permute-start | bytes 55304 | tf_op jit(solution)/shard_map/ppermute | solution.py:1972
  1162.7 9.9 collective-permute-start.3
  1171.1 3.1 copy-start.44
  1172.7 4.7 collective-permute-start.4
  1183.8 22.1 %slice-start = ((s8[5767168]{0:T(1024)(128)(4,1)}), s8[1572864]{0:T(1024)(128)(4,1)S(1)}, s32[]{:S(2)}) async-start(s8[5767168]{0:T(1024)(128)(4,1)} %bitcast.194), calls=%async_computation.4 | async-start | bytes 3145728
  1196.3 9.6 slice-start.1
  (1 other events, 0.7 us)
Sparse Core Ops, SparseCore 0:
  619.2 39.5 all-gather.3
  974.7 40.6 all-gather.5

commit v6 on v5

--- a/solution.py
+++ b/solution.py
@@ -1667,6 +1667,34 @@
             flops=2 * tokens * features * size, bytes_accessed=2 * tokens * features, transcendentals=0
         ),
     )(left, right)
+
+
+def column_kernel(normed_ref, query_ref, left_ref, right_ref, out_ref):
+    size = query_ref.shape[1]
+    out_ref[:, :size] = dot_tn(normed_ref[...], query_ref[...]).astype(BF)
+    out_ref[:, size:] = dot_tn(left_ref[0], right_ref[...]).astype(BF)
+
+
+def column_terms(normed, query_back, left, right, size):
+    parts, tokens, columns = left.shape
+    last = right.shape[1] // size - 1
+    width = query_back.shape[1] + size
+    return pl.pallas_call(
+        column_kernel,
+        grid=(parts,),
+        in_specs=[
+            pl.BlockSpec((tokens, columns), lambda j: (0, j)),
+            pl.BlockSpec(query_back.shape, lambda j: (0, 0)),
+            pl.BlockSpec((1, tokens, columns), lambda j: (j, 0, 0)),
+            pl.BlockSpec((tokens, size), lambda j: (0, last)),
+        ],
+        out_specs=pl.BlockSpec((columns, width), lambda j: (j, 0)),
+        out_shape=jax.ShapeDtypeStruct((parts * columns, width), BF),
+        compiler_params=params(48),
+        cost_estimate=pl.CostEstimate(
+            flops=2 * tokens * parts * columns * width, bytes_accessed=2**24, transcendentals=0
+        ),
+    )(normed, query_back, left, right)
 
 
 def exchange_kernel(in_ref, out_ref, send_sems, recv_sems, local_sem):
@@ -1903,7 +1931,6 @@
         packed = exchange(packed, 10)
     else:
         packed = lax.all_to_all(packed, "seq", split_axis=1, concat_axis=0, tiled=True)
-    output_grad = outer(attended_all, packed, part)
 
     query_back, turned_back, key_back, rotary_sum, value_back, out_sum = attend_back(
         fast, queries, keys_all, values_all, packed, logs, cosine_all, sine_all, out_parts
@@ -1919,10 +1946,9 @@
     partial_back = partial_terms(
         rows, query_back, turned_back, key_back, value_back, rotary_sum, query_weight, expand_weight
     )
-    query_grad = dot_tn(normed_all, query_raw_back).astype(BF)
     expand_grad = dot_tn(latent_normed, expanded_back).astype(BF)
     if fast:
-        column_grads = jnp.concatenate([query_grad, output_grad], axis=1)
+        column_grads = column_terms(normed_all, query_raw_back, attended_all, packed, part)
         summed_back, column_grads, latent_grads = tail_scatter(
             partial_back.reshape(n_seq, rows, -1),
             column_grads.reshape(n_dp, shard, -1),
@@ -1930,6 +1956,8 @@
             5,
         )
     else:
+        query_grad = dot_tn(normed_all, query_raw_back).astype(BF)
+        output_grad = outer(attended_all, packed, part)
         summed_back = lax.psum_scatter(partial_back, "seq", scatter_dimension=0, tiled=True)
     summed_back = summed_back[:, : features + LATENT + ROPE].astype(F32)
     latent_normed_back = summed_back[:, features : features + LATENT]

time: 1230 us -> 1210 us (0.984)
  local copies, waits for them, and re-layouts: 80.9 us -> 64.9 us
    unnamed x136 -> x128, local copies, waits for them, and re-layouts: 52.2 us -> 43.3 us
  transfers between devices with their start and end apart: 9 -> 9, of which waited for: 1 -> 1; matrix products, arithmetic and copies ran while one was open for 7% -> 5% of each run, Pallas kernels for 52% -> 54%
where the time goes in v6:
time: 1210 us; the launch traced here: 1200 us
  Pallas kernels  1030 us (85%)
  local copies, waits for them, and re-layouts  64.9 us (5%)
  between operations  38.9 us (3%)
  other arithmetic  28.2 us (2%)
  matrix products  20.6 us (2%)
  starting transfers between devices  18.2 us (2%)
    pallas_call x1, Pallas kernels, experts(): pl.pallas_call(functools.partial(experts_kernel, remote, capacity), grid=...  369 us
    pallas_call x1, Pallas kernels, out_side(): pl.pallas_call(functools.partial(out_kernel, remote, capacity), grid=(blo...  163 us
    pallas_call x1, Pallas kernels, attend_back(): pl.pallas_call(functools.partial(attend_back_kernel, remote), grid=(heads...  150 us
    pallas_call x1, Pallas kernels, gather_start(): pl.pallas_call(gather_start_kernel, out_shape=[jax.ShapeDtypeStruct((8, *...  84.7 us
    pallas_call x1, Pallas kernels, tail_scatter(): pl.pallas_call(tail_scatter_kernel, out_shape=[jax.ShapeDtypeStruct((rows...  57.3 us
    pallas_call x2, Pallas kernels, plane_gather(): pl.pallas_call(plane_gather_kernel, out_shape=jax.ShapeDtypeStruct((8, *b...  56.8 us
    unnamed x128, local copies, waits for them, and re-layouts  43.3 us
    pallas_call x1, Pallas kernels, sum_grads(): pl.pallas_call(grads_kernel, out_shape=[jax.ShapeDtypeStruct((8, rows, wi...  37 us
  transfers between devices with their start and end apart: 9, of which 1 were waited for; matrix products, arithmetic and copies ran while one was open for 5% of the time, Pallas kernels for 54%

profile of v6, /device:TPU:0, one launch (start us, length us, event | category | flops | bytes accessed | tf_op | source)
XLA Modules:
  0.0 1200.0 jit_solution(3672633154076103889)
XLA Ops:
  7.2 1.9 constant_dynamic-slice_fusion.20
  10.1 1.0 pad_maximum_fusion.4
  11.1 6.4 all-to-all-start
  17.6 1.1 constant_dynamic-slice_fusion.30
  30.2 1.0 constant_dynamic-slice_fusion.29
  32.7 1.6 copy-done.16
  34.3 84.7 %shard_map.272 = (bf16[8,256,2048]{2,1,0:T(8,128)(2,1)S(1)}, f32[8,4,16,256]{3,2,1,0:T(8,128)S(1)}, bf16[4,16,128]{2,1,0:T(8,128)(2,1)S(1)}, bf16[4,512,384]{2,1...) custom-call(bf16[256,2048]{1,0:T(8,128)(2,1)S(1)} %bitcast.169, ...), custom_call_target="tpu_custom_call" | custom-call | bytes 67108864 | tf_op jit(solution)/shard_map/pallas_call | solution.py:454
  119.0 3.3 copy-done.5
  122.3 1.5 copy-done.13
  123.8 1.2 copy-done.17
  125.0 3.4 copy-done.26
  135.3 4.6 fusion.26
  139.9 20.2 %shard_map.273 = (bf16[2048,2048]{1,0:T(8,128)(2,1)}, bf16[2048,384]{1,0:T(8,128)(2,1)S(1)}, bf16[2048,384]{1,0:T(8,128)(2,1)}, bf16[2048,256]{1,0:T(8,128)(2,1)...) custom-call(bf16[2048,2048]{1,0:T(8,128)(2,1)} %bitcast.188, f32[1,2048]{1,0:T(1,128)S(1)} %bitcast.186, ...), custom_call_target="tpu_custom_call" | custom-call | flops 8589934592 | bytes 33554432 | tf_op jit(solution)/shard_map/pallas_call | solution.py:1157
  160.2 2.3 copy-done.10
  162.5 19.0 %shard_map.274 = (bf16[2048,256]{1,0:T(8,128)(2,1)S(1)}, f32[2,2048,128]{2,1,0:T(8,128)S(1)}) custom-call(bf16[2048,384]{1,0:T(8,128)(2,1)S(1)} %get-tuple-element.63.query_ref.turned_ref, bf16[2048,384]{1,0:T(8,128)(2,1)S(1)} %get-tuple-element.63.query_ref.turned_ref, bf16[2048,384]{1,0:T(8,128)(2,1)S(1)} %copy-done.10, bf16[2048,384]{1,0:T(8,128)(2,1)S(1)} %copy-done.10, ...), custom_call_target="tpu_custom_call" | custom-call | flops 3221225472 | bytes 8388608 | tf_op jit(solution)/shard_map/pallas_call | solution.py:1249
  181.6 1.3 copy-done.15
  182.9 40.4 %shard_map.275.left_ref = bf16[8,2048,256]{2,1,0:T(8,128)(2,1)S(1)} custom-call(bf16[2048,256]{1,0:T(8,128)(2,1)S(1)} %get-tuple-element.66.in_ref), custom_call_target="tpu_custom_call" | custom-call | bytes 16777216 | tf_op jit(solution)/shard_map/pallas_call | solution.py:892
  223.3 3.2 copy-done
  226.5 1.3 dynamic-slice_bitcast_fusion
  227.8 1.3 copy.122
  229.9 6.2 multiply_reduce_fusion
  236.4 1.3 constant_dynamic-slice_fusion.12
  240.2 1.5 pad_maximum_fusion.rows_in
  241.7 1.2 copy.147
  243.0 1.3 copy.139.shared_in
  244.3 368.6 %shard_map.276 = (bf16[32,2,256,2048]{3,2,1,0:T(8,128)(2,1)}, f32[2048,1408]{1,0:T(8,128)}, f32[704,2048]{1,0:T(8,128)}, bf16[5120,768]{1,0:T(8,128)(2,1)}, bf16...) custom-call(bf16[2,256,2048]{2,1,0:T(8,128)(2,1)} %pad_maximum_fusion.rows_in, ...), custom_call_target="tpu_custom_call" | custom-call | flops 96636764160 | bytes 134217728 | tf_op jit(solution)/shard_map/pallas_call | solution.py:836
  613.0 1.7 convert.17
  615.8 1.0 copy.145
  616.8 1.9 slice.218
  618.7 163.1 %shard_map.277 = (f32[32,1,256]{2,1,0:T(1,128)}, bf16[32,256,2048]{2,1,0:T(8,128)(2,1)}, bf16[256,2048]{1,0:T(8,128)(2,1)}, bf16[4,176,512]{2,1,0:T(8,128)(2,1)}) custom-call(bf16[32,256,2048]{2,1,0:T(8,128)(2,1)} %get-tuple-element.68.back_ref, bf16[4,176,512]{2,1,0:T(8,128)(2,1)} %bitcast.203, s32[32,1,256]{2,1,0:T(1,128)} %broadcast_in_dim.61.place_ref.refs_0_, ...), custom_call_target="tpu_custom_call" | custom-call | flops 26843545600 | bytes 54525952 | tf_op jit(solution)/shard_map/pallas_call | solution.py:1062
  781.9 2.0 fusion.6
  784.6 5.7 convolution_convert_fusion
  792.1 26.1 %shard_map.278 = bf16[8,256,512]{2,1,0:T(8,128)(2,1)S(1)} custom-call(bf16[256,4096]{1,0:T(8,128)(2,1)S(1)} %bitcast.175), custom_call_target="tpu_custom_call" | custom-call | bytes 4194304 | tf_op jit(solution)/shard_map/pallas_call | solution.py:1722
  818.2 1.3 copy-done.3
  819.5 150.4 %shard_map.279 = (bf16[2048,256]{1,0:T(8,128)(2,1)}, bf16[2048,256]{1,0:T(8,128)(2,1)}, bf16[2048,256]{1,0:T(8,128)(2,1)}, f32[2048,128]{1,0:T(8,128)}, bf16[204...) custom-call(bf16[2048,384]{1,0:T(8,128)(2,1)} %copy-done.9, bf16[2048,384]{1,0:T(8,128)(2,1)} %copy-done.9, ...), custom_call_target="tpu_custom_call" | custom-call | flops 8589934592 | bytes 67108864 | tf_op jit(solution)/shard_map/pallas_call | solution.py:1344
  969.9 1.3 copy-done.7
  980.6 1.2 multiply_reduce_fusion.3
  982.2 1.4 slice_add_fusion.turned_ref
  984.8 8.7 shard_map.280
  993.5 1.3 fusion.19
  995.2 12.9 %shard_map.281 = bf16[2048,640]{1,0:T(8,128)(2,1)} custom-call(bf16[2048,2048]{1,0:T(8,128)(2,1)} %get-tuple-element.82.normed_ref, bf16[2048,384]{1,0:T(8,128)(2,1)S(1)} %pad_maximum_fusion.2.query_ref, bf16[8,2048,256]{2,1,0:T(8,128)(2,1)} %copy-done, bf16[2048,512]{1,0:T(8,128)(2,1)S(1)} %bitcast.171), custom_call_target="tpu_custom_call" | custom-call | flops 5368709120 | bytes 16777216 | tf_op jit(solution)/shard_map/pallas_call | solution.py:1682
  1008.0 1.7 copy-done.6
  1009.8 57.3 %shard_map.282 = (bf16[256,2688]{1,0:T(8,128)(2,1)S(1)}, bf16[512,640]{1,0:T(8,128)(2,1)S(1)}, bf16[128,512]{1,0:T(8,128)(2,1)S(1)}) custom-call(bf16[8,256,2688]{2,1,0:T(8,128)(2,1)} %bitcast.189, bf16[4,512,640]{2,1,0:T(8,128)(2,1)S(1)} %bitcast.174, bf16[4,128,512]{2,1,0:T(8,128)(2,1)S(1)} %bitcast.182), custom_call_target="tpu_custom_call" | custom-call | bytes 33554432 | tf_op jit(solution)/shard_map/pallas_call | solution.py:1523
  1067.8 1.5 multiply_reduce_fusion.1
  1069.3 1.1 subtract_convert_fusion.1
  1070.3 1.2 subtract_convert_fusion
  1071.7 1.4 fusion.14
  1073.2 2.3 collective-permute-start
  1075.6 2.5 fusion.25
  1078.0 2.6 collective-permute-start.1
  1080.7 16.4 %shard_map.283 = bf16[8,256,640]{2,1,0:T(8,128)(2,1)S(1)} custom-call(bf16[256,640]{1,0:T(8,128)(2,1)S(1)} %pad.28.in_ref), custom_call_target="tpu_custom_call" | custom-call | bytes 5242880 | tf_op jit(solution)/shard_map/pallas_call | solution.py:892
  1097.9 3.2 all-to-all-start.1
  1101.1 1.9 collective-permute-start.2
  1103.1 5.8 convolution_convert_fusion.1
  1108.8 1.2 copy.146
  1110.2 37.0 %shard_map.284 = (bf16[8,512,128]{2,1,0:T(8,128)(2,1)S(1)}, bf16[8,512,640]{2,1,0:T(8,128)(2,1)S(1)}, bf16[8,128,512]{2,1,0:T(8,128)(2,1)S(1)}) custom-call(bf16[4,512,128]{2,1,0:T(8,128)(2,1)S(1)} %bitcast.179, bf16[512,640]{1,0:T(8,128)(2,1)S(1)} %get-tuple-element.87.columns_ref, bf16[128,512]{1,0:T(8,128)(2,1)S(1)} %get-tuple-element.88.latents_ref), custom_call_target="tpu_custom_call" | custom-call | bytes 2097152 | tf_op jit(solution)/shard_map/pallas_call | solution.py:958
  1147.3 8.3 shard_map.285
  1155.6 1.4 copy.137
  1157.2 1.5 collective-permute-start.4
  1159.3 2.6 collective-permute-done.4
  1163.2 5.1 convert_element_type.96
  1168.3 12.5 %shard_map.287 = f32[512,5632]{1,0:T(8,128)} custom-call(bf16[8,4,176,512]{3,2,1,0:T(8,128)(2,1)} %bitcast.196), custom_call_target="tpu_custom_call" | custom-call | flops 4294967296 | bytes 17301504 | tf_op jit(solution)/shard_map/pallas_call | solution.py:1633
  1180.8 9.6 copy.176
  1190.4 2.5 copy.177
  (205 shorter events, 19.6 us)
Async XLA Ops:
  11.1 7.9 copy-start.48
  11.1 230.6 %all-to-all-start = ((bf16[4,512,2,88]{1,3,2,0:T(8,128)(2,1)}), bf16[4,512,2,88]{1,3,2,0:T(8,128)(2,1)}, u32[]{:S(2)}, u32[]{:S(2)}) async-start(bf16[4,512,2,88]{1,3,2,0:T(8,128)(2,1)} %pad_maximum_fusion.4), calls=%async_computation | async-start | bytes 1441792 | tf_op jit(solution)/shard_map/all_to_all | solution.py:1850
  17.5 14.1 %copy-start.43 = (s32[1,256,6]{1,0,2:T(1,128)S(1)}, s32[1,256,6]{1,0,2:T(1,128)}, u32[]{:S(2)}) copy-start(s32[1,256,6]{1,0,2:T(1,128)} %param.19) | copy-start | bytes 18436
  17.5 14.7 %copy-start.42 = (f32[1,256,6]{1,0,2:T(1,128)S(1)}, f32[1,256,6]{1,0,2:T(1,128)}, u32[]{:S(2)}) copy-start(f32[1,256,6]{1,0,2:T(1,128)} %param.20) | copy-start | bytes 18436
  17.5 14.7 %copy-start.44 = (s32[1,256]{1,0:T(1,128)S(1)}, s32[1,256]{1,0:T(1,128)}, u32[]{:S(2)}) copy-start(s32[1,256]{1,0:T(1,128)} %param.18) | copy-start | bytes 3076
  17.6 14.7 %copy-start.37 = (bf16[512,576]{0,1:T(8,128)(2,1)S(1)}, bf16[512,576]{0,1:T(8,128)(2,1)}, u32[]{:S(2)}) copy-start(bf16[512,576]{0,1:T(8,128)(2,1)} %param.23) | copy-start | bytes 1769476
  17.6 1145.6 %all-gather.4.cloned.1.call-start = ((), (), s32[]{:S(2)}) async-start(), calls=%async_computation.2 | async-start | bytes 3244032 | tf_op jit(solution)/shard_map/all_gather | solution.py:2052
  30.2 2.5 copy-start.45
  30.2 2.5 copy-start.46
  30.2 2.5 copy-start.47
  30.2 2.5 copy-start.1
  32.7 1.6 copy-start.16
  119.0 3.3 copy-start.5
  122.3 1.5 copy-start.13
  123.8 1.2 copy-start.17
  125.0 3.4 copy-start.26
  128.3 11.6 copy-start.24
  139.9 20.3 %copy-start.11 = (f32[2048,128]{1,0:T(8,128)}, f32[2048,128]{1,0:T(8,128)S(1)}, u32[]{:S(2)}) copy-start(f32[2048,128]{1,0:T(8,128)S(1)} %get-tuple-element.204.sine_ref) | copy-start | bytes 3145732
  139.9 20.3 %copy-start.12 = (f32[2048,128]{1,0:T(8,128)}, f32[2048,128]{1,0:T(8,128)S(1)}, u32[]{:S(2)}) copy-start(f32[2048,128]{1,0:T(8,128)S(1)} %get-tuple-element.205.cosine_ref) | copy-start | bytes 3145732
  160.2 21.4 %copy-start.9 = (bf16[2048,384]{1,0:T(8,128)(2,1)}, bf16[2048,384]{1,0:T(8,128)(2,1)S(1)}, u32[]{:S(2)}) copy-start(bf16[2048,384]{1,0:T(8,128)(2,1)S(1)} %get-tuple-element.63.query_ref.turned_ref) | copy-start | bytes 4718596
  160.2 21.4 %copy-start.19 = (bf16[2048,256]{1,0:T(8,128)(2,1)}, bf16[2048,256]{1,0:T(8,128)(2,1)S(1)}, u32[]{:S(2)}) copy-start(bf16[2048,256]{1,0:T(8,128)(2,1)S(1)} %get-tuple-element.65.value_ref) | copy-start | bytes 3145732
  160.2 2.4 copy-start.10
  181.6 1.3 copy-start.15
  223.3 3.2 copy-start
  229.9 6.2 copy-start.35
  236.1 4.1 copy-start.27
  237.8 2.4 copy-start.30
  618.7 549.6 %all-gather.6.cloned.1.call-start = ((), (), s32[]{:S(2)}) async-start(), calls=%async_computation.3 | async-start | bytes 6488064 | tf_op jit(solution)/shard_map/all_gather | solution.py:2050
  618.7 163.1 %copy-start.28 = (f32[256,2048]{1,0:T(8,128)S(1)}, f32[256,2048]{1,0:T(8,128)}, u32[]{:S(2)}) copy-start(f32[256,2048]{1,0:T(8,128)} %copy-done.27) | copy-start | bytes 6291460
  781.8 2.0 copy-start.31
  781.9 2.0 copy-start.33
  818.1 1.3 copy-start.3
  819.5 150.4 %copy-start.23 = (bf16[4,176,512]{2,1,0:T(8,128)(2,1)S(1)}, bf16[4,176,512]{2,1,0:T(8,128)(2,1)}, u32[]{:S(2)}) copy-start(bf16[4,176,512]{2,1,0:T(8,128)(2,1)} %get-tuple-element.96.in_ref) | copy-start | bytes 2162692
  819.5 158.5 %copy-start.38 = (f32[1,4,4,128]{3,2,1,0:T(4,128)S(1)}, f32[1,4,4,128]{3,2,1,0:T(4,128)}, u32[]{:S(2)}) copy-start(f32[1,4,4,128]{3,2,1,0:T(4,128)} %get-tuple-element.222) | copy-start | bytes 24580
  969.9 11.9 copy-start.2
  969.9 1.3 copy-start.7
  972.2 11.4 copy-start.8
  972.2 11.6 copy-start.25
  982.1 1.7 copy-start.18
  982.1 2.0 copy-start.20
  982.1 2.3 copy-start.21
  982.2 2.6 copy-start.22
  984.8 8.7 copy-start.49
  993.5 1.7 copy-start.4
  1008.0 1.7 copy-start.6
  1067.1 0.7 copy-start.41
  1067.3 4.4 copy-start.14
  1071.7 3.8 copy-start.39
  1071.7 3.8 copy-start.29
  1071.7 3.8 copy-start.32
  1071.7 3.8 copy-start.34
  1071.7 3.8 copy-start.36
  1073.2 4.8 collective-permute-start
  1078.0 23.1 %collective-permute-start.1 = (f32[4608]{0:T(1024)S(1)}, f32[4608]{0:T(1024)S(1)}, u32[]{:S(2)}, u32[]{:S(2)}) collective-permute-start(f32[4608]{0:T(1024)S(1)} %fusion.55), channel_id=1, source_target_pairs={{0,2},{1,3},{2,0},{3,1},{4,6},{5,7},{6,4},{7,5},{8,10},{9,11},{10,... | collective-permute-start | bytes 55304 | tf_op jit(solution)/shard_map/ppermute | solution.py:2000
  1097.9 59.1 %all-to-all-start.1 = ((f32[32,1,256]{2,1,0:T(1,128)}), f32[32,1,256]{2,1,0:T(1,128)S(1)}, u32[]{:S(2)}, u32[]{:S(2)}) async-start(f32[32,1,256]{2,1,0:T(1,128)} %reshape.261), calls=%async_computation.1 | async-start | bytes 65536 | tf_op jit(solution)/shard_map/all_to_all | solution.py:1912
  1101.1 46.1 %collective-permute-start.2 = (f32[4608]{0:T(1024)S(1)}, f32[4608]{0:T(1024)S(1)}, u32[]{:S(2)}, u32[]{:S(2)}) collective-permute-start(f32[4608]{0:T(1024)S(1)} %add.275), channel_id=1, source_target_pairs={{0,4},{1,5},{2,6},{3,7},{4,0},{5,1},{6,2},{7,3},{8,12},{9,13},{10,... | collective-permute-start | bytes 55304 | tf_op jit(solution)/shard_map/ppermute | solution.py:2000
  1147.2 9.9 collective-permute-start.3
  1155.6 3.1 copy-start.40
  1157.2 4.7 collective-permute-start.4
  1168.3 22.1 %slice-start = ((s8[5767168]{0:T(1024)(128)(4,1)}), s8[1572864]{0:T(1024)(128)(4,1)S(1)}, s32[]{:S(2)}) async-start(s8[5767168]{0:T(1024)(128)(4,1)} %bitcast.193), calls=%async_computation.4 | async-start | bytes 3145728
  1180.8 9.6 slice-start.1
Sparse Core Ops, SparseCore 0:
  618.8 39.2 all-gather.3
  972.3 42.9 all-gather.5
